TPU v7x, 128 devices: a whole 4x4x4 slice. The times are simulated.
128 devices in a mesh: batch: 16 (over x, z), seq: 8 (over y, core).
Axes of the slice: x: 4, y: 4, z: 4, core: 2. Of those that a mesh axis runs over, the one named last changes fastest.
Arguments:
- inputs: bfloat16 [16, 1024, 2048], P('batch', 'seq'), may hold values from -6 to 6
- positions: int32 [16, 1024], P('batch', 'seq'), may hold values from 0 to 1023, as said below
- w_qkv: bfloat16 [2048, 6144], P(('batch', 'seq')), may hold values from -0.1875 to 0.1875
- b_qkv: bfloat16 [6144], P(('batch', 'seq')), may hold values from -3 to 3
- w_out: bfloat16 [2048, 2048], P(('batch', 'seq')), may hold values from -0.5 to 0.5
- b_out: bfloat16 [2048], P(('batch', 'seq')), may hold values from -2 to 2
- w_up: bfloat16 [2048, 8192], P(('batch', 'seq')), may hold values from -0.125 to 0.125
- b_up: bfloat16 [8192], P(('batch', 'seq')), may hold values from -3 to 3
- w_down: bfloat16 [8192, 2048], P(('batch', 'seq')), may hold values from -0.0625 to 0.0625
- b_down: bfloat16 [2048], P(('batch', 'seq')), may hold values from -2 to 2
- gain_attn: bfloat16 [2048], P(('batch', 'seq')), may hold values from 0.099609375 to 1.8984375
- shift_attn: bfloat16 [2048], P(('batch', 'seq')), may hold values from -3 to 3
- gain_mlp: bfloat16 [2048], P(('batch', 'seq')), may hold values from 0.099609375 to 1.8984375
- shift_mlp: bfloat16 [2048], P(('batch', 'seq')), may hold values from -3 to 3
- grad_out: bfloat16 [16, 1024, 2048], P('batch', 'seq'), may hold values from -6 to 6
Outputs:
- layer_out: bfloat16 [16, 1024, 2048], P('batch', 'seq')
- grad_in: bfloat16 [16, 1024, 2048], P('batch', 'seq')
- grad_w_qkv: float32 [2048, 6144], P(('batch', 'seq'))
- grad_b_qkv: float32 [6144], P(('batch', 'seq'))
- grad_w_out: float32 [2048, 2048], P(('batch', 'seq'))
- grad_b_out: float32 [2048], P(('batch', 'seq'))
- grad_w_up: float32 [2048, 8192], P(('batch', 'seq'))
- grad_b_up: float32 [8192], P(('batch', 'seq'))
- grad_w_down: float32 [8192, 2048], P(('batch', 'seq'))
- grad_b_down: float32 [2048], P(('batch', 'seq'))
- grad_gain_attn: float32 [2048], P(('batch', 'seq'))
- grad_shift_attn: float32 [2048], P(('batch', 'seq'))
- grad_gain_mlp: float32 [2048], P(('batch', 'seq'))
- grad_shift_mlp: float32 [2048], P(('batch', 'seq'))
Inputs may be any that keep to these rules, and one draw needn't show every extreme that they name: `positions`: in each sequence the first position is 0 and each later one is either 0 (a new document) or one more than the one before; some sequence has no restart.
All inputs are finite; a program needn't handle non-finite values.
Results may differ from a plain program's by a relative error of at most 0.015.
Values may be sent and summed in bfloat16 or wider, within the bound.
A program may use at most 512 MiB of HBM per device.

v0:
```python
from functools import partial

import jax
import jax.numpy as jnp
from jax import lax
from jax.sharding import PartitionSpec as P

H = 16
HD = 128
ROT = 32


EPS = 1e-05


def layer_norm(tensor, gain_vec, shift_vec):
    average = jnp.mean(tensor, -1, keepdims=True)
    centred = tensor - average
    inverse = lax.rsqrt(jnp.mean(centred * centred, -1, keepdims=True) + EPS)
    normed = centred * inverse
    return (normed * gain_vec + shift_vec, normed, inverse)


def norm_back(upstream, normed, inverse, gain_vec):
    scaled = upstream * gain_vec
    adjusted = (
        scaled
        - jnp.mean(scaled, -1, keepdims=True)
        - normed * jnp.mean(scaled * normed, -1, keepdims=True)
    )
    return (adjusted * inverse, jnp.sum(upstream * normed, 0), jnp.sum(upstream, 0))


def tables(positions):
    half_rot = ROT // 2
    exponent = jnp.arange(half_rot).astype(jnp.float32) / half_rot
    frequency = jnp.power(10000.0, -exponent)
    angles = positions.astype(jnp.float32)[..., None] * frequency
    return (jnp.cos(angles)[..., None, :], jnp.sin(angles)[..., None, :])


def rotate(tensor, cos_tab, sine_tab):
    half_rot = ROT // 2
    first_half = tensor[..., :half_rot]
    second_half = tensor[..., half_rot:ROT]
    return jnp.concatenate(
        [
            first_half * cos_tab - second_half * sine_tab,
            second_half * cos_tab + first_half * sine_tab,
            tensor[..., ROT:],
        ],
        -1,
    )


def unrotate(gradient, cos_tab, sine_tab):
    half_rot = ROT // 2
    first_half = gradient[..., :half_rot]
    second_half = gradient[..., half_rot:ROT]
    return jnp.concatenate(
        [
            first_half * cos_tab + second_half * sine_tab,
            second_half * cos_tab - first_half * sine_tab,
            gradient[..., ROT:],
        ],
        -1,
    )


def over_rows(left, right):
    return lax.dot_general(
        left, right, (((0,), (0,)), ((), ())), preferred_element_type=jnp.float32
    )


def against(left, right):
    return lax.dot_general(
        left, right, (((1,), (1,)), ((), ())), preferred_element_type=jnp.float32
    )


def shards(
    inputs,
    positions,
    w_qkv,
    b_qkv,
    w_out,
    b_out,
    w_up,
    b_up,
    w_down,
    b_down,
    gain_attn,
    shift_attn,
    gain_mlp,
    shift_mlp,
    grad_out,
):
    seq_count, block_len, width = inputs.shape
    row_count = seq_count * block_len
    length = block_len * lax.axis_size("seq")
    scaling = HD ** (-0.5)
    gelu_exact = partial(jax.nn.gelu, approximate=False)

    def fetch_attn():
        return (
            lax.all_gather(w_qkv, ("batch", "seq"), axis=0, tiled=True),
            lax.all_gather(b_qkv, ("batch", "seq"), axis=0, tiled=True),
            lax.all_gather(w_out, ("batch", "seq"), axis=0, tiled=True),
            lax.all_gather(b_out, ("batch", "seq"), axis=0, tiled=True),
            lax.all_gather(b_down, ("batch", "seq"), axis=0, tiled=True),
            lax.all_gather(gain_attn, ("batch", "seq"), axis=0, tiled=True),
            lax.all_gather(shift_attn, ("batch", "seq"), axis=0, tiled=True),
            lax.all_gather(gain_mlp, ("batch", "seq"), axis=0, tiled=True),
            lax.all_gather(shift_mlp, ("batch", "seq"), axis=0, tiled=True),
        )

    def fetch_rows():
        return (
            lax.all_gather(w_up, ("batch", "seq"), axis=0, tiled=True),
            lax.all_gather(b_up, ("batch", "seq"), axis=0, tiled=True),
            lax.all_gather(w_down, ("batch", "seq"), axis=0, tiled=True),
        )

    attn_set = fetch_attn()
    flat_rows = inputs.reshape(row_count, width).astype(jnp.float32)
    normed_a, plain_a, inverse_a = layer_norm(
        flat_rows, attn_set[5].astype(jnp.float32), attn_set[6].astype(jnp.float32)
    )
    normed_m, plain_m, inverse_m = layer_norm(
        flat_rows, attn_set[7].astype(jnp.float32), attn_set[8].astype(jnp.float32)
    )
    first_in = normed_a.astype(jnp.bfloat16)
    second_in = normed_m.astype(jnp.bfloat16)
    qkv = jnp.dot(first_in, attn_set[0], preferred_element_type=jnp.float32) + attn_set[1].astype(
        jnp.float32
    )
    qkv = qkv.reshape(seq_count, block_len, 3, H, HD)
    cos_tab, sine_tab = tables(positions)
    queries = (rotate(qkv[:, :, 0], cos_tab, sine_tab) * scaling).astype(jnp.bfloat16)
    key_local = rotate(qkv[:, :, 1], cos_tab, sine_tab).astype(jnp.bfloat16)
    value_local = qkv[:, :, 2].astype(jnp.bfloat16)
    all_keys, all_values = (
        lax.all_gather(key_local, "seq", axis=1, tiled=True),
        lax.all_gather(value_local, "seq", axis=1, tiled=True),
    )
    offset = lax.axis_index("seq") * block_len
    query_pos = offset + jnp.arange(block_len)
    visible = query_pos[:, None] >= jnp.arange(length)[None, :]
    scores = jnp.einsum("sqhd,skhd->shqk", queries, all_keys, preferred_element_type=jnp.float32)
    scores = jnp.where(visible, scores, -1e30)
    peak_score = jnp.max(scores, -1, keepdims=True)
    exponent = jnp.exp(scores - peak_score)
    totals = jnp.sum(exponent, -1, keepdims=True)
    probs = exponent / totals
    log_total = peak_score + jnp.log(totals)
    mixture = jnp.einsum(
        "shqk,skhd->sqhd",
        probs.astype(jnp.bfloat16),
        all_values,
        preferred_element_type=jnp.float32,
    )
    mixture_low = mixture.reshape(row_count, width).astype(jnp.bfloat16)
    attended = jnp.dot(mixture_low, attn_set[2], preferred_element_type=jnp.float32) + attn_set[
        3
    ].astype(jnp.float32)
    upstream = grad_out.reshape(row_count, width)
    upstream_f = upstream.astype(jnp.float32)
    mlp_set = fetch_rows()
    hidden = jnp.dot(second_in, mlp_set[0], preferred_element_type=jnp.float32) + mlp_set[1].astype(
        jnp.float32
    )
    active, gelu_pull = jax.vjp(gelu_exact, hidden)
    active_low = active.astype(jnp.bfloat16)
    fed_forward = jnp.dot(active_low, mlp_set[2], preferred_element_type=jnp.float32)
    layer_out = (
        (flat_rows + attended + fed_forward + attn_set[4].astype(jnp.float32))
        .astype(jnp.bfloat16)
        .reshape(seq_count, block_len, width)
    )
    grad_b_down = jnp.sum(upstream_f, 0)
    mlp_back = fetch_rows()
    grad_w_down = over_rows(active_low, upstream)
    grad_active = against(upstream, mlp_back[2])
    (grad_hidden,) = gelu_pull(grad_active)
    grad_b_up = jnp.sum(grad_hidden, 0)
    grad_hidden_low = grad_hidden.astype(jnp.bfloat16)
    grad_w_up = over_rows(second_in, grad_hidden_low)
    grad_second = against(grad_hidden_low, mlp_back[0])
    mlp_grads = (
        lax.psum_scatter(grad_w_up, ("batch", "seq"), scatter_dimension=0, tiled=True),
        lax.psum_scatter(grad_b_up, ("batch", "seq"), scatter_dimension=0, tiled=True),
        lax.psum_scatter(grad_w_down, ("batch", "seq"), scatter_dimension=0, tiled=True),
    )
    out_w_up, out_b_up, out_w_down = mlp_grads
    attn_back = fetch_attn()
    grad_b_out = jnp.sum(upstream_f, 0)
    grad_w_out = over_rows(mixture_low, upstream)
    grad_mixture = (
        against(upstream, attn_back[2]).astype(jnp.bfloat16).reshape(seq_count, block_len, H, HD)
    )
    scores = jnp.einsum("sqhd,skhd->shqk", queries, all_keys, preferred_element_type=jnp.float32)
    scores = jnp.where(visible, scores, -1e30)
    probs = jnp.exp(scores - log_total)
    weights_low = probs.astype(jnp.bfloat16)
    grad_probs = jnp.einsum(
        "sqhd,skhd->shqk", grad_mixture, all_values, preferred_element_type=jnp.float32
    )
    row_delta = jnp.sum(probs * grad_probs, -1, keepdims=True)
    grad_scores = (probs * (grad_probs - row_delta)).astype(jnp.bfloat16)
    grad_query = (
        jnp.einsum("shqk,skhd->sqhd", grad_scores, all_keys, preferred_element_type=jnp.float32)
        * scaling
    )
    grad_keys = jnp.einsum(
        "shqk,sqhd->kshd", grad_scores, queries, preferred_element_type=jnp.float32
    )
    grad_values = jnp.einsum(
        "shqk,sqhd->kshd", weights_low, grad_mixture, preferred_element_type=jnp.float32
    )
    returned = lax.psum_scatter(
        jnp.stack([grad_keys, grad_values], 2).astype(jnp.bfloat16),
        "seq",
        scatter_dimension=0,
        tiled=True,
    ).astype(jnp.float32)
    grad_key_local = jnp.swapaxes(returned[:, :, 0], 0, 1)
    grad_value_local = jnp.swapaxes(returned[:, :, 1], 0, 1)
    grad_qkv = jnp.stack(
        [
            unrotate(grad_query, cos_tab, sine_tab),
            unrotate(grad_key_local, cos_tab, sine_tab),
            grad_value_local,
        ],
        2,
    ).reshape(row_count, 3 * width)
    grad_b_qkv = jnp.sum(grad_qkv, 0)
    grad_qkv_low = grad_qkv.astype(jnp.bfloat16)
    grad_w_qkv = over_rows(first_in, grad_qkv_low)
    grad_first = against(grad_qkv_low, attn_back[0])
    back_a, grad_gain_a, grad_shift_a = norm_back(
        grad_first, plain_a, inverse_a, attn_back[5].astype(jnp.float32)
    )
    back_m, grad_gain_m, grad_shift_m = norm_back(
        grad_second, plain_m, inverse_m, attn_back[7].astype(jnp.float32)
    )
    grad_in = (
        (upstream_f + back_a + back_m).astype(jnp.bfloat16).reshape(seq_count, block_len, width)
    )
    attn_grads = (
        lax.psum_scatter(grad_w_qkv, ("batch", "seq"), scatter_dimension=0, tiled=True),
        lax.psum_scatter(grad_b_qkv, ("batch", "seq"), scatter_dimension=0, tiled=True),
        lax.psum_scatter(grad_w_out, ("batch", "seq"), scatter_dimension=0, tiled=True),
        lax.psum_scatter(grad_b_out, ("batch", "seq"), scatter_dimension=0, tiled=True),
        lax.psum_scatter(grad_b_down, ("batch", "seq"), scatter_dimension=0, tiled=True),
        lax.psum_scatter(grad_gain_a, ("batch", "seq"), scatter_dimension=0, tiled=True),
        lax.psum_scatter(grad_shift_a, ("batch", "seq"), scatter_dimension=0, tiled=True),
        lax.psum_scatter(grad_gain_m, ("batch", "seq"), scatter_dimension=0, tiled=True),
        lax.psum_scatter(grad_shift_m, ("batch", "seq"), scatter_dimension=0, tiled=True),
    )
    return (
        layer_out,
        grad_in,
        attn_grads[0],
        attn_grads[1],
        attn_grads[2],
        attn_grads[3],
        out_w_up,
        out_b_up,
        out_w_down,
        attn_grads[4],
        attn_grads[5],
        attn_grads[6],
        attn_grads[7],
        attn_grads[8],
    )


def solution(mesh):
    return jax.shard_map(
        shards,
        mesh=mesh,
        in_specs=(
            P("batch", "seq", None),
            P("batch", "seq"),
            P(("batch", "seq"), None),
            P(("batch", "seq")),
            P(("batch", "seq"), None),
            P(("batch", "seq")),
            P(("batch", "seq"), None),
            P(("batch", "seq")),
            P(("batch", "seq"), None),
            P(("batch", "seq")),
            P(("batch", "seq")),
            P(("batch", "seq")),
            P(("batch", "seq")),
            P(("batch", "seq")),
            P("batch", "seq", None),
        ),
        out_specs=(
            P("batch", "seq", None),
            P("batch", "seq", None),
            P(("batch", "seq"), None),
            P(("batch", "seq")),
            P(("batch", "seq"), None),
            P(("batch", "seq")),
            P(("batch", "seq"), None),
            P(("batch", "seq")),
            P(("batch", "seq"), None),
            P(("batch", "seq")),
            P(("batch", "seq")),
            P(("batch", "seq")),
            P(("batch", "seq")),
            P(("batch", "seq")),
        ),
        check_vma=False,
    )
```

profile of v0, /device:TPU:1, one launch (start us, length us, event | category | flops | bytes accessed | tf_op | source)
XLA Modules:
  0.0 3172.5 jit_solution(15892202598129181933)
XLA Ops:
  15.5 70.5 %all-reduce.16 = (bf16[6144]{0:T(1024)(128)(2,1)S(1)}, bf16[2048]{0:T(1024)(128)(2,1)S(1)}, bf16[2048]{0:T(1024)(128)(2,1)S(1)}, bf16[2048]{0:T(1024)(128)(2,1)}...) all-reduce(bf16[6144]{0:T(1024)(128)(2,1)S(1)} %dynamic-update-slic, ...), channel_id=1, replica_groups=mesh['batch'=16,'seq'=8] {'batch','seq'}, use_global_device_ids=true, to_apply=%add.2 | all-reduce | flops 26624 | bytes 106496
  89.6 19.2 all-gather.8.cloned.1.call-done
  108.8 10.3 fusion.30
  129.0 52.1 %all-gather.12.cloned.1.call-done = bf16[2048,2048]{1,0:T(8,128)(2,1)} async-done(((bf16[16,2048]{1,0:T(8,128)(2,1)}), bf16[2048,2048]{1,0:T(8,128)(2,1)}) %all-gather.12.cloned.1.call-update) | async-done | bytes 8388624 | tf_op jit(solution)/shard_map/all_gather | solution.py:109
  181.1 6.2 convolution_convert_fusion
  190.2 22.9 all-gather.10.cloned.1.call-done
  213.1 3.6 select_reduce_fusion
  219.9 31.3 all-gather.18.cloned.1.call-done
  251.2 8.0 multiply_reduce_fusion
  264.7 4.1 convert_bitcast_fusion
  268.8 6.2 pad_maximum_fusion
  275.5 4.8 fusion.34
  281.7 6.6 fusion.38
  288.3 73.4 %all-gather.14.cloned.1.call-done = bf16[2048,8192]{1,0:T(8,128)(2,1)} async-done(((bf16[16,8192]{1,0:T(8,128)(2,1)}), bf16[2048,8192]{1,0:T(8,128)(2,1)}) %all-gather.14.cloned.1.call-update) | async-done | bytes 33554448 | tf_op jit(solution)/shard_map/all_gather | solution.py:120
  361.8 17.1 convolution_add_fusion
  378.9 91.8 %all-gather.16.cloned.1.call-done = bf16[8192,2048]{1,0:T(8,128)(2,1)} async-done(((bf16[64,2048]{1,0:T(8,128)(2,1)}), bf16[8192,2048]{1,0:T(8,128)(2,1)}) %all-gather.16.cloned.1.call-update) | async-done | bytes 33554448 | tf_op jit(solution)/shard_map/all_gather | solution.py:122
  470.8 26.7 fusion.102
  497.4 16.7 fusion.73
  514.1 9.9 reduce-scatter.6.cloned.1.call-done
  533.2 15.2 fusion.63
  548.4 3.6 convert_reduce_fusion.1
  552.0 9.3 fusion.81
  562.0 19.6 fusion.76
  582.7 28.9 fusion.79
  613.2 23.7 fusion.71
  637.9 4.8 fusion.25
  642.8 17.8 fusion.27
  660.5 32.7 %all-reduce.19.cloned.1.call-done = (f32[6144]{0:T(1024)}, f32[2048]{0:T(1024)}, f32[8192]{0:T(1024)}, f32[2048]{0:T(1024)}, f32[2048]{0:T(1024)}, /*index=5*/f32[2048]{0:T(1024)}, f32[2048]{0:T(1024)}) async-done(((f32[6144]{0:T(1024)}, f32[2048]{0:T(1024)}, f32[8192]{0:T(1024)}, f32[2048]{0:T(1024)}, f32[2048]{0:T(1024)}, /*index=5*/f32[2048]{0:T(1024)}, f32[2048]{0:T(1024)}), (f32[6144]{0:T(1024)}, ...) | async-done | bytes 98320
  701.6 652.7 %reduce-scatter.10.cloned.1.call-done = f32[16,2048]{1,0:T(8,128)} async-done(((f32[2048,2048]{1,0:T(8,128)}), f32[16,2048]{1,0:T(8,128)}) %reduce-scatter.10.cloned.1.call-update) | async-done | bytes 131088 | tf_op jit(solution)/shard_map/reduce_scatter | solution.py:253
  1354.3 315.1 %reduce-scatter.8.cloned.1.call-done = f32[16,6144]{1,0:T(8,128)} async-done(((f32[2048,6144]{1,0:T(8,128)}), f32[16,6144]{1,0:T(8,128)}) %reduce-scatter.8.cloned.1.call-update) | async-done | bytes 393232 | tf_op jit(solution)/shard_map/reduce_scatter | solution.py:251
  1669.4 747.1 %reduce-scatter.14.cloned.1.call-done = f32[64,2048]{1,0:T(8,128)} async-done(((f32[8192,2048]{1,0:T(8,128)}), f32[64,2048]{1,0:T(8,128)}) %reduce-scatter.14.cloned.1.call-update) | async-done | bytes 524304 | tf_op jit(solution)/shard_map/reduce_scatter | solution.py:193
  2416.5 748.2 %reduce-scatter.12.cloned.1.call-done = f32[16,8192]{1,0:T(8,128)} async-done(((f32[2048,8192]{1,0:T(8,128)}), f32[16,8192]{1,0:T(8,128)}) %reduce-scatter.12.cloned.1.call-update) | async-done | bytes 524304 | tf_op jit(solution)/shard_map/reduce_scatter | solution.py:191
  (137 shorter events, 57.4 us)
Async XLA Ops:
  7.2 101.6 %all-gather.8.cloned.1.call-start = ((), (), s32[]{:S(2)}) async-start(), calls=%async_computation.5 | async-start | bytes 25362432 | tf_op jit(solution)/shard_map/all_gather | solution.py:107
  7.9 173.2 %all-gather.12.cloned.1.call-start = ((), (), s32[]{:S(2)}) async-start(), calls=%async_computation.7 | async-start | bytes 8454144 | tf_op jit(solution)/shard_map/all_gather | solution.py:109
  8.7 204.4 %all-gather.10.cloned.1.call-start = ((), (), s32[]{:S(2)}) async-start(), calls=%async_computation.6 | async-start | bytes 4718592 | tf_op jit(solution)/shard_map/all_gather | solution.py:144
  86.0 33.1 %copy-start.11 = (f32[2048]{0:T(1024)}, f32[2048]{0:T(1024)S(1)}, u32[]{:S(2)}) copy-start(f32[2048]{0:T(1024)S(1)} %convert_element_type.161) | copy-start | bytes 24580
  119.6 1.7 copy-start.3
  123.5 57.6 %copy-start.5 = (bf16[1,128,2048]{2,1,0:T(8,128)(2,1)S(1)}, bf16[1,128,2048]{2,1,0:T(8,128)(2,1)}, u32[]{:S(2)}) copy-start(bf16[1,128,2048]{2,1,0:T(8,128)(2,1)} %param.29) | copy-start | bytes 1572868
  124.8 126.4 %all-gather.18.cloned.1.call-start = ((), (), s32[]{:S(2)}) async-start(), calls=%async_computation.15 | async-start | bytes 4718592 | tf_op jit(solution)/shard_map/all_gather | solution.py:145
  127.4 234.4 %all-gather.14.cloned.1.call-start = ((), (), s32[]{:S(2)}) async-start(), calls=%async_computation.8 | async-start | bytes 33816576 | tf_op jit(solution)/shard_map/all_gather | solution.py:120
  128.0 342.8 %all-gather.16.cloned.1.call-start = ((), (), s32[]{:S(2)}) async-start(), calls=%async_computation.9 | async-start | bytes 33816576 | tf_op jit(solution)/shard_map/all_gather | solution.py:122
  128.6 395.4 %reduce-scatter.6.cloned.1.call-start = ((), (), s32[]{:S(2)}) async-start(), calls=%async_computation.10 | async-start | bytes 9437184 | tf_op jit(solution)/shard_map/reduce_scatter | solution.py:221
  216.6 3.3 copy-start
  251.2 8.0 slice-start
  251.2 8.0 slice-start.1
  261.3 2.0 copy-start.2
  275.0 418.3 %all-reduce.19.cloned.1.call-start = ((), (), s32[]{:S(2)}) async-start(), calls=%async_computation.16 | async-start | bytes 196608
  275.5 86.3 %copy-start.13 = (f32[2048]{0:T(1024)}, f32[2048]{0:T(1024)S(1)}, u32[]{:S(2)}) copy-start(f32[2048]{0:T(1024)S(1)} %convert_element_type.175) | copy-start | bytes 24580
  275.5 6.2 copy-start.9
  281.7 80.1 %copy-start.1 = (bf16[1,128,2048]{2,1,0:T(8,128)(2,1)S(1)}, bf16[1,128,2048]{2,1,0:T(8,128)(2,1)}, u32[]{:S(2)}) copy-start(bf16[1,128,2048]{2,1,0:T(8,128)(2,1)} %param.15) | copy-start | bytes 1572868
  527.0 1.2 copy-start.8
  551.9 802.4 %reduce-scatter.10.cloned.1.call-start = ((), (), s32[]{:S(2)}) async-start(), calls=%async_computation.12 | async-start | bytes 16908288 | tf_op jit(solution)/shard_map/reduce_scatter | solution.py:253
  561.3 0.7 copy-start.12
  561.3 1108.0 %reduce-scatter.8.cloned.1.call-start = ((), (), s32[]{:S(2)}) async-start(), calls=%async_computation.11 | async-start | bytes 50724864 | tf_op jit(solution)/shard_map/reduce_scatter | solution.py:251
  581.6 1.0 copy-start.6
  581.7 1834.8 %reduce-scatter.14.cloned.1.call-start = ((), (), s32[]{:S(2)}) async-start(), calls=%async_computation.14 | async-start | bytes 67633152 | tf_op jit(solution)/shard_map/reduce_scatter | solution.py:193
  611.6 1.6 copy-start.4
  611.6 1.6 copy-start.14
  611.6 2553.1 %reduce-scatter.12.cloned.1.call-start = ((), (), s32[]{:S(2)}) async-start(), calls=%async_computation.13 | async-start | bytes 67633152 | tf_op jit(solution)/shard_map/reduce_scatter | solution.py:191
  636.9 0.7 copy-start.16
  636.9 0.7 copy-start.15
  636.9 1.0 copy-start.7
  637.9 4.8 copy-start.10
  694.0 2471.2 %copy-start.17 = (f32[16]{0:T(128)}, f32[16]{0:T(128)S(1)}, u32[]{:S(2)}) copy-start(f32[16]{0:T(128)S(1)} %dynamic-slice.1) | copy-start | bytes 196
Sparse Core Ops, SparseCore 0:
  11.1 97.6 all-gather.7
  111.8 69.2 all-gather.11
  183.4 29.6 all-gather.9
  215.2 36.0 all-gather.17
  254.0 107.6 all-gather.13
  364.6 106.0 all-gather.15
  473.2 50.7 reduce-scatter.5
  552.1 141.1 all-reduce.18
  696.4 657.9 reduce-scatter.9
  1361.0 308.3 reduce-scatter.7
  1672.5 743.9 reduce-scatter.13
  2419.4 745.2 reduce-scatter.11
where the time goes:
time: 3180 us; the launch traced here: 3170 us
  waiting for transfers between devices  2800 us (88%)
  matrix products  225 us (7%)
  blocking collectives  70.5 us (2%)
  local copies, waits for them, and re-layouts  33.2 us (1%)
    reduce_scatter x1, waiting for transfers between devices, shards(): lax.psum_scatter(grad_w_up, ('batch', 'seq'), scatter_dimension=0, tiled=...  748 us
    reduce_scatter x1, waiting for transfers between devices, shards(): lax.psum_scatter(grad_w_down, ('batch', 'seq'), scatter_dimension=0, tile...  747 us
    reduce_scatter x1, waiting for transfers between devices, shards(): lax.psum_scatter(grad_w_out, ('batch', 'seq'), scatter_dimension=0, tiled...  653 us
    reduce_scatter x1, waiting for transfers between devices, shards(): lax.psum_scatter(grad_w_qkv, ('batch', 'seq'), scatter_dimension=0, tiled...  315 us
    all_gather x1, waiting for transfers between devices, fetch_rows(): lax.all_gather(w_down, ('batch', 'seq'), axis=0, tiled=True)  91.8 us
    dot_general x4, matrix products, over_rows(): lax.dot_general(left, right, (((0,), (0,)), ((), ())), preferred_element_...  81.5 us
    all_gather x1, waiting for transfers between devices, fetch_rows(): lax.all_gather(w_up, ('batch', 'seq'), axis=0, tiled=True)  73.4 us
    unnamed x1, blocking collectives  70.5 us
  transfers between devices with their start and end apart: 12, of which 12 were waited for; matrix products, arithmetic and copies ran while one was open for 8% of the time, Pallas kernels for 0%

commit v1 on v0

v1 whole, which is shorter than its diff:
```python
from functools import partial

import jax
import jax.numpy as jnp
from jax import lax
from jax.sharding import PartitionSpec as P

H = 16
HD = 128
ROT = 32
EPS = 1e-05
F32 = jnp.float32
BF16 = jnp.bfloat16


def tables(positions):
    half_rot = ROT // 2
    exponent = jnp.arange(half_rot).astype(F32) / half_rot
    frequency = jnp.power(10000.0, -exponent)
    angles = positions.astype(F32)[..., None] * frequency
    return (jnp.cos(angles)[..., None, :], jnp.sin(angles)[..., None, :])


def rotate(tensor, cos_tab, sine_tab):
    half_rot = ROT // 2
    first_half = tensor[..., :half_rot]
    second_half = tensor[..., half_rot:ROT]
    return jnp.concatenate(
        [
            first_half * cos_tab - second_half * sine_tab,
            second_half * cos_tab + first_half * sine_tab,
            tensor[..., ROT:],
        ],
        -1,
    )


def over_rows(left, right):
    return lax.dot_general(
        left, right, (((0,), (0,)), ((), ())), preferred_element_type=F32
    )


def against(left, right):
    return lax.dot_general(
        left, right, (((1,), (1,)), ((), ())), preferred_element_type=F32
    )


def plain(left, right):
    return jnp.dot(left, right, preferred_element_type=F32)


def norm_stats(rows):
    average = jnp.mean(rows, -1, keepdims=True)
    centred = rows - average
    inverse = lax.rsqrt(jnp.mean(centred * centred, -1, keepdims=True) + EPS)
    return centred * inverse, inverse


def shards(
    inputs,
    positions,
    w_qkv,
    b_qkv,
    w_out,
    b_out,
    w_up,
    b_up,
    w_down,
    b_down,
    gain_attn,
    shift_attn,
    gain_mlp,
    shift_mlp,
    grad_out,
):
    _, block_len, width = inputs.shape
    groups = lax.axis_size("batch")
    parts = lax.axis_size("seq")
    every = ("batch", "seq")
    me = lax.axis_index("seq")
    heads = H // parts
    length = block_len * parts
    scaling = HD ** (-0.5)

    x_local = inputs[0]
    g_local = grad_out[0]
    x_rows = lax.all_gather(x_local, "seq", axis=0, tiled=True)
    g_rows = lax.all_gather(g_local, "seq", axis=0, tiled=True)
    pos_rows = lax.all_gather(positions[0], "seq", axis=0, tiled=True)

    small = jnp.concatenate(
        [b_out, b_down, gain_attn, shift_attn, gain_mlp, shift_mlp, b_qkv]
    )
    small = lax.all_gather(small, every, axis=0, tiled=False).astype(F32)
    rows16 = b_out.shape[0]
    b_out_f, b_down_f, gain_a, shift_a, gain_m, shift_m = [
        small[:, i * rows16 : (i + 1) * rows16].reshape(-1) for i in range(6)
    ]
    b_qkv_f = small[:, 6 * rows16 :].reshape(3, parts, heads * HD)
    b_qkv_f = lax.dynamic_index_in_dim(b_qkv_f, me, 1, keepdims=False).reshape(-1)
    b_up_f = lax.all_gather(b_up, "batch", axis=0, tiled=True).astype(F32)

    unit = b_up.shape[0]
    w_up_t = w_up.reshape(-1, groups, parts, unit)
    w_up_t = lax.all_to_all(w_up_t, "seq", split_axis=2, concat_axis=0, tiled=True)
    w_up_t = w_up_t.reshape(-1, groups * unit)
    w_up_f = lax.all_gather(w_up_t, "batch", axis=0, tiled=True)
    w_down_f = lax.all_gather(w_down, "batch", axis=0, tiled=True)
    w_qkv_t = w_qkv.reshape(-1, 3, parts, heads * HD)
    w_qkv_t = lax.all_to_all(w_qkv_t, "seq", split_axis=2, concat_axis=0, tiled=True)
    w_qkv_t = w_qkv_t.reshape(-1, 3 * heads * HD)
    w_qkv_f = lax.all_gather(w_qkv_t, "batch", axis=0, tiled=True)
    there = [
        (b * parts + s, ((b % heads) * parts + s) * parts + b // heads)
        for b in range(groups)
        for s in range(parts)
    ]
    w_out_t = lax.ppermute(w_out, every, there)
    w_out_f = lax.all_gather(w_out_t, "batch", axis=0, tiled=True)

    normed, _ = norm_stats(x_rows.astype(F32))
    first_in = (normed * gain_a + shift_a).astype(BF16)
    second_in = (normed * gain_m + shift_m).astype(BF16)

    hidden = plain(second_in, w_up_f) + b_up_f
    active, gelu_pull = jax.vjp(partial(jax.nn.gelu, approximate=False), hidden)
    active_low = active.astype(BF16)
    grad_active = against(g_rows, w_down_f)
    (grad_hidden,) = gelu_pull(grad_active)
    grad_b_up = jnp.sum(grad_hidden, 0)
    grad_hidden_low = grad_hidden.astype(BF16)
    grad_w_down = over_rows(active_low, g_rows).astype(BF16)
    grad_w_down = lax.psum_scatter(grad_w_down, "batch", scatter_dimension=0, tiled=True)
    grad_w_up = over_rows(second_in, grad_hidden_low).astype(BF16)
    grad_w_up = lax.psum_scatter(grad_w_up, "batch", scatter_dimension=0, tiled=True)
    fed_forward = plain(active_low, w_down_f)
    grad_second = against(grad_hidden_low, w_up_f)

    qkv = (plain(first_in, w_qkv_f) + b_qkv_f).reshape(length, 3, heads, HD)
    cos_tab, sine_tab = tables(pos_rows)
    queries = (rotate(qkv[:, 0], cos_tab, sine_tab) * scaling).astype(BF16)
    keys = rotate(qkv[:, 1], cos_tab, sine_tab).astype(BF16)
    values = qkv[:, 2].astype(BF16)
    token = jnp.arange(length)
    visible = token[:, None] >= token[None, :]
    scores = jnp.einsum("qhd,khd->hqk", queries, keys, preferred_element_type=F32)
    scores = jnp.where(visible, scores, -1e30)
    exponent = jnp.exp(scores - jnp.max(scores, -1, keepdims=True))
    probs = exponent / jnp.sum(exponent, -1, keepdims=True)
    probs_low = probs.astype(BF16)
    mixture = jnp.einsum("hqk,khd->qhd", probs_low, values, preferred_element_type=F32)
    mixture = mixture.reshape(length, -1).astype(BF16)
    grad_w_out = over_rows(mixture, g_rows).astype(BF16)
    grad_w_out = lax.psum_scatter(grad_w_out, "batch", scatter_dimension=0, tiled=True)
    attended = plain(mixture, w_out_f)
    grad_mixture = against(g_rows, w_out_f).astype(BF16).reshape(length, heads, HD)
    grad_probs = jnp.einsum("qhd,khd->hqk", grad_mixture, values, preferred_element_type=F32)
    row_delta = jnp.sum(probs * grad_probs, -1, keepdims=True)
    grad_scores = (probs * (grad_probs - row_delta)).astype(BF16)
    grad_query = (
        jnp.einsum("hqk,khd->qhd", grad_scores, keys, preferred_element_type=F32) * scaling
    )
    grad_key = jnp.einsum("hqk,qhd->khd", grad_scores, queries, preferred_element_type=F32)
    grad_value = jnp.einsum("hqk,qhd->khd", probs_low, grad_mixture, preferred_element_type=F32)
    grad_qkv = jnp.stack(
        [
            rotate(grad_query, cos_tab, -sine_tab),
            rotate(grad_key, cos_tab, -sine_tab),
            grad_value,
        ],
        1,
    ).reshape(length, -1)
    grad_b_qkv = jnp.sum(grad_qkv, 0)
    grad_qkv_low = grad_qkv.astype(BF16)
    grad_w_qkv = over_rows(first_in, grad_qkv_low).astype(BF16)
    grad_w_qkv = lax.psum_scatter(grad_w_qkv, "batch", scatter_dimension=0, tiled=True)
    grad_first = against(grad_qkv_low, w_qkv_f)

    summed = (attended + fed_forward).astype(BF16)
    summed = lax.psum_scatter(summed, "seq", scatter_dimension=0, tiled=True)
    x_f = x_local.astype(F32)
    layer_out = (x_f + summed.astype(F32) + (b_out_f + b_down_f)).astype(BF16)

    back = (grad_first * gain_a + grad_second * gain_m).astype(BF16)
    back = lax.psum_scatter(back, "seq", scatter_dimension=0, tiled=True).astype(F32)
    n_local, r_local = norm_stats(x_f)
    back = r_local * (
        back
        - jnp.mean(back, -1, keepdims=True)
        - n_local * jnp.mean(back * n_local, -1, keepdims=True)
    )
    g_f = g_local.astype(F32)
    grad_in = (g_f + back).astype(BF16)

    grad_w_up = grad_w_up.reshape(parts, -1, groups, 1, unit)
    grad_w_up = lax.all_to_all(grad_w_up, "seq", split_axis=0, concat_axis=3, tiled=True)
    grad_w_up = grad_w_up.reshape(w_up.shape).astype(F32)
    grad_w_qkv = grad_w_qkv.reshape(parts, -1, 3, 1, heads * HD)
    grad_w_qkv = lax.all_to_all(grad_w_qkv, "seq", split_axis=0, concat_axis=3, tiled=True)
    grad_w_qkv = grad_w_qkv.reshape(w_qkv.shape).astype(F32)
    grad_w_out = lax.ppermute(grad_w_out, every, [(d, s) for s, d in there]).astype(F32)

    spread_qkv = jnp.zeros((3, parts, heads * HD), F32)
    spread_qkv = lax.dynamic_update_index_in_dim(
        spread_qkv, grad_b_qkv.reshape(3, 1, -1), me, 1
    )
    spread_up = jnp.zeros((groups, parts, unit), F32)
    spread_up = lax.dynamic_update_index_in_dim(
        spread_up, grad_b_up.reshape(groups, 1, unit), me, 1
    )
    count = groups * parts
    packed = [
        jnp.sum(g_f, 0),
        jnp.sum(grad_first * normed, 0),
        jnp.sum(grad_first, 0),
        jnp.sum(grad_second * normed, 0),
        jnp.sum(grad_second, 0),
        spread_qkv,
        spread_up,
    ]
    packed = jnp.concatenate([p.reshape(count, -1) for p in packed], 1)
    packed = lax.psum_scatter(packed, every, scatter_dimension=0, tiled=True).reshape(-1)
    pieces = [packed[i * rows16 : (i + 1) * rows16] for i in range(5)]
    out_b_qkv = packed[5 * rows16 : 5 * rows16 + b_qkv.shape[0]]
    out_b_up = packed[5 * rows16 + b_qkv.shape[0] :]
    return (
        layer_out[None],
        grad_in[None],
        grad_w_qkv,
        out_b_qkv,
        grad_w_out,
        pieces[0],
        grad_w_up,
        out_b_up,
        grad_w_down.astype(F32),
        pieces[0],
        pieces[1],
        pieces[2],
        pieces[3],
        pieces[4],
    )


def solution(mesh):
    both = ("batch", "seq")
    rows = P("batch", "seq", None)
    matrix = P(both, None)
    vector = P(both)
    return jax.shard_map(
        shards,
        mesh=mesh,
        in_specs=(
            rows,
            P("batch", "seq"),
            matrix,
            vector,
            matrix,
            vector,
            matrix,
            vector,
            matrix,
            vector,
            vector,
            vector,
            vector,
            vector,
            rows,
        ),
        out_specs=(
            rows,
            rows,
            matrix,
            vector,
            matrix,
            vector,
            matrix,
            vector,
            matrix,
            vector,
            vector,
            vector,
            vector,
            vector,
        ),
        check_vma=False,
    )
```

time: 3180 us -> 861 us (0.27)
  waiting for transfers between devices: 2800 us -> 489 us
  matrix products: 225 us -> 126 us
  blocking collectives: 70.5 us -> 141 us
    reduce_scatter x5 -> x6, waiting for transfers between devices: 2470 us -> 356 us  [the longest x1 78.9 us: shards(): lax.psum_scatter(grad_w_down, 'batch', scatter_dimension=0, tiled=True)]
    all_gather x6, waiting for transfers between devices: 291 us -> 32.8 us  [the longest x1 32.8 us: shards(): w_down_f = lax.all_gather(w_down, 'batch', axis=0, tiled=True)]
    unnamed x13 -> x14, waiting for transfers between devices: 35.3 us -> 95.6 us
    dot_general x4, matrix products: 81.5 us -> 28.5 us  [over_rows(): lax.dot_general(left, right, (((0,), (0,)), ((), ())), preferred_element_...]
    dot_general x10 -> x9, matrix products: 78.5 us -> 49.6 us  [the longest x4 35.1 us: plain(): return jnp.dot(left, right, preferred_element_type=F32)]
    unnamed x1 -> x2, blocking collectives: 70.5 us -> 98.2 us
  transfers between devices with their start and end apart: 12 -> 17, of which waited for: 12 -> 10; matrix products, arithmetic and copies ran while one was open for 8% -> 17% of each run, Pallas kernels for 0% -> 0%
where the time goes in v1:
time: 861 us; the launch traced here: 855 us
  waiting for transfers between devices  489 us (57%)
  blocking collectives  141 us (16%)
  matrix products  126 us (15%)
  local copies, waits for them, and re-layouts  34.4 us (4%)
  starting transfers between devices  24.9 us (3%)
  other arithmetic  23.5 us (3%)
  between operations  15.7 us (2%)
    unnamed x2, blocking collectives  98.2 us
    unnamed x14, waiting for transfers between devices  95.6 us
    reduce_scatter x1, waiting for transfers between devices, shards(): lax.psum_scatter(grad_w_down, 'batch', scatter_dimension=0, tiled=True)  78.9 us
    reduce_scatter x1, waiting for transfers between devices, shards(): lax.psum_scatter(grad_w_qkv, 'batch', scatter_dimension=0, tiled=True)  73.9 us
    reduce_scatter x1, waiting for transfers between devices, shards(): lax.psum_scatter(grad_w_up, 'batch', scatter_dimension=0, tiled=True)  70.5 us
    reduce_scatter x1, waiting for transfers between devices, shards(): lax.psum_scatter(grad_w_out, 'batch', scatter_dimension=0, tiled=True)  66.3 us
    dot_general x4, matrix products, against(): lax.dot_general(left, right, (((1,), (1,)), ((), ())), preferred_element_...  39.7 us
    reduce_scatter x1, waiting for transfers between devices, shards(): summed = lax.psum_scatter(summed, 'seq', scatter_dimension=0, tiled=True)  36.9 us
  transfers between devices with their start and end apart: 17, of which 10 were waited for; matrix products, arithmetic and copies ran while one was open for 17% of the time, Pallas kernels for 0%

profile of v1, /device:TPU:1, one launch (start us, length us, event | category | flops | bytes accessed | tf_op | source)
XLA Modules:
  0.0 854.7 jit_solution(7171833479297534842)
XLA Ops:
  9.0 11.8 %all_to_all.48 = bf16[16,3,8,256]{3,0,1,2:T(8,128)(2,1)S(1)} all-to-all(bf16[16,3,8,256]{3,0,1,2:T(8,128)(2,1)S(1)} %copy.119), channel_id=1, replica_groups=mesh['batch'=16,'seq'=8] {'seq'}, dimensions={2} | all-to-all | bytes 393216 | tf_op jit(solution)/shard_map/all_to_all | solution.py:112
  21.7 4.4 collective-permute-start
  26.1 4.1 collective-permute-done
  33.5 14.2 %all_to_all.49 = bf16[8,2,8192]{2,1,0:T(2,128)(2,1)S(1)} all-to-all(bf16[8,2,8192]{2,1,0:T(2,128)(2,1)S(1)} %reshape.278), channel_id=1, replica_groups=mesh['batch'=16,'seq'=8] {'seq'}, dimensions={0} | all-to-all | bytes 524288 | tf_op jit(solution)/shard_map/all_to_all | solution.py:107
  50.4 67.1 %all-reduce = bf16[18432]{0:T(1024)(128)(2,1)S(1)} all-reduce(bf16[18432]{0:T(1024)(128)(2,1)S(1)} %dynamic-update-slice), channel_id=3, replica_groups=mesh['batch'=16,'seq'=8] {'batch','seq'}, use_global_device_ids=true, to_apply=%add | all-reduce | flops 18432 | bytes 73728
  121.3 31.0 %all-reduce.1 = bf16[1024]{0:T(1024)(128)(2,1)S(1)} all-reduce(bf16[1024]{0:T(1024)(128)(2,1)S(1)} %dynamic-update-slice.1), channel_id=1, replica_groups=mesh['batch'=16,'seq'=8] {'batch'}, use_global_device_ids=true, to_apply=%add.1 | all-reduce | flops 1024 | bytes 4096
  152.3 16.8 %all-gather.2 = s32[1,1024]{1,0:T(1,128)S(1)} all-gather(s32[1,128]{1,0:T(1,128)S(1)} %copy-done.12), channel_id=4, replica_groups=mesh['batch'=16,'seq'=8] {'seq'}, dimensions={1}, use_global_device_ids=true | all-gather | bytes 4608 | tf_op jit(solution)/shard_map/all_gather | solution.py:91
  176.3 7.2 convolution_add_fusion
  192.0 8.1 fusion.94
  200.2 4.3 fusion.57
  204.5 5.2 multiply_reduce_fusion
  225.2 9.2 %fusion.97 = f32[1024,2048]{1,0:T(8,128)} fusion(bf16[1024,768]{0,1:T(8,128)(2,1)} %bitcast.220, bf16[2048,768]{1,0:T(8,128)(2,1)} %all-gather.11.cloned.1.call-done), kind=kOutput, calls=%fused_computation.146 | convolution fusion | flops 3221225472 | bytes 13107200 | tf_op jit(solution)/shard_map/dot_general | solution.py:45
  234.3 18.2 %multiply_convert_fusion.1 = (bf16[1024,1024]{1,0:T(8,128)(2,1)}, f32[1024,1024]{1,0:T(8,128)}, f32[1024,1024]{1,0:T(8,128)}) fusion(f32[1024]{0:T(1024)S(1)} %convert_element_type.142, bf16[2048,1024]{1,0:T(8,128)(2,1)} %all-gather.15.cloned.1.call-done, bf16[1,1024,2048]{2,1,0:T(8,128)(2,1)} %all-gather.19.cloned.1.call-done, f32[2048]{0:T(1024)S(1)} %add.135, ...), kind=kOutput, calls=%fused_computation.35 | convolution fusion | flops 4376756224 | bytes 18903040 | tf_op jit(solution)/shard_map/dot_general | solution.py:51
  252.5 32.8 %all-gather.17.cloned.1.call-done = bf16[1024,2048]{1,0:T(8,128)(2,1)} async-done(((bf16[64,2048]{1,0:T(8,128)(2,1)}), bf16[1024,2048]{1,0:T(8,128)(2,1)}) %all-gather.17.cloned.1.call-update) | async-done | bytes 4194320 | tf_op jit(solution)/shard_map/all_gather | solution.py:110
  285.3 13.0 %fusion.95 = (f32[1024]{0:T(1024)S(1)}, bf16[1024,1024]{1,0:T(8,128)(2,1)}) fusion(f32[1024,1024]{1,0:T(8,128)} %get-tuple-element.21, bf16[1024,2048]{1,0:T(8,128)(2,1)} %all-gather.17.cloned.1.call-done, bf16[1,1024,2048]{2,1,0:T(8,128)(2,1)} %all-gather.21.cloned.1.call-done, f32[1024,1024]{1,0:T(8,128)} %get-tuple-element.54, ...), kind=kOutput, calls=%fused_computation.141 | convolution fusion | flops 4311743488 | bytes 18882560 | tf_op jit(solution)/shard_map/dot_general | solution.py:45
  298.4 13.2 %fusion.90 = (f32[2048]{0:T(1024)S(1)}, f32[2048]{0:T(1024)S(1)}, bf16[1024,2048]{1,0:T(8,128)(2,1)}, f32[2048]{0:T(1024)S(1)}, f32[2048]{0:T(1024)S(1)}) fusion(f32[1024]{0:T(1024)S(1)} %add_rsqrt_fusion, f32[1024]{0:T(1024)S(1)} %broadcast_multiply_fusion, bf16[1,1024,2048]{2,1,0:T(8,128)(2,1)} %all-gather.19.cloned.1.call-done, f32[2048]{0:T(1024)S(1)} %mul.267, ...), kind=kOutput, calls=%fused_computation.137 | convolution fusion | flops 4322222080 | bytes 23126016 | tf_op jit(solution)/shard_map/dot_general | solution.py:45
  313.1 8.5 convolution_convert_fusion.1
  321.7 4.6 fusion.54
  328.9 9.5 %convolution_convert_fusion = bf16[2048,1024]{1,0:T(8,128)(2,1)} fusion(bf16[1024,1024]{1,0:T(8,128)(2,1)S(1)} %copy-done.25, bf16[1,1024,2048]{2,1,0:T(8,128)(2,1)} %all-gather.19.cloned.1.call-done, f32[2048]{0:T(1024)S(1)} %add.135, f32[2048]{0:T(1024)S(1)} %mul.267, f32[1024]{0:T(1024)S(1)} %add_rsqrt_fusion, f32[1024]{0:T(1024)S(1)} %broadcast_multiply_fusion), kind=kOutput, calls=%fused_computation.54 | convolution fusion | flops 4309647360 | bytes 10510336 | tf_op jit(solution)/shard_map/dot_general | solution.py:39
  340.0 6.4 fusion.96
  346.4 3.3 add_convert_fusion.1
  349.7 8.3 fusion.34
  359.6 93.0 %all-reduce.5.cloned.1.call-done = f32[128,192]{1,0:T(8,128)} async-done(((f32[128,192]{1,0:T(8,128)}), f32[128,192]{1,0:T(8,128)}) %all-reduce.5.cloned.1.call-update) | async-done | bytes 98320
  454.1 73.9 %reduce-scatter.11.cloned.1.call-done = bf16[128,768]{1,0:T(8,128)(2,1)} async-done(((bf16[2048,768]{1,0:T(8,128)(2,1)}), bf16[128,768]{1,0:T(8,128)(2,1)}) %reduce-scatter.11.cloned.1.call-update) | async-done | bytes 196624 | tf_op jit(solution)/shard_map/reduce_scatter | solution.py:178
  529.7 6.6 all-to-all-start.2
  537.6 66.3 %reduce-scatter.13.cloned.1.call-done = bf16[16,2048]{1,0:T(8,128)(2,1)} async-done(((bf16[256,2048]{1,0:T(8,128)(2,1)}), bf16[16,2048]{1,0:T(8,128)(2,1)}) %reduce-scatter.13.cloned.1.call-update) | async-done | bytes 65552 | tf_op jit(solution)/shard_map/reduce_scatter | solution.py:156
  603.9 6.3 collective-permute-start.1
  613.6 70.5 %reduce-scatter.15.cloned.1.call-done = bf16[128,1024]{1,0:T(8,128)(2,1)} async-done(((bf16[2048,1024]{1,0:T(8,128)(2,1)}), bf16[128,1024]{1,0:T(8,128)(2,1)}) %reduce-scatter.15.cloned.1.call-update) | async-done | bytes 262160 | tf_op jit(solution)/shard_map/reduce_scatter | solution.py:137
  686.6 6.6 all-to-all-start.3
  693.2 30.0 %reduce-scatter.9.cloned.1.call-done = bf16[128,2048]{1,0:T(8,128)(2,1)} async-done(((bf16[1024,2048]{1,0:T(8,128)(2,1)}), bf16[128,2048]{1,0:T(8,128)(2,1)}) %reduce-scatter.9.cloned.1.call-update) | async-done | bytes 524304 | tf_op jit(solution)/shard_map/reduce_scatter | solution.py:187
  724.6 36.9 %reduce-scatter.7.cloned.1.call-done = bf16[128,2048]{1,0:T(8,128)(2,1)} async-done(((bf16[1024,2048]{1,0:T(8,128)(2,1)}), bf16[128,2048]{1,0:T(8,128)(2,1)}) %reduce-scatter.7.cloned.1.call-update) | async-done | bytes 524304 | tf_op jit(solution)/shard_map/reduce_scatter | solution.py:182
  764.3 78.9 %reduce-scatter.17.cloned.1.call-done = bf16[64,2048]{1,0:T(8,128)(2,1)} async-done(((bf16[1024,2048]{1,0:T(8,128)(2,1)}), bf16[64,2048]{1,0:T(8,128)(2,1)}) %reduce-scatter.17.cloned.1.call-update) | async-done | bytes 262160 | tf_op jit(solution)/shard_map/reduce_scatter | solution.py:135
  (188 shorter events, 68.7 us)
Async XLA Ops:
  7.2 164.3 %all-gather.19.cloned.1.call-start = ((), (), s32[]{:S(2)}) async-start(), calls=%async_computation.20 | async-start | bytes 4718592 | tf_op jit(solution)/shard_map/all_gather | solution.py:89
  7.9 168.4 %all-gather.11.cloned.1.call-start = ((), (), s32[]{:S(2)}) async-start(), calls=%async_computation.10 | async-start | bytes 3342336 | tf_op jit(solution)/shard_map/all_gather | solution.py:114
  9.0 40.9 %copy-start.2 = (bf16[1,128,2048]{2,1,0:T(8,128)(2,1)S(1)}, bf16[1,128,2048]{2,1,0:T(8,128)(2,1)}, u32[]{:S(2)}) copy-start(bf16[1,128,2048]{2,1,0:T(8,128)(2,1)} %param.29) | copy-start | bytes 1572868
  20.8 29.2 %copy-start.13 = (bf16[16]{0:T(256)(128)(2,1)S(1)}, bf16[16]{0:T(256)(128)(2,1)}, u32[]{:S(2)}) copy-start(bf16[16]{0:T(256)(128)(2,1)} %param.20) | copy-start | bytes 100
  20.8 29.2 %copy-start.14 = (bf16[16]{0:T(256)(128)(2,1)S(1)}, bf16[16]{0:T(256)(128)(2,1)}, u32[]{:S(2)}) copy-start(bf16[16]{0:T(256)(128)(2,1)} %param.24) | copy-start | bytes 100
  20.8 29.3 %copy-start.15 = (bf16[16]{0:T(256)(128)(2,1)S(1)}, bf16[16]{0:T(256)(128)(2,1)}, u32[]{:S(2)}) copy-start(bf16[16]{0:T(256)(128)(2,1)} %param.25) | copy-start | bytes 100
  20.8 29.3 %copy-start.16 = (bf16[16]{0:T(256)(128)(2,1)S(1)}, bf16[16]{0:T(256)(128)(2,1)}, u32[]{:S(2)}) copy-start(bf16[16]{0:T(256)(128)(2,1)} %param.26) | copy-start | bytes 100
  20.8 29.3 %copy-start.17 = (bf16[16]{0:T(256)(128)(2,1)S(1)}, bf16[16]{0:T(256)(128)(2,1)}, u32[]{:S(2)}) copy-start(bf16[16]{0:T(256)(128)(2,1)} %param.27) | copy-start | bytes 100
  20.8 29.3 %copy-start.18 = (bf16[16]{0:T(256)(128)(2,1)S(1)}, bf16[16]{0:T(256)(128)(2,1)}, u32[]{:S(2)}) copy-start(bf16[16]{0:T(256)(128)(2,1)} %param.28) | copy-start | bytes 100
  20.8 29.3 %copy-start.19 = (bf16[48]{0:T(256)(128)(2,1)S(1)}, bf16[48]{0:T(256)(128)(2,1)}, u32[]{:S(2)}) copy-start(bf16[48]{0:T(256)(128)(2,1)} %param.18) | copy-start | bytes 292
  21.7 178.5 %all-gather.13.cloned.1.call-start = ((), (), s32[]{:S(2)}) async-start(), calls=%async_computation.11 | async-start | bytes 1114112 | tf_op jit(solution)/shard_map/all_gather | solution.py:121
  21.7 8.5 collective-permute-start
  30.9 169.2 %all-gather.21.cloned.1.call-start = ((), (), s32[]{:S(2)}) async-start(), calls=%async_computation.21 | async-start | bytes 4718592 | tf_op jit(solution)/shard_map/all_gather | solution.py:90
  31.5 202.8 %all-gather.15.cloned.1.call-start = ((), (), s32[]{:S(2)}) async-start(), calls=%async_computation.12 | async-start | bytes 4456448 | tf_op jit(solution)/shard_map/all_gather | solution.py:109
  33.0 86.8 %copy-start.23 = (u32[128]{0:T(128)S(1)}, u32[128]{0:T(128)}, u32[]{:S(2)}) copy-start(u32[128]{0:T(128)} %constant.127) | copy-start | bytes 1540
  33.0 88.0 %copy-start.22 = (bf16[64]{0:T(256)(128)(2,1)S(1)}, bf16[64]{0:T(256)(128)(2,1)}, u32[]{:S(2)}) copy-start(bf16[64]{0:T(256)(128)(2,1)} %param.22) | copy-start | bytes 388
  33.1 119.3 %copy-start.12 = (s32[1,128]{1,0:T(1,128)S(1)}, s32[1,128]{1,0:T(1,128)}, u32[]{:S(2)}) copy-start(s32[1,128]{1,0:T(1,128)} %param.16) | copy-start | bytes 1540
  49.3 236.1 %all-gather.17.cloned.1.call-start = ((), (), s32[]{:S(2)}) async-start(), calls=%async_computation.13 | async-start | bytes 4456448 | tf_op jit(solution)/shard_map/all_gather | solution.py:110
  49.8 402.8 %all-reduce.5.cloned.1.call-start = ((), (), s32[]{:S(2)}) async-start(), calls=%async_computation.22 | async-start | bytes 262144
  298.4 14.7 %copy-start.7 = (bf16[1024,3,2,128]{0,3,2,1:T(8,128)(2,1)S(1)}, bf16[1024,3,2,128]{0,3,2,1:T(8,128)(2,1)}, u32[]{:S(2)}) copy-start(bf16[1024,3,2,128]{0,3,2,1:T(8,128)(2,1)} %copy.138) | copy-start | bytes 4718596
  312.9 215.1 %reduce-scatter.11.cloned.1.call-start = ((), (), s32[]{:S(2)}) async-start(), calls=%async_computation.16 | async-start | bytes 3342336 | tf_op jit(solution)/shard_map/reduce_scatter | solution.py:178
  321.6 282.3 %reduce-scatter.13.cloned.1.call-start = ((), (), s32[]{:S(2)}) async-start(), calls=%async_computation.17 | async-start | bytes 1114112 | tf_op jit(solution)/shard_map/reduce_scatter | solution.py:156
  328.9 355.3 %reduce-scatter.15.cloned.1.call-start = ((), (), s32[]{:S(2)}) async-start(), calls=%async_computation.18 | async-start | bytes 4456448 | tf_op jit(solution)/shard_map/reduce_scatter | solution.py:137
  338.4 384.8 %reduce-scatter.9.cloned.1.call-start = ((), (), s32[]{:S(2)}) async-start(), calls=%async_computation.15 | async-start | bytes 4718592 | tf_op jit(solution)/shard_map/reduce_scatter | solution.py:187
  339.2 422.4 %reduce-scatter.7.cloned.1.call-start = ((), (), s32[]{:S(2)}) async-start(), calls=%async_computation.14 | async-start | bytes 4718592 | tf_op jit(solution)/shard_map/reduce_scatter | solution.py:182
  340.0 6.4 copy-start.9
  349.7 493.5 %reduce-scatter.17.cloned.1.call-start = ((), (), s32[]{:S(2)}) async-start(), calls=%async_computation.19 | async-start | bytes 4456448 | tf_op jit(solution)/shard_map/reduce_scatter | solution.py:135
  359.3 402.2 %copy-start.3 = (bf16[1,128,2048]{2,1,0:T(8,128)(2,1)S(1)}, bf16[1,128,2048]{2,1,0:T(8,128)(2,1)}, u32[]{:S(2)}) copy-start(bf16[1,128,2048]{2,1,0:T(8,128)(2,1)} %param.29) | copy-start | bytes 1572868
  454.1 393.1 %copy-start.20 = (f32[16]{0:T(128)}, f32[16]{0:T(128)S(1)}, u32[]{:S(2)}) copy-start(f32[16]{0:T(128)S(1)} %get-tuple-element.88) | copy-start | bytes 196
  529.7 82.8 %all-to-all-start.2 = ((bf16[8,16,3,1,256]{4,1,3,2,0:T(8,128)(2,1)}), bf16[8,16,3,1,256]{4,1,3,2,0:T(8,128)(2,1)S(1)}, u32[]{:S(2)}, u32[]{:S(2)}) async-start(bf16[8,16,3,1,256]{4,1,3,2,0:T(8,128)(2,1)} %copy.139), calls=%async_computation.5 | async-start | bytes 393216 | tf_op jit(solution)/shard_map/all_to_all | solution.py:201
  603.9 8.0 collective-permute-start.1
  686.6 158.4 %all-to-all-start.3 = ((bf16[8,2,8192]{2,1,0:T(2,128)(2,1)}), bf16[8,2,8192]{2,1,0:T(2,128)(2,1)S(1)}, u32[]{:S(2)}, u32[]{:S(2)}) async-start(bf16[8,2,8192]{2,1,0:T(2,128)(2,1)} %reshape.280), calls=%async_computation.8 | async-start | bytes 524288 | tf_op jit(solution)/shard_map/all_to_all | solution.py:198
  (13 other events, 33.5 us)
Sparse Core Ops, SparseCore 0:
  9.7 39.0 all-gather.18
  51.6 48.6 all-gather.10
  103.0 40.2 all-gather.12
  144.8 33.4 all-gather.20
  180.8 51.1 all-gather.14
  234.0 51.2 all-gather.16
  313.0 139.6 all-reduce.4
  456.4 71.5 reduce-scatter.10
  531.5 72.3 reduce-scatter.12
  607.1 76.9 reduce-scatter.14
  686.7 36.4 reduce-scatter.8
  725.6 35.9 reduce-scatter.6
  765.3 77.9 reduce-scatter.16

commit v2 on v1

v2 whole, which is shorter than its diff:
```python
import functools

import jax
import jax.numpy as jnp
from jax import lax
from jax.experimental import pallas as pl
from jax.experimental.pallas import tpu as pltpu
from jax.sharding import PartitionSpec as P

H = 16
HD = 128
ROT = 32
EPS = 1e-05
F32 = jnp.float32
BF16 = jnp.bfloat16
MESH = pl.DeviceIdType.MESH
STEPS = (1, -1, 2)
SEQ_PEERS = [(dy, dc) for dc in (1, 0) for dy in (0, 1, -1, 2) if (dy, dc) != (0, 0)]


def place():
    b = lax.axis_index("batch")
    s = lax.axis_index("seq")
    return b // 4, b % 4, s // 2, s % 2


def shifted(x=0, z=0, y=0, c=0):
    px, pz, py, pc = place()
    px = lax.rem(px + x + 4, 4)
    pz = lax.rem(pz + z + 4, 4)
    py = lax.rem(py + y + 4, 4)
    pc = lax.rem(pc + c, 2)
    return (px * 4 + pz, py * 2 + pc)


def moved(pos, step):
    return lax.rem(pos + step + 4, 4)


class Copies:
    def __init__(self, send, recv):
        self.send, self.recv, self.count, self.made = send, recv, 0, []

    def make(self, src, dst, device):
        k = self.count
        self.count += 1
        return pltpu.make_async_remote_copy(
            src_ref=src,
            dst_ref=dst,
            send_sem=self.send.at[k],
            recv_sem=self.recv.at[k],
            device_id=device,
            device_id_type=MESH,
        )

    def start(self, src, dst, device):
        copy = self.make(src, dst, device)
        copy.start()
        self.made.append(copy)
        return copy

    def drain(self):
        for copy in self.made:
            copy.wait_send()


class Locals:
    def __init__(self, sems):
        self.sems, self.count = sems, 0

    def start(self, src, dst):
        copy = pltpu.make_async_copy(src, dst, self.sems.at[self.count])
        self.count += 1
        copy.start()
        return copy


def greet(extra=None):
    barrier = pltpu.get_barrier_semaphore()
    peers = [dict(x=d) for d in STEPS] + [dict(z=d) for d in STEPS]
    peers += [dict(y=dy, c=dc) for dy, dc in SEQ_PEERS]
    for p in peers:
        pl.semaphore_signal(barrier, inc=1, device_id=shifted(**p), device_id_type=MESH)
    count = len(peers)
    if extra is not None:
        differs, source = extra

        @pl.when(differs)
        def _():
            pl.semaphore_signal(barrier, inc=1, device_id=source, device_id_type=MESH)

        count = jnp.where(differs, count + 1, count)
    pl.semaphore_wait(barrier, count)


def group(buf, first, at, half=None, rows=None):
    span = pl.ds(0, 4) if half is None else pl.ds(2 * half, 2)
    index = (span, at) if first == "x" else (at, span)
    if rows is not None:
        index += (pl.ds(*rows),)
    return buf.at[index]


class Gather:
    def __init__(self, copies, buf, first, rows=None):
        self.copies, self.buf, self.first, self.rows = copies, buf, first, rows
        self.other = "z" if first == "x" else "x"
        x, z, _, _ = place()
        self.at = z if first == "x" else x
        self.own = buf.at[x, z] if rows is None else buf.at[x, z, pl.ds(*rows)]

    def part(self, step, half=None):
        return group(self.buf, self.first, moved(self.at, step), half, self.rows)

    def one(self, src=None):
        src = self.own if src is None else src
        self.sent = [self.copies.start(src, self.own, shifted(**{self.first: d})) for d in STEPS]

    def two(self):
        for c in self.sent:
            c.wait_recv()
        mine = self.part(0)
        self.sent = [self.copies.start(mine, mine, shifted(**{self.other: d})) for d in (1, -1)]

    def three(self):
        sent = []
        for c, d, half in zip(self.sent, (1, -1), (0, 1)):
            c.wait_recv()
            passed = self.part(-d, half)
            sent.append(self.copies.start(passed, passed, shifted(**{self.other: d})))
        self.sent = sent

    def done(self):
        for c in self.sent:
            c.wait_recv()


def out_route(groups=16, parts=8, heads=2):
    b = lax.axis_index("batch")
    s = lax.axis_index("seq")
    to = ((b % heads) * parts + s, b // heads)
    source = (s * heads + b // parts, b % parts)
    differs = jnp.logical_or(to[0] != b, to[1] != s)
    return to, source, differs


def gather_kernel(x_ref, g_ref, small_ref, up_ref, qkv_ref, down_ref, out_ref,
                  X, G, SM, UP, QK, DN, WO, send, recv):
    copies = Copies(send, recv)
    x, z, y, c = place()
    s = y * 2 + c
    to, source, differs = out_route()
    greet((differs, source))

    def across(src, dst):
        dst[...] = src[s]
        return [
            copies.start(src.at[moved(y, dy) * 2 + lax.rem(c + dc, 2)], dst, shifted(y=dy, c=dc))
            for dy, dc in SEQ_PEERS
        ]

    SM[x, z, s] = small_ref[...]
    sm = [copies.start(small_ref, SM.at[x, z, s], shifted(y=dy, c=dc)) for dy, dc in SEQ_PEERS]
    up = across(up_ref, UP.at[x, z, pl.ds(s * 16, 16)])
    down = Gather(copies, DN, "x")
    down.one(down_ref)
    DN[x, z] = down_ref[...]
    def seq_one(src, dst):
        dst[s] = src[...]
        return [copies.start(src, dst.at[s], shifted(y=d)) for d in (1, -1)] + [
            copies.start(src, dst.at[s], shifted(c=1))
        ]

    xs = seq_one(x_ref, X)
    qk = across(qkv_ref, QK.at[x, z, pl.ds(s * 16, 16)])
    out_copy = copies.make(out_ref, WO.at[to[0] // 4, to[0] % 4], to)

    @pl.when(differs)
    def _():
        out_copy.start()

    @pl.when(jnp.logical_not(differs))
    def _():
        WO[x, z] = out_ref[...]

    gs = seq_one(g_ref, G)

    for cp in sm:
        cp.wait_recv()
    small = Gather(copies, SM, "z")
    small.one()
    for cp in up:
        cp.wait_recv()
    upg = Gather(copies, UP, "z")
    upg.one()
    small.two()
    down.two()

    def seq_two(sent, dst):
        more = []
        for cp, d in zip(sent[:2], (1, -1)):
            cp.wait_recv()
            got = dst.at[moved(y, -d) * 2 + c]
            more.append(copies.start(got, got, shifted(c=1)))
        up_way = c == 0
        got = dst.at[jnp.where(up_way, moved(y, -1), moved(y, 1)) * 2 + c]
        py = jnp.where(up_way, moved(y, 1), moved(y, -1))
        b = lax.axis_index("batch")
        fwd = copies.start(got, got, (b, py * 2 + c))
        sent[2].wait_recv()
        return more, fwd

    xs2, xf = seq_two(xs, X)
    small.three()
    for cp in qk:
        cp.wait_recv()
    qa = Gather(copies, QK, "x", (0, 64))
    qb = Gather(copies, QK, "z", (64, 64))
    qa.one()
    qb.one()

    @pl.when(differs)
    def _():
        out_copy.wait_recv()
        out_copy.wait_send()

    wo = Gather(copies, WO, "x")
    wo.one()
    gs2, gf = seq_two(gs, G)
    upg.two()

    def seq_three(more, fwd, dst):
        fwd.wait_recv()
        got = dst.at[moved(y, 2) * 2 + c]
        last = copies.start(got, got, shifted(c=1))
        return more + [last]

    xs3 = seq_three(xs2, xf, X)
    down.three()
    qa.two()
    qb.two()
    wo.two()
    upg.three()
    gs3 = seq_three(gs2, gf, G)
    small.done()
    for cp in xs3 + gs3:
        cp.wait_recv()
    qa.three()
    qb.three()
    wo.three()
    for gth in (down, upg, qa, qb, wo):
        gth.done()
    copies.drain()


def gather(x, g, small, up, qkv, down, out):
    vm = pl.BlockSpec(memory_space=pltpu.VMEM)
    shapes = [
        ((8,) + x.shape, BF16), ((8,) + g.shape, BF16), ((4, 4, 8) + small.shape, small.dtype),
        ((4, 4, 128, up.shape[-1]), BF16), ((4, 4, 128, qkv.shape[-1]), BF16),
        ((4, 4) + down.shape, BF16), ((4, 4) + out.shape, BF16),
    ]
    return pl.pallas_call(
        gather_kernel,
        out_shape=[jax.ShapeDtypeStruct(*s) for s in shapes],
        in_specs=[vm] * 7,
        out_specs=[vm] * 7,
        scratch_shapes=[pltpu.SemaphoreType.DMA((96,)), pltpu.SemaphoreType.DMA((96,))],
        compiler_params=pltpu.CompilerParams(
            collective_id=1, has_side_effects=True, vmem_limit_bytes=60 * 2**20
        ),
    )(x, g, small, up, qkv, down, out)


class Scatter:
    def __init__(self, copies, local, buf, first, own, land, last, rows=None):
        self.copies, self.buf, self.first, self.rows = copies, buf, first, rows
        self.own, self.land, self.last = own, land, last
        self.other = "z" if first == "x" else "x"
        x, z, _, _ = place()
        self.at, self.mine = (z, x) if first == "x" else (x, z)
        self.local = local

    def one(self):
        self.sent = [
            self.copies.start(
                group(self.buf, self.first, moved(self.at, d), None, self.rows),
                self.land.at[k],
                shifted(**{self.other: d}),
            )
            for k, d in enumerate(STEPS)
        ]
        self.kept = self.local.start(group(self.buf, self.first, self.at, None, self.rows), self.own)

    def two(self):
        self.kept.wait()
        for c in self.sent:
            c.wait_recv()
        own, land = self.own, self.land
        rows = own.shape[1]
        step = min(rows, 16)

        def add(t, _):
            i = t // (rows // step)
            r = pl.ds(pl.multiple_of(t % (rows // step) * step, step), step)
            total = own[i, r].astype(F32) + land[0, i, r].astype(F32)
            total += land[1, i, r].astype(F32) + land[2, i, r].astype(F32)
            own[i, r] = total.astype(own.dtype)
            return 0

        lax.fori_loop(0, 4 * (rows // step), add, 0)
        self.sent = [
            self.copies.start(
                own.at[moved(self.mine, d)], self.last.at[k], shifted(**{self.first: d})
            )
            for k, d in enumerate(STEPS)
        ]

    def three(self, put):
        for c in self.sent:
            c.wait_recv()
        own, last = self.own, self.last
        rows = own.shape[1]
        step = min(rows, 16)

        def add(t, _):
            at = pl.multiple_of(t * step, step)
            r = pl.ds(at, step)
            total = own[self.mine, r].astype(F32) + last[0, r].astype(F32)
            total += last[1, r].astype(F32) + last[2, r].astype(F32)
            put(at, step, total)
            return 0

        lax.fori_loop(0, rows // step, add, 0)


class SeqScatter:
    def __init__(self, copies, local, buf, own, pair, last):
        self.copies, self.local, self.buf = copies, local, buf
        self.own, self.pair, self.last = own, pair, last

    def one(self):
        _, _, _, c = place()
        self.sent = self.copies.start(self.buf.at[:, 1 - c], self.pair, shifted(c=1))
        self.kept = self.local.start(self.buf.at[:, c], self.own)

    def two(self):
        _, _, y, _ = place()
        self.kept.wait()
        self.sent.wait_recv()
        own, pair = self.own, self.pair

        def add(t, _):
            r = pl.ds(pl.multiple_of(t % 8 * 16, 16), 16)
            i = t // 8
            own[i, r] = (own[i, r].astype(F32) + pair[i, r].astype(F32)).astype(BF16)
            return 0

        lax.fori_loop(0, 32, add, 0)
        self.sent = [
            self.copies.start(own.at[moved(y, d)], self.last.at[k], shifted(y=d))
            for k, d in enumerate(STEPS)
        ]

    def three(self, put):
        _, _, y, _ = place()
        for c in self.sent:
            c.wait_recv()
        own, last = self.own, self.last

        def add(t, _):
            at = pl.multiple_of(t * 16, 16)
            r = pl.ds(at, 16)
            total = own[y, r].astype(F32) + last[0, r].astype(F32)
            total += last[1, r].astype(F32) + last[2, r].astype(F32)
            put(at, 16, total)
            return 0

        lax.fori_loop(0, 8, add, 0)


def scatter_kernel(P, Q, GD, GU, GQ, GO, V1, V2,
                   sp, sq, gd, gu, gq, go, sv,
                   p_own, p_pair, p_last, q_own, q_pair, q_last,
                   d_own, d_land, d_last, u_own, u_land, u_last,
                   a_own, a_land, a_last, b_own, b_land, b_last,
                   o_own, o_land, o_last, v_land, C, c_own, c_land, c_last,
                   gu_part, gq_part, go_part,
                   send, recv, loc):
    copies, local = Copies(send, recv), Locals(loc)
    x, z, y, c = place()
    s = y * 2 + c
    to, source, differs = out_route()
    greet((differs, to))
    fp = SeqScatter(copies, local, P, p_own, p_pair, p_last)
    fq = SeqScatter(copies, local, Q, q_own, q_pair, q_last)
    sd = Scatter(copies, local, GD, "x", d_own, d_land, d_last)
    su = Scatter(copies, local, GU, "z", u_own, u_land, u_last)
    sa = Scatter(copies, local, GQ, "x", a_own, a_land, a_last, (0, 64))
    sb = Scatter(copies, local, GQ, "z", b_own, b_land, b_last, (64, 64))
    so = Scatter(copies, local, GO, "x", o_own, o_land, o_last)
    sc = Scatter(copies, local, C, "z", c_own, c_land, c_last)
    vs = [
        copies.start(V1.at[moved(y, dy) * 2 + lax.rem(c + dc, 2)], v_land.at[k], shifted(y=dy, c=dc))
        for k, (dy, dc) in enumerate(SEQ_PEERS)
    ]
    fp.one()
    su.one()
    sd.one()
    fq.one()
    sa.one()
    sb.one()
    so.one()
    fp.two()
    fq.two()
    for cp in vs:
        cp.wait_recv()
    w = V1[s]
    for k in range(7):
        w = w + v_land[k]
    for i in range(4):
        for j in range(4):
            r = i * 4 + j
            C[i, j, 0:1, :] = w[r : r + 1]
            C[i, j, 1:2, :] = V2[r : r + 1, :]
    sc.one()
    su.two()
    sd.two()
    sa.two()
    sb.two()
    so.two()
    sc.two()

    def store(ref):
        def put(at, n, total):
            ref[pl.ds(at, n)] = total.astype(ref.dtype)

        return put

    su.three(store(gu_part))

    def back(part, out):
        out[s] = part[pl.ds(pl.multiple_of(s * 16, 16), 16)]
        made = []
        for dy, dc in SEQ_PEERS:
            peer = moved(y, dy) * 2 + lax.rem(c + dc, 2)
            made.append(
                copies.start(
                    part.at[pl.ds(pl.multiple_of(peer * 16, 16), 16)], out.at[s], shifted(y=dy, c=dc)
                )
            )
        return made

    backs = back(gu_part, gu)
    sd.three(store(gd))
    fp.three(store(sp))
    fq.three(store(sq))
    sa.three(store(gq_part))
    sb.three(lambda at, n, total: store(gq_part)(at + 64, n, total))
    backs += back(gq_part, gq)
    so.three(store(go_part))
    out_copy = copies.make(go_part, go, source)

    @pl.when(differs)
    def _():
        out_copy.start()

    @pl.when(jnp.logical_not(differs))
    def _():
        go[...] = go_part[...]

    sc.three(store(sv))

    @pl.when(differs)
    def _():
        out_copy.wait()

    for cp in backs:
        cp.wait_recv()
    copies.drain()


def scatter(P, Q, GD, GU, GQ, GO, V1, V2):
    any_ = pl.BlockSpec(memory_space=pl.ANY)
    vm = pl.BlockSpec(memory_space=pltpu.VMEM)
    n_d, n_u, n_q, n_o = GD.shape[3], GU.shape[3], GQ.shape[3], GO.shape[3]
    S = pltpu.VMEM

    def set_of(rows, cols, kind=BF16):
        return [S((4, rows, cols), kind), S((3, 4, rows, cols), kind), S((3, rows, cols), kind)]

    seq = [S((4, 128, 2048), BF16), S((4, 128, 2048), BF16), S((3, 128, 2048), BF16)]
    return pl.pallas_call(
        scatter_kernel,
        out_shape=[
            jax.ShapeDtypeStruct((128, 2048), F32), jax.ShapeDtypeStruct((128, 2048), F32),
            jax.ShapeDtypeStruct((64, n_d), F32), jax.ShapeDtypeStruct((8, 16, n_u), BF16),
            jax.ShapeDtypeStruct((8, 16, n_q), BF16), jax.ShapeDtypeStruct((16, n_o), BF16),
            jax.ShapeDtypeStruct((8, 128), F32),
        ],
        in_specs=[any_] * 6 + [vm] * 2,
        out_specs=[vm] * 7,
        scratch_shapes=seq + seq + set_of(64, n_d) + set_of(128, n_u) + set_of(64, n_q) + set_of(64, n_q)
        + set_of(16, n_o) + [S((7, 16, 128), F32), S((4, 4, 8, 128), F32)] + set_of(8, 128, F32)
        + [S((128, n_u), BF16), S((128, n_q), BF16), S((16, n_o), BF16),
           pltpu.SemaphoreType.DMA((80,)), pltpu.SemaphoreType.DMA((80,)), pltpu.SemaphoreType.DMA((12,))],
        compiler_params=pltpu.CompilerParams(collective_id=2, has_side_effects=True, vmem_limit_bytes=60 * 2**20),
    )(P, Q, GD, GU, GQ, GO, V1, V2)


def tables(positions):
    half_rot = ROT // 2
    exponent = jnp.arange(half_rot).astype(F32) / half_rot
    frequency = jnp.power(10000.0, -exponent)
    angles = positions.astype(F32)[..., None] * frequency
    return (jnp.cos(angles)[..., None, :], jnp.sin(angles)[..., None, :])


def rotate(tensor, cos_tab, sine_tab):
    half_rot = ROT // 2
    first_half = tensor[..., :half_rot]
    second_half = tensor[..., half_rot:ROT]
    return jnp.concatenate(
        [
            first_half * cos_tab - second_half * sine_tab,
            second_half * cos_tab + first_half * sine_tab,
            tensor[..., ROT:],
        ],
        -1,
    )


def over_rows(left, right):
    return lax.dot_general(
        left, right, (((0,), (0,)), ((), ())), preferred_element_type=F32
    )


def against(left, right):
    return lax.dot_general(
        left, right, (((1,), (1,)), ((), ())), preferred_element_type=F32
    )


def plain(left, right):
    return jnp.dot(left, right, preferred_element_type=F32)


def norm_stats(rows):
    average = jnp.mean(rows, -1, keepdims=True)
    centred = rows - average
    inverse = lax.rsqrt(jnp.mean(centred * centred, -1, keepdims=True) + EPS)
    return centred * inverse, inverse


def shards(
    inputs,
    positions,
    w_qkv,
    b_qkv,
    w_out,
    b_out,
    w_up,
    b_up,
    w_down,
    b_down,
    gain_attn,
    shift_attn,
    gain_mlp,
    shift_mlp,
    grad_out,
):
    _, block_len, width = inputs.shape
    groups = lax.axis_size("batch")
    parts = lax.axis_size("seq")
    me = lax.axis_index("seq")
    b_me = lax.axis_index("batch")
    heads = H // parts
    length = block_len * parts
    scaling = HD ** (-0.5)
    x_local = inputs[0]
    g_local = grad_out[0]
    unit = b_up.shape[0]
    cut = b_qkv.shape[0]
    rows16 = b_out.shape[0]

    spot = positions[0]
    small = jnp.concatenate(
        [b_out, b_down, gain_attn, shift_attn, gain_mlp, shift_mlp, b_qkv, b_up]
        + [(spot // 32).astype(BF16), (spot % 32).astype(BF16)]
    )
    filled = small.shape[0]
    small = jnp.pad(small, (0, 2048 - filled)).reshape(16, 128)
    up_cut = w_up.reshape(-1, groups, parts, unit).transpose(2, 0, 1, 3).reshape(parts, -1, groups * unit)
    qkv_cut = w_qkv.reshape(-1, 3, parts, heads * HD).transpose(2, 0, 1, 3).reshape(parts, -1, 3 * heads * HD)
    X, G, SM, UP, QK, DN, WO = gather(x_local, g_local, small, up_cut, qkv_cut, w_down, w_out)
    x_rows = X.reshape(length, width)
    g_rows = G.reshape(length, width)
    w_up_f = UP.reshape(width, -1)
    w_qkv_f = QK.reshape(width, -1)
    w_down_f = DN.reshape(-1, width)
    w_out_f = WO.reshape(-1, width)
    small = SM.reshape(groups, parts, 2048)[:, :, :filled].astype(F32)
    b_out_f, b_down_f, gain_a, shift_a, gain_m, shift_m = [
        small[:, :, i * rows16 : (i + 1) * rows16].reshape(-1) for i in range(6)
    ]
    at = 6 * rows16
    b_qkv_f = small[:, :, at : at + cut].reshape(3, parts, heads * HD)
    b_qkv_f = lax.dynamic_index_in_dim(b_qkv_f, me, 1, keepdims=False).reshape(-1)
    at += cut
    b_up_f = lax.dynamic_index_in_dim(small[:, :, at : at + unit], me, 1, keepdims=False).reshape(-1)
    at += unit
    digits = lax.dynamic_index_in_dim(small[:, :, at:], b_me, 0, keepdims=False)
    pos_rows = (32.0 * digits[:, :block_len] + digits[:, block_len:]).reshape(-1)

    normed, _ = norm_stats(x_rows.astype(F32))
    first_in = (normed * gain_a + shift_a).astype(BF16)
    second_in = (normed * gain_m + shift_m).astype(BF16)

    hidden = plain(second_in, w_up_f) + b_up_f
    active, gelu_pull = jax.vjp(functools.partial(jax.nn.gelu, approximate=False), hidden)
    active_low = active.astype(BF16)
    grad_active = against(g_rows, w_down_f)
    (grad_hidden,) = gelu_pull(grad_active)
    grad_b_up = jnp.sum(grad_hidden, 0)
    grad_hidden_low = grad_hidden.astype(BF16)
    grad_w_down = over_rows(active_low, g_rows).astype(BF16)
    grad_w_up = over_rows(second_in, grad_hidden_low).astype(BF16)
    fed_forward = plain(active_low, w_down_f)
    grad_second = against(grad_hidden_low, w_up_f)

    qkv = (plain(first_in, w_qkv_f) + b_qkv_f).reshape(length, 3, heads, HD)
    cos_tab, sine_tab = tables(pos_rows)
    queries = (rotate(qkv[:, 0], cos_tab, sine_tab) * scaling).astype(BF16)
    keys = rotate(qkv[:, 1], cos_tab, sine_tab).astype(BF16)
    values = qkv[:, 2].astype(BF16)
    token = jnp.arange(length)
    visible = token[:, None] >= token[None, :]
    scores = jnp.einsum("qhd,khd->hqk", queries, keys, preferred_element_type=F32)
    scores = jnp.where(visible, scores, -1e30)
    exponent = jnp.exp(scores - jnp.max(scores, -1, keepdims=True))
    probs = exponent / jnp.sum(exponent, -1, keepdims=True)
    probs_low = probs.astype(BF16)
    mixture = jnp.einsum("hqk,khd->qhd", probs_low, values, preferred_element_type=F32)
    mixture = mixture.reshape(length, -1).astype(BF16)
    grad_w_out = over_rows(mixture, g_rows).astype(BF16)
    attended = plain(mixture, w_out_f)
    grad_mixture = against(g_rows, w_out_f).astype(BF16).reshape(length, heads, HD)
    grad_probs = jnp.einsum("qhd,khd->hqk", grad_mixture, values, preferred_element_type=F32)
    row_delta = jnp.sum(probs * grad_probs, -1, keepdims=True)
    grad_scores = (probs * (grad_probs - row_delta)).astype(BF16)
    grad_query = (
        jnp.einsum("hqk,khd->qhd", grad_scores, keys, preferred_element_type=F32) * scaling
    )
    grad_key = jnp.einsum("hqk,qhd->khd", grad_scores, queries, preferred_element_type=F32)
    grad_value = jnp.einsum("hqk,qhd->khd", probs_low, grad_mixture, preferred_element_type=F32)
    grad_qkv = jnp.stack(
        [
            rotate(grad_query, cos_tab, -sine_tab),
            rotate(grad_key, cos_tab, -sine_tab),
            grad_value,
        ],
        1,
    ).reshape(length, -1)
    grad_b_qkv = jnp.sum(grad_qkv, 0)
    grad_qkv_low = grad_qkv.astype(BF16)
    grad_w_qkv = over_rows(first_in, grad_qkv_low).astype(BF16)
    grad_first = against(grad_qkv_low, w_qkv_f)

    summed = (attended + fed_forward).astype(BF16)
    back = (grad_first * gain_a + grad_second * gain_m).astype(BF16)
    g_f = g_local.astype(F32)
    spread_qkv = jnp.zeros((3, parts, heads * HD), F32)
    spread_qkv = lax.dynamic_update_index_in_dim(
        spread_qkv, grad_b_qkv.reshape(3, 1, -1), me, 1
    )
    packed = [
        jnp.sum(g_f, 0),
        jnp.sum(grad_first * normed, 0),
        jnp.sum(grad_first, 0),
        jnp.sum(grad_second * normed, 0),
        jnp.sum(grad_second, 0),
        spread_qkv,
    ]
    packed = jnp.concatenate([p.reshape(groups, parts, -1) for p in packed], 2)
    packed = jnp.swapaxes(packed, 0, 1)
    ups = jnp.pad(grad_b_up.reshape(groups, unit), ((0, 0), (0, 128 - unit)))
    grid = (4, groups // 4)
    pairs = (parts // 2, 2, block_len, width)
    summed, back, out_w_down, grad_w_up, grad_w_qkv, grad_w_out, sums = scatter(
        summed.reshape(pairs),
        back.reshape(pairs),
        grad_w_down.reshape(grid + w_down.shape),
        grad_w_up.reshape(grid + (-1, groups * unit)),
        grad_w_qkv.reshape(grid + (-1, 3 * heads * HD)),
        grad_w_out.reshape(grid + w_out.shape),
        packed,
        ups,
    )

    x_f = x_local.astype(F32)
    layer_out = (x_f + summed + (b_out_f + b_down_f)).astype(BF16)
    n_local, r_local = norm_stats(x_f)
    back = r_local * (
        back
        - jnp.mean(back, -1, keepdims=True)
        - n_local * jnp.mean(back * n_local, -1, keepdims=True)
    )
    grad_in = (g_f + back).astype(BF16)
    grad_w_up = grad_w_up.reshape(parts, -1, groups, unit).transpose(1, 2, 0, 3).reshape(w_up.shape)
    grad_w_qkv = grad_w_qkv.reshape(parts, -1, 3, heads * HD).transpose(1, 2, 0, 3).reshape(w_qkv.shape)
    pieces = [sums[0, i * rows16 : (i + 1) * rows16] for i in range(5)]
    return (
        layer_out[None],
        grad_in[None],
        grad_w_qkv.astype(F32),
        sums[0, 5 * rows16 :],
        grad_w_out.astype(F32),
        pieces[0],
        grad_w_up.astype(F32),
        sums[1, :unit],
        out_w_down,
        pieces[0],
        pieces[1],
        pieces[2],
        pieces[3],
        pieces[4],
    )


def solution(mesh):
    both = ("batch", "seq")
    rows = P("batch", "seq", None)
    matrix = P(both, None)
    vector = P(both)
    return jax.shard_map(
        shards,
        mesh=mesh,
        in_specs=(
            rows,
            P("batch", "seq"),
            matrix,
            vector,
            matrix,
            vector,
            matrix,
            vector,
            matrix,
            vector,
            vector,
            vector,
            vector,
            vector,
            rows,
        ),
        out_specs=(
            rows,
            rows,
            matrix,
            vector,
            matrix,
            vector,
            matrix,
            vector,
            matrix,
            vector,
            vector,
            vector,
            vector,
            vector,
        ),
        check_vma=False,
    )
```

time: 861 us -> 382 us (0.44)
  waiting for transfers between devices: 489 us -> 0 us
  Pallas kernels: 0 us -> 201 us
  blocking collectives: 141 us -> 0 us
  starting transfers between devices: 24.9 us -> 0 us
  matrix products: 126 us -> 108 us
  between operations: 15.7 us -> 1.48 us
    reduce_scatter x6 -> x0, waiting for transfers between devices: 356 us -> none  [the longest x1 78.9 us: shards(): lax.psum_scatter(grad_w_down, 'batch', scatter_dimension=0, tiled=True)]
    pallas_call x0 -> x2, Pallas kernels: none -> 201 us  [the longest x1 103 us: scatter(): pl.pallas_call(scatter_kernel, out_shape=[jax.ShapeDtypeStruct((128, 2048...]
    unnamed x2 -> x0, blocking collectives: 98.2 us -> none
    unnamed x14 -> x0, waiting for transfers between devices: 95.6 us -> none
    all_gather x6 -> x0, waiting for transfers between devices: 32.8 us -> none  [the longest x1 32.8 us: shards(): w_down_f = lax.all_gather(w_down, 'batch', axis=0, tiled=True)]
    all_to_all x2 -> x0, blocking collectives: 26 us -> none  [the longest x1 14.2 us: shards(): lax.all_to_all(w_up_t, 'seq', split_axis=2, concat_axis=0, tiled=True)]
    all_gather x1 -> x0, blocking collectives: 16.8 us -> none  [shards(): pos_rows = lax.all_gather(positions[0], 'seq', axis=0, tiled=True)]
    all_to_all x2 -> x0, starting transfers between devices: 13.2 us -> none  [the longest x1 6.62 us: shards(): lax.all_to_all(grad_w_qkv, 'seq', split_axis=0, concat_axis=3, tiled=True)]
  transfers between devices with their start and end apart: 17 -> 0, of which waited for: 10 -> 0; matrix products, arithmetic and copies ran while one was open for 17% -> 0% of each run, Pallas kernels for 0% -> 0%
where the time goes in v2:
time: 382 us; the launch traced here: 375 us
  Pallas kernels  201 us (53%)
  matrix products  108 us (28%)
  local copies, waits for them, and re-layouts  33.8 us (9%)
  other arithmetic  30.9 us (8%)
    pallas_call x1, Pallas kernels, scatter(): pl.pallas_call(scatter_kernel, out_shape=[jax.ShapeDtypeStruct((128, 2048...  103 us
    pallas_call x1, Pallas kernels, gather(): pl.pallas_call(gather_kernel, out_shape=[jax.ShapeDtypeStruct(*s) for s i...  97.9 us
    dot_general x4, matrix products, against(): lax.dot_general(left, right, (((1,), (1,)), ((), ())), preferred_element_...  42.5 us
    dot_general x4, matrix products, plain(): return jnp.dot(left, right, preferred_element_type=F32)  22.6 us
    dot_general x4, matrix products, over_rows(): lax.dot_general(left, right, (((0,), (0,)), ((), ())), preferred_element_...  19.8 us
    unnamed x84, local copies, waits for them, and re-layouts  8.44 us
    sub x1, matrix products, shards(): exponent = jnp.exp(scores - jnp.max(scores, -1, keepdims=True))  7.82 us

profile of v2, /device:TPU:1, one launch (start us, length us, event | category | flops | bytes accessed | tf_op | source)
XLA Modules:
  0.0 374.7 jit_solution(10943674837529598404)
XLA Ops:
  1.3 5.4 %concatenate.19 = bf16[464]{0:T(512)(128)(2,1)S(1)} concatenate(bf16[16]{0:T(256)(128)(2,1)} %param.20, bf16[16]{0:T(256)(128)(2,1)} %param.24, bf16[16]{0:T(256)(128)(2,1)} %param.25, bf16[16]{0:T(256)(128)(2,1)} %param.26, bf16[16]{0:T(256)(128)(2,1)} %param.27, bf16[16]{0:T(256)(128)(2,1)} %param.28, bf16[48]{0:T(256)(128)(2,1)} %param.18, bf16[64]{0:T(256)(128)(2,1)} %param.22, ...), dimensions={0} | concatenate | bytes 1856 | tf_op jit(solution)/shard_map/concatenate | solution.py:588
  7.3 1.5 reshape.369
  11.9 97.9 %shard_map.254 = (bf16[8,128,2048]{2,1,0:T(8,128)(2,1)}, bf16[8,128,2048]{2,1,0:T(8,128)(2,1)}, bf16[4,4,8,16,128]{4,3,2,1,0:T(8,128)(2,1)}, bf16[4,4,128,1024]{...) custom-call(bf16[128,2048]{1,0:T(8,128)(2,1)} %bitcast.159, ...), custom_call_target="tpu_custom_call" | custom-call | tf_op jit(solution)/shard_map/pallas_call | solution.py:263
  112.1 3.0 convert_reduce_fusion
  116.9 6.3 %add_convert_fusion.4 = (bf16[8,128,2048]{2,1,0:T(8,128)(2,1)}, bf16[8,128,2048]{2,1,0:T(8,128)(2,1)S(1)}) fusion(bf16[8,128,2048]{2,1,0:T(8,128)(2,1)} %get-tuple-element.28, f32[2048]{0:T(1024)S(1)} %add.142, f32[2048]{0:T(1024)S(1)} %mul.275, f32[8,128]{1,0:T(8,128)S(1)} %get-tuple-element.89, f32[8,128]{1,0:T(8,128)S(1)} %get-tuple-element.87, ...), kind=kLoop, calls=%fused_computation.12 | loop fusion | flops 18874368 | bytes 12623872 | tf_op jit(solution)/shard_map/convert_element_type | solution.py:617
  123.3 6.0 %fusion.63 = f32[1024,1024]{1,0:T(8,128)} fusion(bf16[1024,2048]{1,0:T(8,128)(2,1)S(1)} %bitcast.173, bf16[2048,1024]{1,0:T(8,128)(2,1)S(1)} %bitcast.199), kind=kOutput, calls=%fused_computation.140 | convolution fusion | flops 4294967296 | bytes 12582912 | tf_op jit(solution)/shard_map/dot_general | solution.py:546
  129.5 18.1 %fusion.59 = (f32[1024]{0:T(1024)S(1)}, bf16[1024,1024]{1,0:T(8,128)(2,1)}, f32[1024,1024]{1,0:T(8,128)S(1)}) fusion(f32[1024,1024]{1,0:T(8,128)} %fusion.63, f32[1024]{0:T(1024)S(1)} %add.156, bf16[1024,2048]{1,0:T(8,128)(2,1)} %bitcast.194, bf16[1024,2048]{1,0:T(8,128)(2,1)} %bitcast.200), kind=kOutput, calls=%fused_computation.137 | convolution fusion | flops 4372560896 | bytes 18882560 | tf_op jit(solution)/shard_map/dot_general | solution.py:540
  149.8 6.7 %fusion.64 = f32[1024,2048]{1,0:T(8,128)} fusion(bf16[1024,1024]{1,0:T(8,128)(2,1)S(1)} %multiply_convert_fusion.1, bf16[1024,2048]{1,0:T(8,128)(2,1)S(1)} %bitcast.201), kind=kOutput, calls=%fused_computation.141 | convolution fusion | flops 4294967296 | bytes 14680064 | tf_op jit(solution)/shard_map/dot_general | solution.py:546
  156.7 6.4 %convolution_add_fusion = f32[1024,768]{0,1:T(8,128)S(1)} fusion(bf16[1024,2048]{1,0:T(8,128)(2,1)} %bitcast.171, bf16[2048,768]{1,0:T(8,128)(2,1)} %bitcast.202, f32[768]{0:T(1024)S(1)} %add.146), kind=kOutput, calls=%fused_computation.49 | convolution fusion | flops 3222011904 | bytes 10488832 | tf_op jit(solution)/shard_map/dot_general | solution.py:546
  163.2 1.6 iota_compare_fusion
  168.1 1.6 subtract_convert_fusion
  171.3 7.8 %fusion.62 = (f32[2,1024]{1,0:T(2,128)S(1)}, f32[2,1024,1024]{1,2,0:T(8,128)}) fusion(pred[1024,1024]{0,1:T(8,128)(4,1)} %iota_compare_fusion, bf16[1024,2,128]{2,0,1:T(8,128)(2,1)S(1)} %fusion.37, bf16[1024,2,96]{2,0,1:T(8,128)(2,1)} %slice.203, bf16[1024,2,16]{2,0,1:T(8,128)(2,1)S(1)} %copy-done.14, bf16[1024,2,16]{2,0,1:T(8,128)(2,1)S(1)} %copy-done.12), kind=kOutput, calls=%fused_computation.139 | convolution fusion | flops 544736256 | bytes 10493952 | tf_op jit(solution)/shard_map/sub | solution.py:641
  179.1 4.6 %fusion.23 = bf16[2,128,1024]{2,1,0:T(8,128)(2,1)S(1)} fusion(f32[1024,3,2,128]{0,3,2,1:T(8,128)} %bitcast.181, f32[2,1024,1024]{1,2,0:T(8,128)} %get-tuple-element.93, f32[2,1024]{1,0:T(2,128)S(1)} %get-tuple-element.92), kind=kOutput, calls=%fused_computation.59 | convolution fusion | flops 541327360 | bytes 9445376 | tf_op jit(solution)/shard_map/hqk,khd->qhd/dot_general | solution.py:644
  184.0 1.5 slice-done.1
  185.7 3.4 add_convert_fusion.2
  191.1 2.3 fusion.19
  193.4 2.6 multiply_reduce_fusion.2
  196.0 2.7 multiply_convert_fusion
  198.8 2.2 fusion.22
  202.5 3.4 convolution_bitcast_fusion
  208.5 1.5 fusion.14
  210.1 2.6 copy.111
  212.7 9.2 %fusion.65 = f32[1024,2048]{1,0:T(8,128)} fusion(bf16[1024,768]{0,1:T(8,128)(2,1)} %bitcast.177, bf16[2048,768]{1,0:T(8,128)(2,1)} %bitcast.203), kind=kOutput, calls=%fused_computation.142 | convolution fusion | flops 3221225472 | bytes 13107200 | tf_op jit(solution)/shard_map/dot_general | solution.py:540
  221.9 14.0 %fusion.56 = (f32[2048]{0:T(1024)S(1)}, f32[2048]{0:T(1024)S(1)}, bf16[1024,2048]{1,0:T(8,128)(2,1)}, f32[2048]{0:T(1024)S(1)}, f32[2048]{0:T(1024)S(1)}, /*index=5*/bf16[1024,2048]{1,0:T(8,128)(2,1)}) fusion(f32[1024]{0:T(1024)S(1)} %get-tuple-element.88, f32[1024]{0:T(1024)S(1)} %get-tuple-element.86, bf16[8,128,2048]{2,1,0:T(8,128)(2,1)S(1)} %copy-done.1, ...), kind=kOutput, calls=%fused_computation.134 | convolution fusion | flops 4328513536 | bytes 27328512 | tf_op jit(solution)/shard_map/dot_general | solution.py:540
  235.9 6.3 %convolution_convert_fusion.1 = bf16[1024,2048]{1,0:T(8,128)(2,1)} fusion(bf16[1024,1024]{1,0:T(8,128)(2,1)S(1)} %copy-done.11, bf16[1024,2048]{1,0:T(8,128)(2,1)S(1)} %bitcast.196), kind=kOutput, calls=%fused_computation.39 | convolution fusion | flops 4297064448 | bytes 10485760 | tf_op jit(solution)/shard_map/dot_general | solution.py:534
  242.2 6.3 %convolution_convert_fusion = bf16[2048,1024]{1,0:T(8,128)(2,1)} fusion(bf16[1024,2048]{1,0:T(8,128)(2,1)S(1)} %copy-done.33, bf16[1024,1024]{1,0:T(8,128)(2,1)S(1)} %copy-done.34), kind=kOutput, calls=%fused_computation.38 | convolution fusion | flops 4297064448 | bytes 10485760 | tf_op jit(solution)/shard_map/dot_general | solution.py:534
  248.5 4.9 %convolution_convert_fusion.2 = bf16[2048,768]{1,0:T(8,128)(2,1)} fusion(bf16[1024,2048]{1,0:T(8,128)(2,1)S(1)} %bitcast.172, bf16[1024,768]{0,1:T(8,128)(2,1)S(1)} %bitcast.178), kind=kOutput, calls=%fused_computation.40 | convolution fusion | flops 3222798336 | bytes 8912896 | tf_op jit(solution)/shard_map/dot_general | solution.py:534
  253.4 2.3 convolution_convert_fusion.3
  256.3 1.4 fusion.13
  259.3 102.8 %shard_map.255 = (f32[128,2048]{1,0:T(8,128)}, f32[128,2048]{1,0:T(8,128)}, f32[64,2048]{1,0:T(8,128)}, bf16[8,16,1024]{2,1,0:T(8,128)(2,1)}, bf16[8,16,768]{2,1...) custom-call(bf16[4,2,128,2048]{3,2,1,0:T(8,128)(2,1)} %bitcast.156, bf16[4,2,128,2048]{3,2,1,0:T(8,128)(2,1)} %bitcast.167, ...), custom_call_target="tpu_custom_call" | custom-call | tf_op jit(solution)/shard_map/pallas_call | solution.py:493
  362.6 1.6 fusion.58
  364.3 3.1 fusion.43
  (160 shorter events, 32.2 us)
Async XLA Ops:
  112.1 3.5 copy-start
  116.9 6.4 %copy-start.31 = (bf16[4,4,128,1024]{3,2,1,0:T(8,128)(2,1)S(1)}, bf16[4,4,128,1024]{3,2,1,0:T(8,128)(2,1)}, u32[]{:S(2)}) copy-start(bf16[4,4,128,1024]{3,2,1,0:T(8,128)(2,1)} %get-tuple-element.32) | copy-start | bytes 12582916
  129.5 18.1 %copy-start.5 = (f32[1024,1024]{1,0:T(8,128)S(1)}, f32[1024,1024]{1,0:T(8,128)}, u32[]{:S(2)}) copy-start(f32[1024,1024]{1,0:T(8,128)} %fusion.63) | copy-start | bytes 12582916
  149.8 6.8 %copy-start.10 = (bf16[1024,1024]{1,0:T(8,128)(2,1)}, bf16[1024,1024]{1,0:T(8,128)(2,1)S(1)}, u32[]{:S(2)}) copy-start(bf16[1024,1024]{1,0:T(8,128)(2,1)S(1)} %multiply_convert_fusion.1) | copy-start | bytes 6291460
  179.1 4.9 %slice-start = ((s8[8388608]{0:T(1024)(128)(4,1)}), s8[4194304]{0:T(1024)(128)(4,1)S(1)}, s32[]{:S(2)}) async-start(s8[8388608]{0:T(1024)(128)(4,1)} %bitcast.162), calls=%async_computation | async-start | bytes 8388608
  179.1 6.4 %slice-start.1 = ((s8[8388608]{0:T(1024)(128)(4,1)}), s8[4194304]{0:T(1024)(128)(4,1)S(1)}, s32[]{:S(2)}) async-start(s8[8388608]{0:T(1024)(128)(4,1)} %bitcast.162), calls=%async_computation.1 | async-start | bytes 8388608
  179.1 6.6 %copy-start.19 = (bf16[4,4,16,2048]{3,2,1,0:T(8,128)(2,1)S(1)}, bf16[4,4,16,2048]{3,2,1,0:T(8,128)(2,1)}, u32[]{:S(2)}) copy-start(bf16[4,4,16,2048]{3,2,1,0:T(8,128)(2,1)} %get-tuple-element.31) | copy-start | bytes 3145732
  183.7 5.4 %copy-start.20 = (bf16[2,128,1024]{2,1,0:T(8,128)(2,1)}, bf16[2,128,1024]{2,1,0:T(8,128)(2,1)S(1)}, u32[]{:S(2)}) copy-start(bf16[2,128,1024]{2,1,0:T(8,128)(2,1)S(1)} %fusion.23) | copy-start | bytes 1572868
  183.7 6.7 %slice-start.2 = ((s8[8388608]{0:T(1024)(128)(4,1)}), s8[4194304]{0:T(1024)(128)(4,1)S(1)}, s32[]{:S(2)}) async-start(s8[8388608]{0:T(1024)(128)(4,1)} %bitcast.164), calls=%async_computation.2 | async-start | bytes 8388608
  185.7 3.5 copy-start.29
  185.7 5.4 %slice-start.3 = ((s8[8388608]{0:T(1024)(128)(4,1)}), s8[4194304]{0:T(1024)(128)(4,1)S(1)}, s32[]{:S(2)}) async-start(s8[8388608]{0:T(1024)(128)(4,1)} %bitcast.164), calls=%async_computation.3 | async-start | bytes 8388608
  196.0 2.7 copy-start.13
  196.0 2.7 copy-start.15
  196.0 2.7 copy-start.16
  198.7 3.5 copy-start.2
  212.7 9.2 %copy-start.1 = (bf16[8,128,2048]{2,1,0:T(8,128)(2,1)S(1)}, bf16[8,128,2048]{2,1,0:T(8,128)(2,1)}, u32[]{:S(2)}) copy-start(bf16[8,128,2048]{2,1,0:T(8,128)(2,1)} %get-tuple-element.28) | copy-start | bytes 12582916
  212.7 9.2 %copy-start.34 = (bf16[1024,1024]{1,0:T(8,128)(2,1)S(1)}, bf16[1024,1024]{1,0:T(8,128)(2,1)}, u32[]{:S(2)}) copy-start(bf16[1024,1024]{1,0:T(8,128)(2,1)} %get-tuple-element.49) | copy-start | bytes 6291460
  221.9 14.0 %copy-start.11 = (bf16[1024,1024]{1,0:T(8,128)(2,1)S(1)}, bf16[1024,1024]{1,0:T(8,128)(2,1)}, u32[]{:S(2)}) copy-start(bf16[1024,1024]{1,0:T(8,128)(2,1)} %copy-done.10) | copy-start | bytes 6291460
  221.9 14.0 %copy-start.30 = (bf16[8,128,2048]{2,1,0:T(8,128)(2,1)S(1)}, bf16[8,128,2048]{2,1,0:T(8,128)(2,1)}, u32[]{:S(2)}) copy-start(bf16[8,128,2048]{2,1,0:T(8,128)(2,1)} %get-tuple-element.34) | copy-start | bytes 12582916
  235.9 6.3 %copy-start.33 = (bf16[1024,2048]{1,0:T(8,128)(2,1)S(1)}, bf16[1024,2048]{1,0:T(8,128)(2,1)}, u32[]{:S(2)}) copy-start(bf16[1024,2048]{1,0:T(8,128)(2,1)} %get-tuple-element.54) | copy-start | bytes 12582916
  242.2 6.3 %copy-start.8 = (bf16[8,128,2048]{2,1,0:T(8,128)(2,1)S(1)}, bf16[8,128,2048]{2,1,0:T(8,128)(2,1)}, u32[]{:S(2)}) copy-start(bf16[8,128,2048]{2,1,0:T(8,128)(2,1)} %get-tuple-element.55) | copy-start | bytes 12582916
  242.2 6.3 %copy-start.17 = (bf16[1024,3,2,128]{0,3,2,1:T(8,128)(2,1)S(1)}, bf16[1024,3,2,128]{0,3,2,1:T(8,128)(2,1)}, u32[]{:S(2)}) copy-start(bf16[1024,3,2,128]{0,3,2,1:T(8,128)(2,1)} %copy.111) | copy-start | bytes 4718596
  248.5 4.9 %copy-start.21 = (bf16[2,128,1024]{2,1,0:T(8,128)(2,1)S(1)}, bf16[2,128,1024]{2,1,0:T(8,128)(2,1)}, u32[]{:S(2)}) copy-start(bf16[2,128,1024]{2,1,0:T(8,128)(2,1)} %copy-done.20) | copy-start | bytes 1572868
  253.4 2.3 copy-start.4
  259.3 102.8 %copy-start.3 = (bf16[1,128,2048]{2,1,0:T(8,128)(2,1)S(1)}, bf16[1,128,2048]{2,1,0:T(8,128)(2,1)}, u32[]{:S(2)}) copy-start(bf16[1,128,2048]{2,1,0:T(8,128)(2,1)} %param.15) | copy-start | bytes 1572868
  259.3 104.9 %copy-start.24 = (f32[16,8,16]{2,1,0:T(8,128)S(1)}, f32[16,8,16]{2,1,0:T(8,128)}, u32[]{:S(2)}) copy-start(f32[16,8,16]{2,1,0:T(8,128)} %get-tuple-element.73) | copy-start | bytes 24580
  362.1 5.3 %copy-start.25 = (bf16[8,16,768]{2,1,0:T(8,128)(2,1)S(1)}, bf16[8,16,768]{2,1,0:T(8,128)(2,1)}, u32[]{:S(2)}) copy-start(bf16[8,16,768]{2,1,0:T(8,128)(2,1)} %get-tuple-element.37) | copy-start | bytes 589828
  362.6 6.2 %copy-start.27 = (f32[8,128]{1,0:T(8,128)S(1)}, f32[8,128]{1,0:T(8,128)}, u32[]{:S(2)}) copy-start(f32[8,128]{1,0:T(8,128)} %get-tuple-element.38) | copy-start | bytes 12292
  362.6 6.7 %copy-start.26 = (bf16[16,2048]{1,0:T(8,128)(2,1)S(1)}, bf16[16,2048]{1,0:T(8,128)(2,1)}, u32[]{:S(2)}) copy-start(bf16[16,2048]{1,0:T(8,128)(2,1)} %get-tuple-element.39) | copy-start | bytes 196612
  362.6 8.0 %copy-start.23 = (bf16[8,16,1024]{2,1,0:T(8,128)(2,1)S(1)}, bf16[8,16,1024]{2,1,0:T(8,128)(2,1)}, u32[]{:S(2)}) copy-start(bf16[8,16,1024]{2,1,0:T(8,128)(2,1)} %get-tuple-element.40) | copy-start | bytes 786436
  367.4 6.3 %copy-start.22 = (f32[64,2048]{1,0:T(8,128)S(1)}, f32[64,2048]{1,0:T(8,128)}, u32[]{:S(2)}) copy-start(f32[64,2048]{1,0:T(8,128)} %get-tuple-element.151) | copy-start | bytes 1572868
  370.6 3.9 %copy-start.28 = (f32[16]{0:T(128)}, f32[16]{0:T(128)S(1)}, u32[]{:S(2)}) copy-start(f32[16]{0:T(128)S(1)} %get-tuple-element.148) | copy-start | bytes 196
  (7 other events, 11.7 us)

commit v3 on v2

v3 whole, which is shorter than its diff:
```python
import jax
import jax.numpy as jnp
from jax import lax
from jax.experimental import pallas as pl
from jax.experimental.pallas import tpu as pltpu
from jax.sharding import PartitionSpec as P

H = 16
HD = 128
ROT = 32
EPS = 1e-05
C = 2048
SCALE = HD ** (-0.5)
F32 = jnp.float32
BF16 = jnp.bfloat16
MESH = pl.DeviceIdType.MESH
STEPS = (1, -1, 2)
SEQ_PEERS = [(dy, dc) for dc in (1, 0) for dy in (0, 1, -1, 2) if (dy, dc) != (0, 0)]


def place():
    b = lax.axis_index("batch")
    s = lax.axis_index("seq")
    return b // 4, b % 4, s // 2, s % 2


def shifted(x=0, z=0, y=0, c=0):
    px, pz, py, pc = place()
    px = lax.rem(px + x + 4, 4)
    pz = lax.rem(pz + z + 4, 4)
    py = lax.rem(py + y + 4, 4)
    pc = lax.rem(pc + c, 2)
    return (px * 4 + pz, py * 2 + pc)


def moved(pos, step):
    return lax.rem(pos + step + 4, 4)


class Copies:
    def __init__(self, send, recv):
        self.send, self.recv, self.count, self.made = send, recv, 0, []

    def make(self, src, dst, device):
        k = self.count
        self.count += 1
        return pltpu.make_async_remote_copy(
            src_ref=src,
            dst_ref=dst,
            send_sem=self.send.at[k],
            recv_sem=self.recv.at[k],
            device_id=device,
            device_id_type=MESH,
        )

    def start(self, src, dst, device):
        copy = self.make(src, dst, device)
        copy.start()
        self.made.append(copy)
        return copy

    def drain(self):
        for copy in self.made:
            copy.wait_send()


class Locals:
    def __init__(self, sems):
        self.sems, self.count = sems, 0

    def start(self, src, dst):
        copy = pltpu.make_async_copy(src, dst, self.sems.at[self.count])
        self.count += 1
        copy.start()
        return copy


def greet(extra=None):
    barrier = pltpu.get_barrier_semaphore()
    peers = [dict(x=d) for d in STEPS] + [dict(z=d) for d in STEPS]
    peers += [dict(y=dy, c=dc) for dy, dc in SEQ_PEERS]
    for p in peers:
        pl.semaphore_signal(barrier, inc=1, device_id=shifted(**p), device_id_type=MESH)
    count = len(peers)
    if extra is not None:
        differs, source = extra

        @pl.when(differs)
        def _():
            pl.semaphore_signal(barrier, inc=1, device_id=source, device_id_type=MESH)

        count = jnp.where(differs, count + 1, count)
    pl.semaphore_wait(barrier, count)


def group(buf, first, at, half=None, rows=None):
    span = pl.ds(0, 4) if half is None else pl.ds(2 * half, 2)
    index = (span, at) if first == "x" else (at, span)
    if rows is not None:
        index += (pl.ds(*rows),)
    return buf.at[index]


class Gather:
    def __init__(self, copies, buf, first, rows=None):
        self.copies, self.buf, self.first, self.rows = copies, buf, first, rows
        self.other = "z" if first == "x" else "x"
        x, z, _, _ = place()
        self.at = z if first == "x" else x
        self.own = buf.at[x, z] if rows is None else buf.at[x, z, pl.ds(*rows)]

    def part(self, step, half=None):
        return group(self.buf, self.first, moved(self.at, step), half, self.rows)

    def one(self, src=None):
        src = self.own if src is None else src
        self.sent = [self.copies.start(src, self.own, shifted(**{self.first: d})) for d in STEPS]

    def two(self):
        for c in self.sent:
            c.wait_recv()
        mine = self.part(0)
        self.sent = [self.copies.start(mine, mine, shifted(**{self.other: d})) for d in (1, -1)]

    def three(self):
        sent = []
        for c, d, half in zip(self.sent, (1, -1), (0, 1)):
            c.wait_recv()
            passed = self.part(-d, half)
            sent.append(self.copies.start(passed, passed, shifted(**{self.other: d})))
        self.sent = sent

    def done(self):
        for c in self.sent:
            c.wait_recv()


def out_route(groups=16, parts=8, heads=2):
    b = lax.axis_index("batch")
    s = lax.axis_index("seq")
    to = ((b % heads) * parts + s, b // heads)
    source = (s * heads + b // parts, b % parts)
    differs = jnp.logical_or(to[0] != b, to[1] != s)
    return to, source, differs


def dot(a, b, ca=1, cb=0):
    return lax.dot_general(a, b, (((ca,), (cb,)), ((), ())), preferred_element_type=F32)


def turn(v, tc, ta, tb):
    return v * tc + pltpu.roll(v, 112, 1) * ta + pltpu.roll(v, 16, 1) * tb


def project(i, F1, QK, bq, TC, TA, TB, Q, K, V):
    r = pl.ds(pl.multiple_of(i * 256, 256), 256)
    w = QK[...].reshape(C, 768)
    full = dot(F1[r], w) + bq[...]
    tc, ta, tb = TC[r], TA[r], TB[r]
    for h in range(2):
        at = h * 128
        q = turn(full[:, at : at + 128], tc, ta, tb) * SCALE
        Q[r, at : at + 128] = q.astype(BF16)
        k = turn(full[:, 256 + at : 384 + at], tc, ta, tb)
        K[r, at : at + 128] = k.astype(BF16)
        V[r, at : at + 128] = full[:, 512 + at : 640 + at].astype(BF16)


def head_pass(h, Q, K, V, GM, MIX, GL, DK, DV, TC, TA, TB, gb):
    cols = pl.ds(h * 128, 128)
    gq_cols, gk_cols, gv_cols = (pl.ds(o + h * 128, 128) for o in (0, 256, 512))
    for i in reversed(range(4)):
        r = pl.ds(i * 256, 256)
        n = (i + 1) * 256
        q, g = Q[r, cols], GM[r, cols]
        k, v = K[0:n, cols], V[0:n, cols]
        s = dot(q, k, 1, 1)
        row = lax.broadcasted_iota(jnp.int32, (256, n), 0) + i * 256
        col = lax.broadcasted_iota(jnp.int32, (256, n), 1)
        s = jnp.where(row >= col, s, -1e30)
        p = jnp.exp(s - jnp.max(s, -1, keepdims=True))
        p = p * (1.0 / jnp.sum(p, -1, keepdims=True))
        p_low = p.astype(BF16)
        MIX[r, cols] = dot(p_low, v).astype(BF16)
        gp = dot(g, v, 1, 1)
        gs = (p * (gp - jnp.sum(p * gp, -1, keepdims=True))).astype(BF16)
        dk, dv = dot(gs, q, 0, 0), dot(p_low, g, 0, 0)
        if i == 3:
            DK[...], DV[...] = dk, dv
        else:
            DK[0:n, :] += dk
            DV[0:n, :] += dv
        gq = dot(gs, k) * SCALE
        gq = turn(gq, TC[r], -TA[r], -TB[r])
        GL[r, gq_cols] = gq.astype(BF16)
        part = jnp.sum(gq, 0, keepdims=True)
        total = part if i == 3 else total + part
    gb[:, gq_cols] = total
    gk = turn(DK[...], TC[...], -TA[...], -TB[...])
    GL[:, gk_cols] = gk.astype(BF16)
    gb[:, gk_cols] = jnp.sum(gk, 0, keepdims=True)
    gv = DV[...]
    GL[:, gv_cols] = gv.astype(BF16)
    gb[:, gv_cols] = jnp.sum(gv, 0, keepdims=True)


def front_kernel(x_ref, g_ref, small_ref, rot_ref, up_ref, qkv_ref, down_ref, out_ref,
                 go, f2o, no, upo, dno, acto, ghlo, gqo, goo, po, so, vec, gsum, gbu, gbq,
                 X, G, SA, RA, SM, UP, QK, DN, WO, F1, F2, NB, ACT, GHL, GQ, GO,
                 Q, K, V, GM, MIX, GL, DK, DV, TC, TA, TB, BQ,
                 send, recv, loc):
    copies, local = Copies(send, recv), Locals(loc)
    x, z, y, c = place()
    s = y * 2 + c
    to, source, differs = out_route()
    greet((differs, source))

    def block(k):
        return pl.ds(pl.multiple_of(k * 128, 128), 128)

    SA[s] = small_ref[...]
    RA[s] = rot_ref[...]
    sm = [copies.start(small_ref, SA.at[s], shifted(y=dy, c=dc)) for dy, dc in SEQ_PEERS]

    def across(src, dst):
        dst[...] = src[s]
        return [
            copies.start(src.at[moved(y, dy) * 2 + lax.rem(c + dc, 2)], dst, shifted(y=dy, c=dc))
            for dy, dc in SEQ_PEERS
        ]

    rows16 = pl.ds(pl.multiple_of(s * 16, 16), 16)
    qk = across(qkv_ref, QK.at[x, z, rows16])
    out_copy = copies.make(out_ref, WO.at[to[0] // 4, to[0] % 4], to)

    @pl.when(differs)
    def _():
        out_copy.start()

    @pl.when(jnp.logical_not(differs))
    def _():
        WO[x, z] = out_ref[...]

    def seq_one(src, dst):
        own = dst.at[block(s)]
        own[...] = src[...]
        return [copies.start(src, own, shifted(y=d)) for d in (1, -1)] + [
            copies.start(src, own, shifted(c=1))
        ]

    def seq_two(sent, dst):
        more = []
        for cp, d in zip(sent[:2], (1, -1)):
            cp.wait_recv()
            got = dst.at[block(moved(y, -d) * 2 + c)]
            more.append(copies.start(got, got, shifted(c=1)))
        up_way = c == 0
        got = dst.at[block(jnp.where(up_way, moved(y, -1), moved(y, 1)) * 2 + c)]
        py = jnp.where(up_way, moved(y, 1), moved(y, -1))
        fwd = copies.start(got, got, (lax.axis_index("batch"), py * 2 + c))
        sent[2].wait_recv()
        return more, fwd

    def seq_three(more, fwd, dst):
        fwd.wait_recv()
        got = dst.at[block(moved(y, 2) * 2 + c)]
        return more + [copies.start(got, got, shifted(c=1))]

    xs = seq_one(x_ref, X)
    ra = [copies.start(rot_ref, RA.at[s], shifted(y=dy, c=dc)) for dy, dc in SEQ_PEERS]
    up = across(up_ref, UP.at[x, z, rows16])
    gs = seq_one(g_ref, G)
    DN[x, z] = down_ref[...]

    for cp in sm:
        cp.wait_recv()
    total = SA[0].astype(F32)
    for k in range(1, 8):
        total += SA[k].astype(F32)
    row = lax.broadcasted_iota(jnp.int32, (16, 128), 0)
    SM[x, z] = jnp.where(row == 9, SA[s].astype(F32), total).astype(BF16)
    small = Gather(copies, SM, "z")
    small.one()

    for cp in qk:
        cp.wait_recv()
    qa = Gather(copies, QK, "x", (0, 64))
    qb = Gather(copies, QK, "z", (64, 64))
    qa.one()
    qb.one()

    @pl.when(differs)
    def _():
        out_copy.wait_recv()
        out_copy.wait_send()

    wo = Gather(copies, WO, "x")
    wo.one()
    small.two()
    qa.two()
    qb.two()
    wo.two()
    down = Gather(copies, DN, "x")
    down.one(down_ref)
    for cp in up:
        cp.wait_recv()
    upg = Gather(copies, UP, "z")
    upg.one()
    small.three()
    xs2, xf = seq_two(xs, X)
    qa.three()
    qb.three()
    wo.three()
    total = jnp.zeros((1, C), F32)
    for k in range(8):
        total += jnp.sum(g_ref[16 * k : 16 * (k + 1)].astype(F32), 0, keepdims=True)
    gsum[...] = total
    small.done()
    for i in range(4):
        for j in range(4):
            b = i * 4 + j
            tile = SM[i, j].astype(F32)
            vec[0:6, b * 128 : (b + 1) * 128] = tile[0:6]
            for k in range(3):
                BQ[3 * b + k : 3 * b + k + 1, :] = tile[6 + k : 7 + k]
            if b % 2 == 0:
                kept = tile[9:10]
            else:
                vec[6:7, b // 2 * 128 : (b // 2 + 1) * 128] = kept + tile[9:10]

    def norm(k):
        def step(t, _):
            r = pl.ds(pl.multiple_of(k * 128 + t * 16, 16), 16)
            v = X[r].astype(F32)
            v = v - jnp.mean(v, -1, keepdims=True)
            n = v * lax.rsqrt(jnp.mean(v * v, -1, keepdims=True) + EPS)
            NB[r] = n.astype(BF16)
            F1[r] = (n * vec[2:3, :] + vec[3:4, :]).astype(BF16)
            F2[r] = (n * vec[4:5, :] + vec[5:6, :]).astype(BF16)
            return 0

        lax.fori_loop(0, 8, step, 0)

    norm(s)
    norm(y * 2 + 1 - c)
    norm(moved(y, -1) * 2 + c)
    norm(moved(y, 1) * 2 + c)
    xs3 = seq_three(xs2, xf, X)
    gs2, gf = seq_two(gs, G)
    xs3[0].wait_recv()
    norm(moved(y, -1) * 2 + 1 - c)
    xs3[1].wait_recv()
    norm(moved(y, 1) * 2 + 1 - c)
    norm(moved(y, 2) * 2 + c)
    xs3[2].wait_recv()
    norm(moved(y, 2) * 2 + 1 - c)
    saves = [local.start(F2, f2o), local.start(NB, no)]
    down.two()
    upg.two()

    for cp in ra:
        cp.wait_recv()
    lane = lax.broadcasted_iota(jnp.int32, (128, 128), 1)
    for k in range(8):
        r = pl.ds(k * 128, 128)
        tile = jnp.concatenate([RA[k], jnp.zeros((96, 128), F32)], 0).T
        TC[r] = jnp.where(lane < 16, tile, jnp.where(lane < 32, pltpu.roll(tile, 16, 1), 1.0))
        TA[r] = jnp.where(lane < 16, -pltpu.roll(tile, 112, 1), 0.0)
        TB[r] = jnp.where((lane >= 16) & (lane < 32), tile, 0.0)
    for gth in (qa, qb):
        gth.done()

    for part in range(3):
        at = pl.multiple_of(part * 16 + s * 2, 2)
        pair = BQ[pl.ds(at, 2), :]
        for k in range(2):
            gbq[:, part * 256 + k * 128 : part * 256 + (k + 1) * 128] = pair[k : k + 1]
    bias = gbq[...]
    vec[9:10, 0:768] = bias

    def first(i, _):
        project(i, F1, QK, vec.at[9:10, 0:768], TC, TA, TB, Q, K, V)
        return 0

    lax.fori_loop(0, 4, first, 0)
    gs3 = seq_three(gs2, gf, G)
    wo.done()
    for cp in gs3:
        cp.wait_recv()
    saves.append(local.start(G, go))

    def mixed(i, _):
        r = pl.ds(pl.multiple_of(i * 256, 256), 256)
        GM[r] = dot(G[r], WO[...].reshape(256, C), 1, 1).astype(BF16)
        return 0

    lax.fori_loop(0, 4, mixed, 0)
    for h in range(2):
        head_pass(h, Q, K, V, GM, MIX, GL, DK, DV, TC, TA, TB, gbq)
    down.three()
    upg.three()

    def grad_out(j, _):
        q = pl.ds(pl.multiple_of(j * 1024, 1024), 1024)
        GO[:, :, :, q] = dot(MIX[...], G[:, q], 0, 0).astype(BF16).reshape(4, 4, 16, 1024)
        return 0

    lax.fori_loop(0, 2, grad_out, 0)
    saves.append(local.start(GO, goo))

    def grad_qkv(i, _):
        r = pl.ds(pl.multiple_of(i * 512, 512), 512)
        GQ[i] = dot(F1[:, r], GL[...], 0, 0).astype(BF16).reshape(4, 128, 768)
        return 0

    lax.fori_loop(0, 4, grad_qkv, 0)
    saves.append(local.start(GQ, gqo))
    for cp in xs + xs2 + [xf, xs3[2]]:
        cp.wait_send()
    copies.made = [cp for cp in copies.made if all(cp is not m for m in xs + xs2 + [xf, xs3[2]])]

    def attend(t, _):
        i, j = t // 2, t % 2
        r = pl.ds(pl.multiple_of(i * 512, 512), 512)
        q = pl.ds(pl.multiple_of(j * 1024, 1024), 1024)
        X[r, q] = dot(MIX[r], WO[:, :, :, q].reshape(256, 1024)).astype(BF16)
        return 0

    lax.fori_loop(0, 4, attend, 0)
    saves.append(local.start(X, po))
    vec[10:12, :] = jnp.zeros((2, C), F32)

    def grad_first(t, _):
        i, j = t // 4, t % 4
        r = pl.ds(pl.multiple_of(i * 256, 256), 256)
        q = pl.ds(pl.multiple_of(j * 512, 512), 512)
        u = dot(GL[r], QK[j].reshape(512, 768), 1, 1)
        vec[10:11, q] += jnp.sum(u * NB[r, q].astype(F32), 0, keepdims=True)
        vec[11:12, q] += jnp.sum(u, 0, keepdims=True)
        F1[r, q] = (u * vec[2:3, q]).astype(BF16)
        return 0

    lax.fori_loop(0, 16, grad_first, 0)
    saves.append(local.start(F1, so))

    gbu[...] = jnp.zeros_like(gbu)
    upg.done()
    saves.append(local.start(UP, upo))
    down.done()
    saves.append(local.start(DN, dno))

    def hidden(t, _):
        i, j = t // 2, t % 2
        r = pl.ds(pl.multiple_of(i * 256, 256), 256)
        q = pl.ds(pl.multiple_of(j * 512, 512), 512)
        h = dot(F2[r], UP[:, :, :, q].reshape(C, 512)) + vec[6:7, q]
        ga = dot(G[r], DN[pl.ds(2 * j, 2)].reshape(512, C), 1, 1)
        cdf = 0.5 + 0.5 * lax.erf(h * (0.5**0.5))
        ACT[r, q] = (h * cdf).astype(BF16)
        gh = ga * (cdf + h * (jnp.exp(h * h * -0.5) * 0.3989422804014327))
        gbu[:, q] += jnp.sum(gh, 0, keepdims=True)
        GHL[r, q] = gh.astype(BF16)
        return 0

    lax.fori_loop(0, 8, hidden, 0)
    saves += [local.start(ACT, acto), local.start(GHL, ghlo)]
    for cp in saves:
        cp.wait()
    copies.drain()


def front(x, g, small, rot, up, qkv, down, out):
    vm = pl.BlockSpec(memory_space=pltpu.VMEM)
    any_ = pl.BlockSpec(memory_space=pl.ANY)
    full = (1024, C)
    n_up, n_qkv = up.shape[-1], qkv.shape[-1]
    up_all, qk_all = (4, 4, 128, n_up), (4, 4, 128, n_qkv)
    dn_all, wo_all = (4, 4) + down.shape, (4, 4) + out.shape
    unit = (1024, n_up)
    held = [full, full, full, up_all, dn_all, unit, unit, qk_all, wo_all, full, full]
    S = pltpu.VMEM
    two = (1024, n_qkv // 3)
    scratch = [
        (full, BF16), (full, BF16), ((8, 16, 128), BF16), ((8, 32, 128), F32), ((4, 4, 16, 128), BF16),
        (up_all, BF16), (qk_all, BF16), (dn_all, BF16), (wo_all, BF16),
        (full, BF16), (full, BF16), (full, BF16), (unit, BF16), (unit, BF16), (qk_all, BF16), (wo_all, BF16),
        (two, BF16), (two, BF16), (two, BF16), (two, BF16), (two, BF16), ((1024, n_qkv), BF16),
        ((1024, HD), F32), ((1024, HD), F32), ((1024, HD), F32), ((1024, HD), F32), ((1024, HD), F32),
        ((48, 128), F32),
    ]
    return pl.pallas_call(
        front_kernel,
        out_shape=[jax.ShapeDtypeStruct(h, BF16) for h in held]
        + [jax.ShapeDtypeStruct(h, F32) for h in ((16, C), (1, C), (1, n_up), (1, n_qkv))],
        in_specs=[vm] * 8,
        out_specs=[any_] * 11 + [vm] * 4,
        scratch_shapes=[S(*h) for h in scratch]
        + [pltpu.SemaphoreType.DMA((96,)), pltpu.SemaphoreType.DMA((96,)), pltpu.SemaphoreType.DMA((12,))],
        compiler_params=pltpu.CompilerParams(
            collective_id=1, has_side_effects=True, vmem_limit_bytes=63 * 2**20
        ),
    )(x, g, small, rot, up, qkv, down, out)


def add_rows(shape, into, parts):
    slabs, rows = shape
    step = min(rows, 16)

    def add(t, _):
        i = t // (rows // step)
        r = pl.ds(pl.multiple_of(t % (rows // step) * step, step), step)
        total = parts[0](i, r).astype(F32)
        for p in parts[1:]:
            total += p(i, r).astype(F32)
        into(i, r, total)
        return 0

    lax.fori_loop(0, slabs * (rows // step), add, 0)


class Scatter:
    def __init__(self, copies, buf, first, relay, land, last, rows=None):
        self.copies, self.buf, self.first, self.rows = copies, buf, first, rows
        self.relay, self.land, self.last = relay, land, last
        self.other = "z" if first == "x" else "x"
        x, z, _, _ = place()
        self.at, self.mine = (z, x) if first == "x" else (x, z)
        self.count = buf.shape[2] if rows is None else rows[1]
        self.base = 0 if rows is None else rows[0]

    def part(self, step, half=None):
        return group(self.buf, self.first, moved(self.at, step), half, self.rows)

    def slab(self, step, i, r):
        at = moved(self.at, step)
        r = pl.ds(self.base + r.start, r.size)
        return (i, at, r) if self.first == "x" else (at, i, r)

    def one(self):
        start, to = self.copies.start, self.other
        self.far = [
            start(self.part(2, k), self.relay.at[k], shifted(**{to: d})) for k, d in enumerate((1, -1))
        ]
        self.near = [
            start(self.part(d, 1 - k), self.land.at[k, pl.ds(2 - 2 * k, 2)], shifted(**{to: d}))
            for k, d in enumerate((1, -1))
        ]

    def mid(self):
        for k, d in enumerate((1, -1)):
            self.far[k].wait_recv()

            def put(i, r, total, k=k, d=d):
                self.buf[self.slab(d, i + 2 * k, r)] = total.astype(self.buf.dtype)

            add_rows(
                (2, self.count),
                put,
                [lambda i, r, k=k, d=d: self.buf[self.slab(d, i + 2 * k, r)],
                 lambda i, r, k=k: self.relay[k, i, r]],
            )
            self.near.append(
                self.copies.start(
                    self.part(d, k), self.land.at[k, pl.ds(2 * k, 2)], shifted(**{self.other: d})
                )
            )

    def two(self):
        for cp in self.near:
            cp.wait_recv()

        def put(i, r, total):
            self.buf[self.slab(0, i, r)] = total.astype(self.buf.dtype)

        add_rows(
            (4, self.count),
            put,
            [lambda i, r: self.buf[self.slab(0, i, r)],
             lambda i, r: self.land[0, i, r], lambda i, r: self.land[1, i, r]],
        )
        x, z, _, _ = place()
        self.sent = []
        for k, d in enumerate(STEPS):
            there = moved(self.mine, d)
            index = (there, self.at) if self.first == "x" else (self.at, there)
            if self.rows is not None:
                index += (pl.ds(*self.rows),)
            self.sent.append(
                self.copies.start(self.buf.at[index], self.last.at[k], shifted(**{self.first: d}))
            )

    def three(self, put):
        for cp in self.sent:
            cp.wait_recv()
        add_rows(
            (1, self.count),
            lambda i, r, total: put(r, total),
            [lambda i, r: self.buf[self.slab(0, self.mine, r)]]
            + [lambda i, r, k=k: self.last[k, r] for k in range(3)],
        )


class SeqScatter:
    def __init__(self, copies, buf, pair, relay, land):
        self.copies, self.buf, self.pair, self.relay, self.land = copies, buf, pair, relay, land
        _, _, self.y, self.c = place()

    def one(self):
        self.sent = self.copies.start(self.buf.at[:, 1 - self.c], self.pair, shifted(c=1))

    def two(self):
        self.sent.wait_recv()
        buf, c = self.buf, self.c

        def put(i, r, total):
            buf[i, c, r] = total.astype(BF16)

        add_rows((4, 128), put, [lambda i, r: buf[i, c, r], lambda i, r: self.pair[i, r]])
        start = self.copies.start
        far = moved(self.y, 2)
        halves = (pl.ds(0, 64), pl.ds(64, 64))
        self.far = [
            start(buf.at[far, c, halves[k]], self.relay.at[k], shifted(y=d)) for k, d in enumerate((1, -1))
        ]
        self.near = [
            start(buf.at[moved(self.y, d), c, halves[1 - k]], self.land.at[k, halves[1 - k]], shifted(y=d))
            for k, d in enumerate((1, -1))
        ]

    def mid(self):
        buf, c = self.buf, self.c
        for k, d in enumerate((1, -1)):
            self.far[k].wait_recv()
            to = moved(self.y, d)

            def rows(r, k=k):
                return pl.ds(64 * k + r.start, r.size)

            def put(i, r, total, rows=rows, to=to):
                buf[to, c, rows(r)] = total.astype(BF16)

            add_rows(
                (1, 64),
                put,
                [lambda i, r, rows=rows, to=to: buf[to, c, rows(r)],
                 lambda i, r, k=k: self.relay[k, r]],
            )
            self.near.append(
                self.copies.start(
                    buf.at[to, c, pl.ds(64 * k, 64)], self.land.at[k, pl.ds(64 * k, 64)], shifted(y=d)
                )
            )

    def three(self, put):
        for cp in self.near:
            cp.wait_recv()
        buf, y, c = self.buf, self.y, self.c
        add_rows(
            (1, 128),
            lambda i, r, total: put(r, total),
            [lambda i, r: buf[y, c, r], lambda i, r: self.land[0, r], lambda i, r: self.land[1, r]],
        )


def back_kernel(g_in, f2_in, n_in, up_in, dn_in, act_in, ghl_in, gq_in, go_in, p_in, s_in,
                vec, g_sum, g_bu, g_bq,
                sp, sq, gd, gu, gq, go, sv,
                A, B, NB, UP, DN, ACT, GHL, GQ, GO, GD, GU,
                p_pair, p_relay, p_land, q_pair, q_relay, q_land,
                d_relay, d_land, d_last, u_relay, u_land, u_last,
                a_relay, a_land, a_last, b_relay, b_land, b_last,
                o_relay, o_land, o_last, BQ, VT, v_land, CT, c_relay, c_land, c_last,
                sums, gu_part, gq_part, go_part,
                send, recv, loc):
    copies, local = Copies(send, recv), Locals(loc)
    x, z, y, c = place()
    s = y * 2 + c
    to, source, differs = out_route()
    loads = {}
    for name, src, dst in (
        ("gq", gq_in, GQ), ("go", go_in, GO), ("act", act_in, ACT), ("g", g_in, A),
        ("ghl", ghl_in, GHL), ("f2", f2_in, B), ("dn", dn_in, DN), ("up", up_in, UP), ("n", n_in, NB),
    ):
        loads[name] = local.start(src, dst)
    greet((differs, to))
    fp = SeqScatter(copies, A, p_pair, p_relay, p_land)
    fq = SeqScatter(copies, B, q_pair, q_relay, q_land)
    sd = Scatter(copies, GD, "x", d_relay, d_land, d_last)
    su = Scatter(copies, GU, "z", u_relay, u_land, u_last)
    sa = Scatter(copies, GQ, "x", a_relay, a_land, a_last, (0, 64))
    sb = Scatter(copies, GQ, "z", b_relay, b_land, b_last, (64, 64))
    so = Scatter(copies, GO, "x", o_relay, o_land, o_last)
    sc = Scatter(copies, CT, "z", c_relay, c_land, c_last)
    loads["gq"].wait()
    sa.one()
    sb.one()
    loads["go"].wait()
    so.one()
    loads["act"].wait()
    loads["g"].wait()

    def grad_down(t, _):
        i, j = t // 2, t % 2
        u = pl.ds(pl.multiple_of(i * 256, 256), 256)
        q = pl.ds(pl.multiple_of(j * 1024, 1024), 1024)
        right = A[:, :, :, q].reshape(1024, 1024)
        GD[i, :, :, q] = dot(ACT[:, u], right, 0, 0).astype(BF16).reshape(4, 64, 1024)
        return 0

    lax.fori_loop(0, 8, grad_down, 0)
    sd.one()
    loads["p"] = local.start(p_in, A)
    loads["ghl"].wait()
    loads["f2"].wait()

    def grad_up(t, _):
        i, j = t // 2, t % 2
        r = pl.ds(pl.multiple_of(i * 512, 512), 512)
        q = pl.ds(pl.multiple_of(j * 512, 512), 512)
        left = B[:, :, :, r].reshape(1024, 512)
        GU[i, :, :, q] = dot(left, GHL[:, q], 0, 0).astype(BF16).reshape(4, 128, 512)
        return 0

    lax.fori_loop(0, 8, grad_up, 0)
    su.one()
    loads["s"] = local.start(s_in, B)
    sa.mid()
    sb.mid()
    so.mid()
    loads["dn"].wait()
    loads["p"].wait()

    def feed(t, _):
        i, j = t // 4, t % 4
        r = pl.ds(pl.multiple_of(i * 512, 512), 512)
        q = pl.ds(pl.multiple_of(j * 512, 512), 512)
        two = pl.ds(2 * i, 2)
        total = dot(ACT[r], DN[:, :, :, q].reshape(1024, 512)) + A[two, :, :, q].reshape(512, 512).astype(F32)
        A[two, :, :, q] = total.astype(BF16).reshape(2, 2, 128, 512)
        return 0

    lax.fori_loop(0, 8, feed, 0)
    fp.one()
    loads["up"].wait()
    loads["n"].wait()
    loads["s"].wait()
    sums[...] = jnp.zeros_like(sums)

    def second(t, _):
        i, j = t // 4, t % 4
        r = pl.ds(pl.multiple_of(i * 256, 256), 256)
        q = pl.ds(pl.multiple_of(j * 512, 512), 512)
        u = dot(GHL[r], UP[j].reshape(512, 1024), 1, 1)
        sums[0:1, q] += jnp.sum(u * NB[r, q].astype(F32), 0, keepdims=True)
        sums[1:2, q] += jnp.sum(u, 0, keepdims=True)
        total = u * vec[4:5, q] + B[i, :, :, q].reshape(256, 512).astype(F32)
        B[i, :, :, q] = total.astype(BF16).reshape(2, 128, 512)
        return 0

    lax.fori_loop(0, 8, second, 0)
    fp.two()
    lax.fori_loop(8, 16, second, 0)
    fq.one()

    BQ[...] = jnp.zeros_like(BQ)
    for part in range(3):
        for k in range(2):
            row = part * 16 + s * 2 + k
            at = part * 256 + k * 128
            BQ[pl.ds(row, 1), :] = g_bq[:, at : at + 128]
    for b in range(16):
        at = b * 128
        VT[b, 0:1, :] = g_sum[:, at : at + 128]
        VT[b, 1:3, :] = vec[10:12, at : at + 128]
        VT[b, 3:5, :] = sums[0:2, at : at + 128]
        VT[b, 5:8, :] = BQ[3 * b : 3 * b + 3, :]
    vs = [
        copies.start(VT, v_land.at[k], shifted(y=dy, c=dc)) for k, (dy, dc) in enumerate(SEQ_PEERS)
    ]
    sa.two()
    sb.two()
    sd.mid()
    su.mid()
    fq.two()
    fp.mid()
    so.two()
    for cp in vs:
        cp.wait_recv()
    for b in range(16):
        total = VT[b]
        for k in range(7):
            total += v_land[k, b]
        CT[b // 4, b % 4, 0:8, :] = total
        CT[b // 4, b % 4, 8:9, :] = g_bu[:, b // 2 * 128 : b // 2 * 128 + 128]
        CT[b // 4, b % 4, 9:16, :] = jnp.zeros((7, 128), F32)
    sc.one()

    def store(ref, base=0):
        def put(r, total):
            ref[pl.ds(base + r.start, r.size)] = total.astype(ref.dtype)

        return put

    def spread(part, out):
        out[s] = part[pl.ds(pl.multiple_of(s * 16, 16), 16)]
        made = []
        for dy, dc in SEQ_PEERS:
            peer = moved(y, dy) * 2 + lax.rem(c + dc, 2)
            made.append(
                copies.start(
                    part.at[pl.ds(pl.multiple_of(peer * 16, 16), 16)], out.at[s], shifted(y=dy, c=dc)
                )
            )
        return made

    sa.three(store(gq_part))
    sb.three(store(gq_part, 64))
    backs = spread(gq_part, gq)
    so.three(store(go_part))
    out_copy = copies.make(go_part, go, source)

    @pl.when(differs)
    def _():
        out_copy.start()

    @pl.when(jnp.logical_not(differs))
    def _():
        go[...] = go_part[...]

    fq.mid()
    sc.mid()
    su.two()
    sd.two()
    fp.three(store(sp))
    sc.two()
    fq.three(store(sq))
    su.three(store(gu_part))
    backs += spread(gu_part, gu)
    sd.three(store(gd))
    sc.three(store(sv))

    @pl.when(differs)
    def _():
        out_copy.wait()

    for cp in backs:
        cp.wait_recv()
    copies.drain()


def back(g, f2, n, up, dn, act, ghl, gq, go, p, s, *small):
    any_ = pl.BlockSpec(memory_space=pl.ANY)
    vm = pl.BlockSpec(memory_space=pltpu.VMEM)
    n_d, n_u, n_q, n_o = dn.shape[3], up.shape[3], gq.shape[3], go.shape[3]
    S = pltpu.VMEM
    blocks = (4, 2, 128, C)

    def set_of(rows, cols, kind=BF16):
        return [S((2, 2, rows, cols), kind), S((2, 4, rows, cols), kind), S((3, rows, cols), kind)]

    seq = [S((4, 128, C), BF16), S((2, 64, C), BF16), S((2, 128, C), BF16)]
    held = [blocks, blocks, n.shape, up.shape, dn.shape, act.shape, ghl.shape, gq.shape, go.shape, dn.shape, up.shape]
    return pl.pallas_call(
        back_kernel,
        out_shape=[
            jax.ShapeDtypeStruct((128, C), F32), jax.ShapeDtypeStruct((128, C), F32),
            jax.ShapeDtypeStruct((64, n_d), F32), jax.ShapeDtypeStruct((8, 16, n_u), BF16),
            jax.ShapeDtypeStruct((8, 16, n_q), BF16), jax.ShapeDtypeStruct((16, n_o), BF16),
            jax.ShapeDtypeStruct((16, 128), F32),
        ],
        in_specs=[any_] * 11 + [vm] * 4,
        out_specs=[vm] * 7,
        scratch_shapes=[S(h, BF16) for h in held] + seq + seq
        + set_of(64, n_d) + set_of(128, n_u) + set_of(64, n_q) + set_of(64, n_q) + set_of(16, n_o)
        + [S((48, 128), F32), S((16, 8, 128), F32), S((7, 16, 8, 128), F32), S((4, 4, 16, 128), F32)] + set_of(16, 128, F32)
        + [S((8, C), F32), S((128, n_u), BF16), S((128, n_q), BF16), S((16, n_o), BF16),
           pltpu.SemaphoreType.DMA((96,)), pltpu.SemaphoreType.DMA((96,)), pltpu.SemaphoreType.DMA((12,))],
        compiler_params=pltpu.CompilerParams(
            collective_id=2, has_side_effects=True, vmem_limit_bytes=63 * 2**20
        ),
    )(g.reshape(blocks), f2.reshape(blocks), n, up, dn, act, ghl, gq, go, p.reshape(blocks), s.reshape(blocks), *small)


def tables(positions):
    half_rot = ROT // 2
    exponent = jnp.arange(half_rot).astype(F32) / half_rot
    frequency = jnp.power(10000.0, -exponent)
    angles = positions.astype(F32)[None] * frequency[:, None]
    return jnp.concatenate([jnp.cos(angles), jnp.sin(angles)])


def norm_stats(rows):
    average = jnp.mean(rows, -1, keepdims=True)
    centred = rows - average
    inverse = lax.rsqrt(jnp.mean(centred * centred, -1, keepdims=True) + EPS)
    return centred * inverse, inverse


def shards(
    inputs,
    positions,
    w_qkv,
    b_qkv,
    w_out,
    b_out,
    w_up,
    b_up,
    w_down,
    b_down,
    gain_attn,
    shift_attn,
    gain_mlp,
    shift_mlp,
    grad_out,
):
    _, block_len, width = inputs.shape
    groups = lax.axis_size("batch")
    parts = lax.axis_size("seq")
    me = lax.axis_index("seq")
    b_me = lax.axis_index("batch")
    heads = H // parts
    x_local = inputs[0]
    g_local = grad_out[0]
    unit = b_up.shape[0]
    cut = b_qkv.shape[0]
    rows16 = b_out.shape[0]

    lane = jnp.arange(128)
    vectors = jnp.stack([b_out, b_down, gain_attn, shift_attn, gain_mlp, shift_mlp])
    vectors = jnp.where(lane // rows16 == me, jnp.tile(vectors, (1, parts)), 0)
    three = jnp.where(jnp.arange(parts * cut) // cut == me, jnp.tile(b_qkv, parts), 0)
    ups = jnp.where(lane // unit == b_me % 2, jnp.tile(b_up, 2), 0)
    small = jnp.concatenate(
        [
            vectors,
            three.reshape(-1, 128),
            ups[None],
            jnp.zeros((6, 128), BF16),
        ]
    )
    up_cut = w_up.reshape(-1, groups, parts, unit).transpose(2, 0, 1, 3).reshape(parts, -1, groups * unit)
    qkv_cut = w_qkv.reshape(-1, 3, parts, heads * HD).transpose(2, 0, 1, 3).reshape(parts, -1, 3 * heads * HD)
    (G, F2, NB, UP, DN, ACT, GHL, GQ, GO, PM, SB, vec, g_sum, g_bu, g_bq) = front(
        x_local, g_local, small, tables(positions[0]), up_cut, qkv_cut, w_down, w_out
    )
    summed, back_sum, out_w_down, grad_w_up, grad_w_qkv, grad_w_out, sums = back(
        G, F2, NB, UP, DN, ACT, GHL, GQ, GO, PM, SB, vec, g_sum, g_bu, g_bq
    )

    x_f = x_local.astype(F32)
    layer_out = (x_f + summed + (vec[0] + vec[1])).astype(BF16)
    n_local, r_local = norm_stats(x_f)
    turned = r_local * (
        back_sum
        - jnp.mean(back_sum, -1, keepdims=True)
        - n_local * jnp.mean(back_sum * n_local, -1, keepdims=True)
    )
    grad_in = (g_local.astype(F32) + turned).astype(BF16)
    grad_w_up = grad_w_up.reshape(parts, -1, groups, unit).transpose(1, 2, 0, 3).reshape(w_up.shape)
    grad_w_qkv = grad_w_qkv.reshape(parts, -1, 3, heads * HD).transpose(1, 2, 0, 3).reshape(w_qkv.shape)
    pieces = lax.dynamic_slice_in_dim(sums[:5], me * rows16, rows16, 1)
    grad_b_qkv = lax.dynamic_slice_in_dim(sums[5:8].reshape(-1), me * cut, cut)
    grad_b_up = lax.dynamic_slice_in_dim(sums[8], b_me % 2 * unit, unit)
    return (
        layer_out[None],
        grad_in[None],
        grad_w_qkv.astype(F32),
        grad_b_qkv,
        grad_w_out.astype(F32),
        pieces[0],
        grad_w_up.astype(F32),
        grad_b_up,
        out_w_down,
        pieces[0],
        pieces[1],
        pieces[2],
        pieces[3],
        pieces[4],
    )


def solution(mesh):
    both = ("batch", "seq")
    rows = P("batch", "seq", None)
    matrix = P(both, None)
    vector = P(both)
    return jax.shard_map(
        shards,
        mesh=mesh,
        in_specs=(
            rows,
            P("batch", "seq"),
            matrix,
            vector,
            matrix,
            vector,
            matrix,
            vector,
            matrix,
            vector,
            vector,
            vector,
            vector,
            vector,
            rows,
        ),
        out_specs=(
            rows,
            rows,
            matrix,
            vector,
            matrix,
            vector,
            matrix,
            vector,
            matrix,
            vector,
            vector,
            vector,
            vector,
            vector,
        ),
        check_vma=False,
    )
```

time: 382 us -> 231 us (0.60); the launches traced: 375 us -> 230 us
  matrix products: 108 us -> 0 us
  other arithmetic: 30.9 us -> 7.22 us
  local copies, waits for them, and re-layouts: 33.8 us -> 14.4 us
  Pallas kernels: 201 us -> 208 us
    dot_general x17 -> x0, matrix products: 100 us -> none  [the longest x4 42.5 us: against(): lax.dot_general(left, right, (((1,), (1,)), ((), ())), preferred_element_...]
    convert_element_type x7 -> x0, other arithmetic: 13 us -> none  [the longest x1 6.35 us: shards(): first_in = (normed * gain_a + shift_a).astype(BF16)]
    sub x1 -> x0, matrix products: 7.82 us -> none  [shards(): exponent = jnp.exp(scores - jnp.max(scores, -1, keepdims=True))]
    pallas_call x2, Pallas kernels: 201 us -> 208 us  [the longest x1 114 us: front(): pl.pallas_call(front_kernel, out_shape=[jax.ShapeDtypeStruct(h, BF16) for...]
    concatenate x2 -> x0, local copies, waits for them, and re-layouts: 6.21 us -> none  [the longest x1 5.43 us: shards(): jnp.concatenate([b_out, b_down, gain_attn, shift_attn, gain_mlp, shift_ml...]
    unnamed x84 -> x22, local copies, waits for them, and re-layouts: 8.44 us -> 3.17 us
    slice x8 -> x2, local copies, waits for them, and re-layouts: 4.35 us -> 0.01 us  [the longest x1 0.01 us: shards(): grad_b_up = lax.dynamic_slice_in_dim(sums[8], b_me % 2 * unit, unit)]
where the time goes in v3:
time: 231 us; the launch traced here: 230 us
  Pallas kernels  208 us (90%)
  local copies, waits for them, and re-layouts  14.4 us (6%)
  other arithmetic  7.22 us (3%)
    pallas_call x1, Pallas kernels, front(): pl.pallas_call(front_kernel, out_shape=[jax.ShapeDtypeStruct(h, BF16) for...  114 us
    pallas_call x1, Pallas kernels, back(): pl.pallas_call(back_kernel, out_shape=[jax.ShapeDtypeStruct((128, C), F32...  94.1 us

profile of v3, /device:TPU:1, one launch (start us, length us, event | category | flops | bytes accessed | tf_op | source)
XLA Modules:
  0.0 230.3 jit_solution(10794918707169228367)
XLA Ops:
  0.7 0.7 tile.31
  1.4 0.8 stack.27
  2.2 0.1 tile.13
  2.3 0.7 tile.14
  3.1 0.6 pad_maximum_fusion.1.small_ref
  3.7 0.7 convert_bitcast_fusion
  4.4 0.1 multiply_cosine_fusion
  4.5 0.6 pad_maximum_fusion.rot_ref
  5.1 1.5 reshape.153
  6.6 1.1 reshape.154.up_ref
  7.7 1.0 copy.40
  8.7 0.1 copy.45
  8.8 0.9 reshape.156.qkv_ref
  9.7 113.7 %shard_map.254 = (bf16[1024,2048]{1,0:T(8,128)(2,1)}, bf16[1024,2048]{1,0:T(8,128)(2,1)}, bf16[1024,2048]{1,0:T(8,128)(2,1)}, bf16[4,4,128,1024]{3,2,1,0:T(8,128...) custom-call(bf16[128,2048]{1,0:T(8,128)(2,1)} %bitcast.57, ...), custom_call_target="tpu_custom_call" | custom-call | tf_op jit(solution)/shard_map/pallas_call | solution.py:491
  123.4 94.1 %shard_map.255 = (f32[128,2048]{1,0:T(8,128)}, f32[128,2048]{1,0:T(8,128)}, f32[64,2048]{1,0:T(8,128)}, bf16[8,16,1024]{2,1,0:T(8,128)(2,1)}, bf16[8,16,768]{2,1...) custom-call(bf16[4,2,128,2048]{3,2,1,0:T(8,128)(2,1)} %bitcast.58, bf16[4,2,128,2048]{3,2,1,0:T(8,128)(2,1)} %bitcast.59, ...), custom_call_target="tpu_custom_call" | custom-call | tf_op jit(solution)/shard_map/pallas_call | solution.py:863
  217.5 1.3 reshape.165
  218.8 0.6 copy.39
  219.5 1.2 reshape.163
  220.6 0.2 reshape.164
  220.9 0.2 copy.38
  221.1 0.9 copy.41
  222.0 0.2 convert_reduce_fusion
  222.1 0.3 fusion.9
  222.4 1.6 fusion.18
  224.0 0.9 slice_add_fusion
  225.0 1.6 fusion.13
  226.5 0.7 convert_element_type.66
  227.2 0.6 dynamic-slice_bitcast_fusion
  227.9 0.5 slice_bitcast_fusion.1
  228.4 0.6 dynamic_slice.11
  229.0 0.5 copy.48
  229.5 0.8 copy.49
  (35 shorter events, 0.5 us)
Async XLA Ops:
  217.5 3.1 %copy-start.5 = (bf16[8,16,768]{2,1,0:T(8,128)(2,1)S(1)}, bf16[8,16,768]{2,1,0:T(8,128)(2,1)}, u32[]{:S(2)}) copy-start(bf16[8,16,768]{2,1,0:T(8,128)(2,1)} %get-tuple-element.53) | copy-start | bytes 589828
  217.5 4.5 %copy-start = (bf16[1,128,2048]{2,1,0:T(8,128)(2,1)S(1)}, bf16[1,128,2048]{2,1,0:T(8,128)(2,1)}, u32[]{:S(2)}) copy-start(bf16[1,128,2048]{2,1,0:T(8,128)(2,1)} %param.15) | copy-start | bytes 1572868
  218.8 6.1 %copy-start.2 = (bf16[1,128,2048]{2,1,0:T(8,128)(2,1)S(1)}, bf16[1,128,2048]{2,1,0:T(8,128)(2,1)}, u32[]{:S(2)}) copy-start(bf16[1,128,2048]{2,1,0:T(8,128)(2,1)} %param.29) | copy-start | bytes 1572868
  219.5 5.5 %copy-start.1 = (f32[128,2048]{1,0:T(8,128)S(1)}, f32[128,2048]{1,0:T(8,128)}, u32[]{:S(2)}) copy-start(f32[128,2048]{1,0:T(8,128)} %get-tuple-element.52) | copy-start | bytes 3145732
  220.8 4.1 %copy-start.3 = (f32[128,2048]{1,0:T(8,128)S(1)}, f32[128,2048]{1,0:T(8,128)}, u32[]{:S(2)}) copy-start(f32[128,2048]{1,0:T(8,128)} %get-tuple-element.51) | copy-start | bytes 3145732
  220.8 5.7 %copy-start.6 = (bf16[16,2048]{1,0:T(8,128)(2,1)S(1)}, bf16[16,2048]{1,0:T(8,128)(2,1)}, u32[]{:S(2)}) copy-start(bf16[16,2048]{1,0:T(8,128)(2,1)} %get-tuple-element.55) | copy-start | bytes 196612
  220.9 6.4 %copy-start.7 = (f32[16,128]{1,0:T(8,128)S(1)}, f32[16,128]{1,0:T(8,128)}, u32[]{:S(2)}) copy-start(f32[16,128]{1,0:T(8,128)} %get-tuple-element.54) | copy-start | bytes 24580
  221.1 8.4 %copy-start.4 = (f32[64,2048]{1,0:T(8,128)S(1)}, f32[64,2048]{1,0:T(8,128)}, u32[]{:S(2)}) copy-start(f32[64,2048]{1,0:T(8,128)} %get-tuple-element.121) | copy-start | bytes 1572868
  228.4 1.9 copy-start.8

commit v4 on v1

v4 whole, which is shorter than its diff:
```python
import jax
import jax.numpy as jnp
from jax import lax
from jax.experimental import pallas as pl
from jax.experimental.pallas import tpu as pltpu
from jax.sharding import PartitionSpec as P

H = 16
HD = 128
ROT = 32
EPS = 1e-05
C = 2048
SCALE = HD ** (-0.5)
F32 = jnp.float32
BF16 = jnp.bfloat16
MESH = pl.DeviceIdType.MESH
STEPS = (1, -1, 2)
SEQ_PEERS = [(dy, dc) for dc in (1, 0) for dy in (0, 1, -1, 2) if (dy, dc) != (0, 0)]


def place():
    b = lax.axis_index("batch")
    s = lax.axis_index("seq")
    return b // 4, b % 4, s // 2, s % 2


def shifted(x=0, z=0, y=0, c=0):
    px, pz, py, pc = place()
    px = lax.rem(px + x + 4, 4)
    pz = lax.rem(pz + z + 4, 4)
    py = lax.rem(py + y + 4, 4)
    pc = lax.rem(pc + c, 2)
    return (px * 4 + pz, py * 2 + pc)


def moved(pos, step):
    return lax.rem(pos + step + 4, 4)


class Copies:
    def __init__(self, send, recv):
        self.send, self.recv, self.count, self.made = send, recv, 0, []

    def make(self, src, dst, device):
        k = self.count
        self.count += 1
        return pltpu.make_async_remote_copy(
            src_ref=src,
            dst_ref=dst,
            send_sem=self.send.at[k],
            recv_sem=self.recv.at[k],
            device_id=device,
            device_id_type=MESH,
        )

    def start(self, src, dst, device):
        copy = self.make(src, dst, device)
        copy.start()
        self.made.append(copy)
        return copy

    def drain(self):
        for copy in self.made:
            copy.wait_send()


class Locals:
    def __init__(self, sems):
        self.sems, self.count = sems, 0

    def start(self, src, dst):
        copy = pltpu.make_async_copy(src, dst, self.sems.at[self.count])
        self.count += 1
        copy.start()
        return copy


def greet(*extra):
    barrier = pltpu.get_barrier_semaphore()
    peers = [dict(x=d) for d in STEPS] + [dict(z=d) for d in STEPS]
    peers += [dict(y=dy, c=dc) for dy, dc in SEQ_PEERS]
    for p in peers:
        pl.semaphore_signal(barrier, inc=1, device_id=shifted(**p), device_id_type=MESH)
    count = len(peers)
    for differs, device in extra:

        @pl.when(differs)
        def _(device=device):
            pl.semaphore_signal(barrier, inc=1, device_id=device, device_id_type=MESH)

        count = jnp.where(differs, count + 1, count)
    pl.semaphore_wait(barrier, count)


def group(buf, first, at, half=None, rows=None):
    span = pl.ds(0, 4) if half is None else pl.ds(2 * half, 2)
    index = (span, at) if first == "x" else (at, span)
    if rows is not None:
        index += (pl.ds(*rows),)
    return buf.at[index]


class Gather:
    def __init__(self, copies, buf, first, rows=None):
        self.copies, self.buf, self.first, self.rows = copies, buf, first, rows
        self.other = "z" if first == "x" else "x"
        x, z, _, _ = place()
        self.at = z if first == "x" else x
        self.own = buf.at[x, z] if rows is None else buf.at[x, z, pl.ds(*rows)]

    def part(self, step, half=None):
        return group(self.buf, self.first, moved(self.at, step), half, self.rows)

    def one(self, src=None):
        src = self.own if src is None else src
        self.sent = [self.copies.start(src, self.own, shifted(**{self.first: d})) for d in STEPS]
        self.all = list(self.sent)

    def two(self):
        for c in self.sent:
            c.wait_recv()
        send = lambda d, half: self.copies.start(
            self.part(0, half), self.part(0, half), shifted(**{self.other: d})
        )
        self.early = [send(1, 0), send(-1, 1)]
        self.late = [send(1, 1), send(-1, 0)]
        self.all += self.early + self.late

    def three(self):
        for c, d, half in zip(self.early, (1, -1), (0, 1)):
            c.wait_recv()
            passed = self.part(-d, half)
            self.late.append(self.copies.start(passed, passed, shifted(**{self.other: d})))
        self.all += self.late[2:]

    def done(self):
        for c in self.late:
            c.wait_recv()


def out_route(groups=16, parts=8, heads=2):
    b = lax.axis_index("batch")
    s = lax.axis_index("seq")
    to = ((b % heads) * parts + s, b // heads)
    source = (s * heads + b // parts, b % parts)
    differs = jnp.logical_or(to[0] != b, to[1] != s)
    return to, source, differs


def dot(a, b, ca=1, cb=0):
    return lax.dot_general(a, b, (((ca,), (cb,)), ((), ())), preferred_element_type=F32)


Q_AT, K_AT, V_AT, U_AT, L_AT, M_AT = 0, 256, 512, 768, 1024, 1792


def turn(v, tc, ta, tb):
    return v * tc + pltpu.roll(v, 112, 1) * ta + pltpu.roll(v, 16, 1) * tb


def project(i, F1, QK, bq, TC, TA, TB, A):
    r = pl.ds(pl.multiple_of(i * 256, 256), 256)
    two = pl.ds(2 * i, 2)
    full = dot(F1[i].reshape(256, C), QK[...].reshape(C, 768)) + bq[...]
    tc, ta, tb = TC[r], TA[r], TB[r]

    def put(at, v):
        A[two, :, at : at + 128] = v.astype(BF16).reshape(2, 128, 128)

    for at in (0, 128):
        put(Q_AT + at, turn(full[:, at : at + 128], tc, ta, tb) * SCALE)
        put(K_AT + at, turn(full[:, 256 + at : 384 + at], tc, ta, tb))
        put(V_AT + at, full[:, 512 + at : 640 + at])


def head_pass(h, A, DK, DV, TC, TA, TB, gb):
    at = h * 128

    def rows(first, count, column):
        return A[first : first + count, :, column + at : column + at + 128].reshape(count * 128, 128)

    def put(first, count, column, v):
        A[first : first + count, :, column + at : column + at + 128] = v.astype(BF16).reshape(count, 128, 128)

    for i in reversed(range(4)):
        r = pl.ds(i * 256, 256)
        m = 2 * (i + 1)
        n = 128 * m
        q, g = rows(2 * i, 2, Q_AT), rows(2 * i, 2, U_AT)
        k, v = rows(0, m, K_AT), rows(0, m, V_AT)
        s = dot(q, k, 1, 1)
        row = lax.broadcasted_iota(jnp.int32, (256, n), 0) + i * 256
        col = lax.broadcasted_iota(jnp.int32, (256, n), 1)
        s = jnp.where(row >= col, s, -1e30)
        p = jnp.exp(s - jnp.max(s, -1, keepdims=True))
        p = p * (1.0 / jnp.sum(p, -1, keepdims=True))
        p_low = p.astype(BF16)
        put(2 * i, 2, M_AT, dot(p_low, v))
        gp = dot(g, v, 1, 1)
        gs = (p * (gp - jnp.sum(p * gp, -1, keepdims=True))).astype(BF16)
        dk, dv = dot(gs, q, 0, 0), dot(p_low, g, 0, 0)
        if i == 3:
            DK[...], DV[...] = dk, dv
        else:
            DK[0:n, :] += dk
            DV[0:n, :] += dv
        gq = dot(gs, k) * SCALE
        gq = turn(gq, TC[r], -TA[r], -TB[r])
        put(2 * i, 2, L_AT, gq)
        part = jnp.sum(gq, 0, keepdims=True)
        total = part if i == 3 else total + part
    gb[:, at : at + 128] = total
    gk = turn(DK[...], TC[...], -TA[...], -TB[...])
    put(0, 8, L_AT + 256, gk)
    gb[:, 256 + at : 384 + at] = jnp.sum(gk, 0, keepdims=True)
    gv = DV[...]
    put(0, 8, L_AT + 512, gv)
    gb[:, 512 + at : 640 + at] = jnp.sum(gv, 0, keepdims=True)


def add_rows(shape, into, parts):
    slabs, rows = shape
    step = min(rows, 16)

    def add(t, _):
        i = t // (rows // step)
        r = pl.ds(pl.multiple_of(t % (rows // step) * step, step), step)
        total = parts[0](i, r).astype(F32)
        for p in parts[1:]:
            total += p(i, r).astype(F32)
        into(i, r, total)
        return 0

    lax.fori_loop(0, slabs * (rows // step), add, 0)


class Scatter:
    def __init__(self, copies, buf, pool, first, rows=None):
        self.copies, self.buf, self.first, self.rows = copies, buf, first, rows
        cut = () if rows is None else (pl.ds(*rows),)
        self.pool = pool
        self.cut = cut
        self.other = "z" if first == "x" else "x"
        x, z, _, _ = place()
        self.at, self.mine = (z, x) if first == "x" else (x, z)
        self.count = buf.shape[2] if rows is None else rows[1]
        self.base = 0 if rows is None else rows[0]

    def part(self, step, half=None):
        return group(self.buf, self.first, moved(self.at, step), half, self.rows)

    def slab(self, step, i, r):
        at = moved(self.at, step)
        r = pl.ds(self.base + r.start, r.size)
        return (i, at, r) if self.first == "x" else (at, i, r)

    def relay(self, k):
        return self.pool.at[(0, pl.ds(2 * k, 2)) + self.cut]

    def land(self, k, half):
        return self.pool.at[(1 + k, pl.ds(2 * half, 2)) + self.cut]

    def last(self, k):
        return self.pool.at[(3, k) + self.cut]

    def held(self, i, j, r):
        return self.pool[i, j, pl.ds(self.base + r.start, r.size)]

    def one(self):
        start, to = self.copies.start, self.other
        self.far = [
            start(self.part(2, k), self.relay(k), shifted(**{to: d})) for k, d in enumerate((1, -1))
        ]
        self.near = [
            start(self.part(d, 1 - k), self.land(k, 1 - k), shifted(**{to: d}))
            for k, d in enumerate((1, -1))
        ]

    def mid(self):
        for k, d in enumerate((1, -1)):
            self.far[k].wait_recv()

            def put(i, r, total, k=k, d=d):
                self.buf[self.slab(d, i + 2 * k, r)] = total.astype(self.buf.dtype)

            add_rows(
                (2, self.count),
                put,
                [lambda i, r, k=k, d=d: self.buf[self.slab(d, i + 2 * k, r)],
                 lambda i, r, k=k: self.held(0, 2 * k + i, r)],
            )
            self.near.append(
                self.copies.start(
                    self.part(d, k), self.land(k, k), shifted(**{self.other: d})
                )
            )

    def two(self):
        for cp in self.near:
            cp.wait_recv()

        def put(i, r, total):
            self.buf[self.slab(0, i, r)] = total.astype(self.buf.dtype)

        add_rows(
            (4, self.count),
            put,
            [lambda i, r: self.buf[self.slab(0, i, r)],
             lambda i, r: self.held(1, i, r), lambda i, r: self.held(2, i, r)],
        )
        x, z, _, _ = place()
        self.sent = []
        for k, d in enumerate(STEPS):
            there = moved(self.mine, d)
            index = (there, self.at) if self.first == "x" else (self.at, there)
            if self.rows is not None:
                index += (pl.ds(*self.rows),)
            self.sent.append(
                self.copies.start(self.buf.at[index], self.last(k), shifted(**{self.first: d}))
            )

    def three(self, put):
        for cp in self.sent:
            cp.wait_recv()
        add_rows(
            (1, self.count),
            lambda i, r, total: put(r, total),
            [lambda i, r: self.buf[self.slab(0, self.mine, r)]]
            + [lambda i, r, k=k: self.held(3, k, r) for k in range(3)],
        )


class SeqScatter:
    def __init__(self, copies, buf, pool):
        self.copies, self.buf, self.pool = copies, buf, pool
        _, _, self.y, self.c = place()

    def one(self):
        self.sent = self.copies.start(self.buf.at[:, 1 - self.c], self.pool.at[pl.ds(0, 4)], shifted(c=1))

    def two(self):
        self.sent.wait_recv()
        buf, c = self.buf, self.c

        def put(i, r, total):
            buf[i, c, r] = total.astype(BF16)

        add_rows((4, 128), put, [lambda i, r: buf[i, c, r], lambda i, r: self.pool[i, r]])
        start = self.copies.start
        far = moved(self.y, 2)
        halves = (pl.ds(0, 64), pl.ds(64, 64))
        self.far = [
            start(buf.at[far, c, halves[k]], self.pool.at[4, halves[k]], shifted(y=d)) for k, d in enumerate((1, -1))
        ]
        self.near = [
            start(buf.at[moved(self.y, d), c, halves[1 - k]], self.pool.at[5 + k, halves[1 - k]], shifted(y=d))
            for k, d in enumerate((1, -1))
        ]

    def mid(self):
        buf, c = self.buf, self.c
        for k, d in enumerate((1, -1)):
            self.far[k].wait_recv()
            to = moved(self.y, d)

            def rows(r, k=k):
                return pl.ds(64 * k + r.start, r.size)

            def put(i, r, total, rows=rows, to=to):
                buf[to, c, rows(r)] = total.astype(BF16)

            add_rows(
                (1, 64),
                put,
                [lambda i, r, rows=rows, to=to: buf[to, c, rows(r)],
                 lambda i, r, rows=rows: self.pool[4, rows(r)]],
            )
            self.near.append(
                self.copies.start(
                    buf.at[to, c, pl.ds(64 * k, 64)], self.pool.at[5 + k, pl.ds(64 * k, 64)], shifted(y=d)
                )
            )

    def three(self, put):
        for cp in self.near:
            cp.wait_recv()
        buf, y, c = self.buf, self.y, self.c
        add_rows(
            (1, 128),
            lambda i, r, total: put(r, total),
            [lambda i, r: buf[y, c, r], lambda i, r: self.pool[5, r], lambda i, r: self.pool[6, r]],
        )


def layer_kernel(x_ref, g_ref, pos_ref, freq_ref, bo_ref, bd_ref, ga_ref, sa_ref, gm_ref, sm_ref, bq_ref, bu_ref,
                 up_ref, qkv_ref, down_ref, out_ref,
                 y_out, x_out, gd_out, gu_all, gq_all, go_all, sv,
                 X, G, SA, RA, SM, UP, QK, DN, WO, F1, F2, NB, ACT, GHL, GQ, GO, GD, GU, PP,
                 DK, DV, TC, TA, TB,
                 BQ, VT, v_land, CT, CP, vec, gsum, gbu, gbq, go_part,
                 send, recv, ready, loc):
    copies, local = Copies(send, recv), Locals(loc)
    x, z, y, c = place()
    s = y * 2 + c
    b_me = lax.axis_index("batch")
    to, source, differs = out_route()
    loads = [
        local.start(qkv_ref.at[:, pl.ds(C * p, C)], F1.at[0, 0, pl.ds(16 * p, 16)]) for p in range(3)
    ]
    x_load = local.start(x_ref, X.at[y, c])
    up_loads = [
        local.start(up_ref.at[:, pl.ds(C * p, C)], F2.at[0, 0, pl.ds(16 * p, 16)]) for p in range(4)
    ]
    down_load = local.start(down_ref, DN.at[x, z])
    g_load = local.start(g_ref, G.at[y, c])
    greet((differs, source), (differs, to))
    xz_peers = [shifted(**{a: d}) for a in ("x", "z") for d in STEPS]
    y_peers = [shifted(c=1)] + [shifted(y=d) for d in (1, -1)]

    def tell(k, peers):
        for p in peers:
            pl.semaphore_signal(ready.at[k], inc=1, device_id=p, device_id_type=MESH)

    def hear(k, peers):
        pl.semaphore_wait(ready.at[k], len(peers))

    def sent(group):
        for cp in group:
            cp.wait_send()
        copies.made = [cp for cp in copies.made if all(cp is not m for m in group)]

    down = [Gather(copies, DN, "x", (0, 32)), Gather(copies, DN, "z", (32, 32))]
    for g in down:
        g.one(down_ref.at[pl.ds(*g.rows)])

    def across(src, width, dst):
        def piece(k):
            return src.at[pl.ds(pl.multiple_of(k * 16, 16), 16), pl.ds(0, width)]

        dst[...] = piece(s)[...]
        return [
            copies.start(piece(moved(y, dy) * 2 + lax.rem(c + dc, 2)), dst, shifted(y=dy, c=dc))
            for dy, dc in SEQ_PEERS
        ]

    rows16 = pl.ds(pl.multiple_of(s * 16, 16), 16)
    for cp in loads:
        cp.wait()
    for k in range(8):
        for part in range(3):
            GHL[16 * k : 16 * (k + 1), 256 * part : 256 * (part + 1)] = (
                F1[0, 0, 16 * part : 16 * (part + 1), 256 * k : 256 * (k + 1)]
            )
    qk = across(GHL, 768, QK.at[x, z, rows16])
    out_copy = copies.make(out_ref, WO.at[to[0] // 4, to[0] % 4], to)

    @pl.when(differs)
    def _():
        out_copy.start()

    out_load = pltpu.make_async_copy(out_ref, WO.at[x, z], loc.at[15])

    @pl.when(jnp.logical_not(differs))
    def _():
        out_load.start()

    def placed(ref, width, at):
        v = jnp.concatenate([ref[...].astype(F32), jnp.zeros((1, width - ref.shape[1]), F32)], 1)
        return pltpu.roll(jnp.broadcast_to(v, (8, width)), at, 1)[0:1]

    vec[16:32, 0:128] = jnp.zeros((16, 128), F32)
    for k, ref in enumerate((bo_ref, bd_ref, ga_ref, sa_ref, gm_ref, sm_ref)):
        vec[16 + k : 17 + k, 0:128] = placed(ref, 128, s * 16)
    wide = placed(bq_ref, 384, s * 48)
    for k in range(3):
        vec[22 + k : 23 + k, 0:128] = wide[:, 128 * k : 128 * (k + 1)]
    vec[25:26, 0:128] = placed(bu_ref, 128, b_me % 2 * 64)
    SA[s] = vec[16:32, 0:128].astype(BF16)
    sm = [copies.start(SA.at[s], SA.at[s], shifted(y=dy, c=dc)) for dy, dc in SEQ_PEERS]

    def seq_one(src, dst):
        own = dst.at[y, c]
        return [copies.start(src, own, shifted(y=d)) for d in (1, -1)] + [
            copies.start(src, own, shifted(c=1))
        ]

    def seq_two(sent, dst):
        more = []
        for cp, d in zip(sent[:2], (1, -1)):
            cp.wait_recv()
            got = dst.at[moved(y, -d), c]
            more.append(copies.start(got, got, shifted(c=1)))
        up_way = c == 0
        got = dst.at[jnp.where(up_way, moved(y, -1), moved(y, 1)), c]
        py = jnp.where(up_way, moved(y, 1), moved(y, -1))
        fwd = copies.start(got, got, (b_me, py * 2 + c))
        sent[2].wait_recv()
        return more, fwd

    def seq_three(more, fwd, dst):
        fwd.wait_recv()
        got = dst.at[moved(y, 2), c]
        return more + [copies.start(got, got, shifted(c=1))]

    xs = seq_one(x_ref, X)
    angle = pos_ref[...].astype(F32) * freq_ref[...]
    RA[s, 0:16, :] = jnp.cos(angle)
    RA[s, 16:32, :] = jnp.sin(angle)
    ra = [copies.start(RA.at[s], RA.at[s], shifted(y=dy, c=dc)) for dy, dc in SEQ_PEERS]
    for cp in up_loads:
        cp.wait()
    lane = lax.broadcasted_iota(jnp.int32, (16, 128), 1)
    for k in range(8):
        for p in range(8):
            at = (8 * p + k // 2) * 128
            r, at = 16 * (at // C), at % C
            one = F2[0, 0, r : r + 16, at : at + 128].astype(F32)
            two = F2[0, 0, r : r + 16, at + 512 : at + 640].astype(F32)
            if k % 2 == 0:
                two = pltpu.roll(two, 64, 1)
            else:
                one = pltpu.roll(one, 64, 1)
            ACT[16 * k : 16 * (k + 1), 128 * p : 128 * (p + 1)] = jnp.where(lane < 64, one, two).astype(BF16)
    up = across(ACT, 1024, UP.at[x, z, rows16])

    for cp in qk:
        cp.wait_recv()
    qa = Gather(copies, QK, "x", (0, 48))
    qb = Gather(copies, QK, "z", (48, 80))
    qa.one()
    qb.one()

    @pl.when(differs)
    def _():
        out_copy.wait()

    @pl.when(jnp.logical_not(differs))
    def _():
        out_load.wait()

    wo = Gather(copies, WO, "x")
    wo.one()
    for cp in sm:
        cp.wait_recv()
    total = SA[0].astype(F32)
    for k in range(1, 8):
        total += SA[k].astype(F32)
    row = lax.broadcasted_iota(jnp.int32, (16, 128), 0)
    SM[x, z] = jnp.where(row == 9, SA[s].astype(F32), total).astype(BF16)
    small = Gather(copies, SM, "z")
    small.one()
    g_load.wait()
    total = jnp.zeros((1, C), F32)
    for k in range(8):
        total += jnp.sum(G[y, c, 16 * k : 16 * (k + 1)].astype(F32), 0, keepdims=True)
    gsum[...] = total
    qa.two()
    qb.two()
    small.two()
    wo.two()
    xs2, xf = seq_two(xs, X)
    gs = seq_one(g_ref, G)
    small.three()
    qa.three()
    qb.three()
    for cp in up:
        cp.wait_recv()
    upg = [Gather(copies, UP, "x", (0, 64)), Gather(copies, UP, "z", (64, 64))]
    for g in upg:
        g.one()
    wo.three()
    down_load.wait()
    for g in down:
        g.two()
    small.done()
    for i in range(4):
        for j in range(4):
            b = i * 4 + j
            tile = SM[i, j].astype(F32)
            vec[0:6, b * 128 : (b + 1) * 128] = tile[0:6]
            for k in range(3):
                BQ[3 * b + k : 3 * b + k + 1, :] = tile[6 + k : 7 + k]
            if b % 2 == 0:
                kept = tile[9:10]
            else:
                vec[6:7, b // 2 * 128 : (b // 2 + 1) * 128] = kept + tile[9:10]

    def norm(ky, kc):
        def step(t, _):
            r = pl.ds(pl.multiple_of(t * 16, 16), 16)
            v = X[ky, kc, r].astype(F32)
            v = v - jnp.mean(v, -1, keepdims=True)
            n = v * lax.rsqrt(jnp.mean(v * v, -1, keepdims=True) + EPS)
            NB[ky * 2 + kc, r] = n.astype(BF16)
            F1[ky, kc, r] = (n * vec[2:3, :] + vec[3:4, :]).astype(BF16)
            F2[ky, kc, r] = (n * vec[4:5, :] + vec[5:6, :]).astype(BF16)
            return 0

        lax.fori_loop(0, 8, step, 0)

    x_load.wait()
    norm(y, c)
    norm(y, 1 - c)
    norm(moved(y, -1), c)
    norm(moved(y, 1), c)
    xs3 = seq_three(xs2, xf, X)
    xs3[0].wait_recv()
    norm(moved(y, -1), 1 - c)
    xs3[1].wait_recv()
    norm(moved(y, 1), 1 - c)
    gs2, gf = seq_two(gs, G)
    norm(moved(y, 2), c)
    xs3[2].wait_recv()
    norm(moved(y, 2), 1 - c)
    for cp in ra:
        cp.wait_recv()

    lane = lax.broadcasted_iota(jnp.int32, (128, 128), 1)
    for k in range(8):
        r = pl.ds(k * 128, 128)
        tile = jnp.concatenate([RA[k], jnp.zeros((96, 128), F32)], 0).T
        TC[r] = jnp.where(lane < 16, tile, jnp.where(lane < 32, pltpu.roll(tile, 16, 1), 1.0))
        TA[r] = jnp.where(lane < 16, -pltpu.roll(tile, 112, 1), 0.0)
        TB[r] = jnp.where((lane >= 16) & (lane < 32), tile, 0.0)
    for gth in (qa, qb):
        gth.done()
    for part in range(3):
        pair = BQ[pl.ds(part * 16 + s * 2, 2), :]
        for k in range(2):
            at = part * 256 + k * 128
            vec[9:10, at : at + 128] = pair[k : k + 1]

    def first(i, _):
        project(i, F1, QK, vec.at[9:10, 0:768], TC, TA, TB, PP)
        return 0

    lax.fori_loop(0, 4, first, 0)
    for g in upg:
        g.two()
    gs3 = seq_three(gs2, gf, G)
    wo.done()
    for cp in gs3:
        cp.wait_recv()

    def mixed(i, _):
        total = dot(G[i].reshape(256, C), WO[...].reshape(256, C), 1, 1)
        PP[pl.ds(2 * i, 2), :, U_AT:L_AT] = total.astype(BF16).reshape(2, 128, 256)
        return 0

    lax.fori_loop(0, 4, mixed, 0)
    for g in down:
        g.three()
    for h in range(2):
        head_pass(h, PP, DK, DV, TC, TA, TB, gbq)
    for g in upg:
        g.three()

    def grad_out(j, _):
        q = pl.ds(pl.multiple_of(j * 1024, 1024), 1024)
        mix = PP[:, :, M_AT:].reshape(1024, 256)
        GO[:, :, :, q] = dot(mix, G[:, :, :, q].reshape(1024, 1024), 0, 0).astype(BF16).reshape(4, 4, 16, 1024)
        return 0

    lax.fori_loop(0, 2, grad_out, 0)

    def grad_qkv(i, _):
        r = pl.ds(pl.multiple_of(i * 512, 512), 512)
        right = PP[:, :, L_AT:M_AT].reshape(1024, 768)
        GQ[i] = dot(F1[:, :, :, r].reshape(1024, 512), right, 0, 0).astype(BF16).reshape(4, 128, 768)
        return 0

    lax.fori_loop(0, 4, grad_qkv, 0)
    sent(xs + xs2 + [xf, xs3[2]])

    def attend(t, _):
        i, j = t // 2, t % 2
        q = pl.ds(pl.multiple_of(j * 1024, 1024), 1024)
        mix = PP[pl.ds(4 * i, 4), :, M_AT:].reshape(512, 256)
        total = dot(mix, WO[:, :, :, q].reshape(256, 1024))
        X[pl.ds(2 * i, 2), :, :, q] = total.astype(BF16).reshape(2, 2, 128, 1024)
        return 0

    lax.fori_loop(0, 4, attend, 0)
    vec[10:12, :] = jnp.zeros((2, C), F32)

    def grad_first(t, _):
        i, j = t // 4, t % 4
        q = pl.ds(pl.multiple_of(j * 512, 512), 512)
        left = PP[pl.ds(2 * i, 2), :, L_AT:M_AT].reshape(256, 768)
        u = dot(left, QK[j].reshape(512, 768), 1, 1)
        n = NB[pl.ds(2 * i, 2), :, q].reshape(256, 512).astype(F32)
        vec[10:11, q] += jnp.sum(u * n, 0, keepdims=True)
        vec[11:12, q] += jnp.sum(u, 0, keepdims=True)
        F1[i, :, :, q] = (u * vec[2:3, q]).astype(BF16).reshape(2, 128, 512)
        return 0

    lax.fori_loop(0, 16, grad_first, 0)

    for g in (qa, qb, wo):
        sent(g.all)
    sent(qk + up)
    tell(0, xz_peers)
    tell(4, y_peers)

    sa = Scatter(copies, GQ, QK, "x", (0, 48))
    sb = Scatter(copies, GQ, QK, "z", (48, 80))
    so = Scatter(copies, GO, WO, "x")
    fp = SeqScatter(copies, X, PP)
    fq = SeqScatter(copies, F1, NB)
    gbu[...] = jnp.zeros_like(gbu)
    hear(0, xz_peers)
    for g in (sa, sb, so):
        g.one()
    for g in down + upg:
        g.done()

    def hidden(t, _):
        i, j = t // 2, t % 2
        r = pl.ds(pl.multiple_of(i * 256, 256), 256)
        q = pl.ds(pl.multiple_of(j * 512, 512), 512)
        h = dot(F2[i].reshape(256, C), UP[:, :, :, q].reshape(C, 512)) + vec[6:7, q]
        ga = dot(G[i].reshape(256, C), DN[pl.ds(2 * j, 2)].reshape(512, C), 1, 1)
        cdf = 0.5 + 0.5 * lax.erf(h * (0.5**0.5))
        ACT[r, q] = (h * cdf).astype(BF16)
        gh = ga * (cdf + h * (jnp.exp(h * h * -0.5) * 0.3989422804014327))
        gbu[:, q] += jnp.sum(gh, 0, keepdims=True)
        GHL[r, q] = gh.astype(BF16)
        return 0

    lax.fori_loop(0, 8, hidden, 0)
    for g in (sa, sb, so):
        g.mid()

    def feed(t, _):
        i, j = t // 4, t % 4
        r = pl.ds(pl.multiple_of(i * 512, 512), 512)
        q = pl.ds(pl.multiple_of(j * 512, 512), 512)
        two = pl.ds(2 * i, 2)
        total = dot(ACT[r], DN[:, :, :, q].reshape(1024, 512)) + X[two, :, :, q].reshape(512, 512).astype(F32)
        X[two, :, :, q] = total.astype(BF16).reshape(2, 2, 128, 512)
        return 0

    lax.fori_loop(0, 8, feed, 0)
    hear(4, y_peers)
    fp.one()
    for g in down:
        sent(g.all)
    tell(1, xz_peers)

    sd = [Scatter(copies, GD, DN, "x", (0, 32)), Scatter(copies, GD, DN, "z", (32, 32))]
    su = [Scatter(copies, GU, UP, "x", (0, 64)), Scatter(copies, GU, UP, "z", (64, 64))]
    sc = Scatter(copies, CT, CP, "z")

    def grad_down(t, _):
        i, j = t // 2, t % 2
        u = pl.ds(pl.multiple_of(i * 256, 256), 256)
        q = pl.ds(pl.multiple_of(j * 1024, 1024), 1024)
        right = G[:, :, :, q].reshape(1024, 1024)
        GD[i, :, :, q] = dot(ACT[:, u], right, 0, 0).astype(BF16).reshape(4, 64, 1024)
        return 0

    lax.fori_loop(0, 8, grad_down, 0)
    sent(gs3 + [gf])
    again = [local.start(x_ref, G.at[0, 0]), local.start(g_ref, G.at[0, 1])]
    hear(1, xz_peers)
    for g in sd:
        g.one()
    for g in (sa, sb, so):
        g.two()
    fp.two()
    vec[12:14, :] = jnp.zeros((2, C), F32)

    def second(t, _):
        i, j = t // 4, t % 4
        r = pl.ds(pl.multiple_of(i * 256, 256), 256)
        q = pl.ds(pl.multiple_of(j * 512, 512), 512)
        u = dot(GHL[r], UP[j].reshape(512, 1024), 1, 1)
        n = NB[pl.ds(2 * i, 2), :, q].reshape(256, 512).astype(F32)
        vec[12:13, q] += jnp.sum(u * n, 0, keepdims=True)
        vec[13:14, q] += jnp.sum(u, 0, keepdims=True)
        total = u * vec[4:5, q] + F1[i, :, :, q].reshape(256, 512).astype(F32)
        F1[i, :, :, q] = total.astype(BF16).reshape(2, 128, 512)
        return 0

    lax.fori_loop(0, 16, second, 0)
    for g in upg:
        sent(g.all)
    tell(2, xz_peers)
    tell(3, y_peers)

    def grad_up(t, _):
        i, j = t // 2, t % 2
        r = pl.ds(pl.multiple_of(i * 512, 512), 512)
        q = pl.ds(pl.multiple_of(j * 512, 512), 512)
        left = F2[:, :, :, r].reshape(1024, 512)
        GU[i, :, :, q] = dot(left, GHL[:, q], 0, 0).astype(BF16).reshape(4, 128, 512)
        return 0

    lax.fori_loop(0, 8, grad_up, 0)
    hear(2, xz_peers)
    for g in su:
        g.one()
    hear(3, y_peers)
    fq.one()

    BQ[...] = jnp.zeros_like(BQ)
    for part in range(3):
        for k in range(2):
            at = part * 256 + k * 128
            BQ[pl.ds(part * 16 + s * 2 + k, 1), :] = gbq[:, at : at + 128]
    for b in range(16):
        at = b * 128
        VT[b, 0:1, :] = gsum[:, at : at + 128]
        VT[b, 1:5, :] = vec[10:14, at : at + 128]
        VT[b, 5:8, :] = BQ[3 * b : 3 * b + 3, :]
    vs = [
        copies.start(VT, v_land.at[k], shifted(y=dy, c=dc)) for k, (dy, dc) in enumerate(SEQ_PEERS)
    ]
    for g in sd:
        g.mid()
    fp.mid()

    def store(ref, base=0):
        def put(r, total):
            ref[pl.ds(base + r.start, r.size)] = total.astype(ref.dtype)

        return put

    gu_part = ACT.at[pl.ds(0, 128)]
    gq_part = ACT.at[pl.ds(128, 128), pl.ds(0, 768)]

    def spread(part, out):
        out[s] = part[pl.ds(pl.multiple_of(s * 16, 16), 16)]
        made = []
        for dy, dc in SEQ_PEERS:
            peer = moved(y, dy) * 2 + lax.rem(c + dc, 2)
            made.append(
                copies.start(
                    part.at[pl.ds(pl.multiple_of(peer * 16, 16), 16)], out.at[s], shifted(y=dy, c=dc)
                )
            )
        return made

    fq.two()
    sa.three(store(gq_part))
    sb.three(store(gq_part, 48))
    backs = spread(gq_part, gq_all)
    so.three(store(go_part))
    out_back = copies.make(go_part, go_all, source)

    @pl.when(differs)
    def _():
        out_back.start()

    @pl.when(jnp.logical_not(differs))
    def _():
        go_all[...] = go_part[...]

    for cp in vs:
        cp.wait_recv()
    for b in range(16):
        total = VT[b]
        for k in range(7):
            total += v_land[k, b]
        CT[b // 4, b % 4, 0:8, :] = total
        CT[b // 4, b % 4, 8:9, :] = gbu[:, b // 2 * 128 : b // 2 * 128 + 128]
        CT[b // 4, b % 4, 9:16, :] = jnp.zeros((7, 128), F32)
    sc.one()
    for g in su:
        g.mid()
    for g in sd:
        g.two()
    fq.mid()
    sc.mid()

    def layer_out(r, total):
        bias = vec[0:1, :] + vec[1:2, :]
        y_out[r] = (G[0, 0, r].astype(F32) + total + bias).astype(BF16)

    for cp in again:
        cp.wait()
    fp.three(layer_out)
    sc.two()
    for g in su:
        g.two()
    for k, g in enumerate(sd):
        g.three(store(gd_out, 32 * k))

    def grad_in(r, total):
        v = G[0, 0, r].astype(F32)
        v = v - jnp.mean(v, -1, keepdims=True)
        inv = lax.rsqrt(jnp.mean(v * v, -1, keepdims=True) + EPS)
        n = v * inv
        total = total - jnp.mean(total, -1, keepdims=True) - n * jnp.mean(total * n, -1, keepdims=True)
        x_out[r] = (G[0, 1, r].astype(F32) + total * inv).astype(BF16)

    fq.three(grad_in)
    for k, g in enumerate(su):
        g.three(store(gu_part, 64 * k))
    backs += spread(gu_part, gu_all)
    sc.three(store(sv))

    @pl.when(differs)
    def _():
        out_back.wait()

    for cp in backs:
        cp.wait_recv()
    copies.drain()


def layer(x, g, pos, freq, vectors, up, qkv, down, out):
    any_ = pl.BlockSpec(memory_space=pl.ANY)
    vm = pl.BlockSpec(memory_space=pltpu.VMEM)
    n_up, n_qkv = up.shape[-1] // 8, qkv.shape[-1] // 8
    up_all, qk_all = (4, 4, 128, n_up), (4, 4, 128, n_qkv)
    dn_all, wo_all = (4, 4) + down.shape, (4, 4) + out.shape
    blocks, unit = (4, 2, 128, C), (1024, n_up)
    S = pltpu.VMEM
    scratch = [
        (blocks, BF16), (blocks, BF16), ((8, 16, 128), BF16), ((8, 32, 128), F32), ((4, 4, 16, 128), BF16),
        (up_all, BF16), (qk_all, BF16), (dn_all, BF16), (wo_all, BF16),
        (blocks, BF16), (blocks, BF16), ((8, 128, C), BF16), (unit, BF16), (unit, BF16),
        (qk_all, BF16), (wo_all, BF16), (dn_all, BF16), (up_all, BF16), ((8, 128, C), BF16),
        ((1024, HD), F32), ((1024, HD), F32), ((1024, HD), F32), ((1024, HD), F32), ((1024, HD), F32),
        ((48, 128), F32), ((16, 8, 128), F32), ((7, 16, 8, 128), F32), ((4, 4, 16, 128), F32), ((4, 4, 16, 128), F32),
        ((32, C), F32), ((1, C), F32), ((1, n_up), F32), ((1, n_qkv), F32),
        (out.shape, BF16),
    ]
    outs = [
        (x.shape, BF16), (x.shape, BF16), (down.shape, F32),
        ((8, 16, n_up), BF16), ((8, 16, n_qkv), BF16), (out.shape, BF16), ((16, 128), F32),
    ]
    return pl.pallas_call(
        layer_kernel,
        out_shape=[jax.ShapeDtypeStruct(*o) for o in outs],
        in_specs=[any_, any_] + [vm] * 10 + [any_] * 4,
        out_specs=[vm] * 7,
        scratch_shapes=[S(*h) for h in scratch]
        + [pltpu.SemaphoreType.DMA((230,)), pltpu.SemaphoreType.DMA((230,)), pltpu.SemaphoreType.REGULAR((5,)), pltpu.SemaphoreType.DMA((16,))],
        compiler_params=pltpu.CompilerParams(
            collective_id=1, has_side_effects=True, vmem_limit_bytes=64 * 2**20 - 2**16
        ),
    )(x, g, pos, freq, *vectors, up, qkv, down, out)


def finish_kernel(y_in, x_in, gd_in, gu_in, gq_in, go_in, sv,
                  y_out, x_out, gd, gu, gq, go, b_out, b_down, ga, sa, gm, sm, bq, bu):
    s = lax.axis_index("seq")
    b = lax.axis_index("batch")
    y_out[...] = y_in[...]
    x_out[...] = x_in[...]
    gd[...] = gd_in[...]
    go[...] = go_in[...].astype(F32)
    for k in range(8):
        for part in range(3):
            piece = gq_in[k, :, 256 * part : 256 * (part + 1)]
            gq[:, C * part + 256 * k : C * part + 256 * (k + 1)] = piece.astype(F32)
    lane = lax.broadcasted_iota(jnp.int32, (16, 128), 1)
    for j in range(4):
        for p in range(8):
            one = gu_in[2 * j, :, 128 * p : 128 * (p + 1)].astype(F32)
            two = gu_in[2 * j + 1, :, 128 * p : 128 * (p + 1)].astype(F32)
            at = (8 * p + j) * 128
            gu[:, at : at + 128] = jnp.where(lane < 64, one, pltpu.roll(two, 64, 1))
            gu[:, at + 512 : at + 640] = jnp.where(lane < 64, pltpu.roll(one, 64, 1), two)
    mine = pltpu.roll(sv[...], lax.rem(128 - s * 16, 128), 1)
    for k, ref in enumerate((b_out, ga, sa, gm, sm)):
        ref[...] = mine[k : k + 1, 0:16]
    b_down[...] = mine[0:1, 0:16]
    wide = jnp.concatenate([jnp.broadcast_to(sv[k : k + 1, :], (8, 128)) for k in (5, 6, 7)], 1)
    bq[...] = pltpu.roll(wide, lax.rem(384 - s * 48, 384), 1)[0:1, 0:48]
    tail = pltpu.roll(sv[8:16, :], lax.rem(b, 2) * 64, 1)
    bu[...] = tail[0:1, 0:64]


def finish(*parts):
    vm = pl.BlockSpec(memory_space=pltpu.VMEM)
    y, xg, gd, gu, gq, go, _ = parts
    outs = [(y.shape, BF16), (xg.shape, BF16), (gd.shape, F32), ((16, 8 * gu.shape[-1]), F32), ((16, 8 * gq.shape[-1]), F32), (go.shape, F32)]
    outs += [((1, 16), F32)] * 6 + [((1, 48), F32), ((1, 64), F32)]
    return pl.pallas_call(
        finish_kernel,
        out_shape=[jax.ShapeDtypeStruct(*o) for o in outs],
        in_specs=[vm] * 7,
        out_specs=[vm] * len(outs),
    )(*parts)


def shards(
    inputs,
    positions,
    w_qkv,
    b_qkv,
    w_out,
    b_out,
    w_up,
    b_up,
    w_down,
    b_down,
    gain_attn,
    shift_attn,
    gain_mlp,
    shift_mlp,
    grad_out,
):
    half_rot = ROT // 2
    exponent = jnp.arange(half_rot).astype(F32) / half_rot
    frequency = jnp.broadcast_to(jnp.power(10000.0, -exponent)[:, None], (half_rot, 128))
    vectors = [
        v[None] for v in (b_out, b_down, gain_attn, shift_attn, gain_mlp, shift_mlp, b_qkv, b_up)
    ]
    parts = layer(inputs[0], grad_out[0], positions, frequency, vectors, w_up, w_qkv, w_down, w_out)
    layer_out, grad_in, g_down, g_up, g_qkv, g_out, *rest = finish(*parts)
    g_b_out, g_b_down, g_gain_a, g_shift_a, g_gain_m, g_shift_m, g_b_qkv, g_b_up = [v[0] for v in rest]
    return (
        layer_out[None],
        grad_in[None],
        g_qkv,
        g_b_qkv,
        g_out,
        g_b_out,
        g_up,
        g_b_up,
        g_down,
        g_b_down,
        g_gain_a,
        g_shift_a,
        g_gain_m,
        g_shift_m,
    )


def solution(mesh):
    both = ("batch", "seq")
    rows = P("batch", "seq", None)
    matrix = P(both, None)
    vector = P(both)
    return jax.shard_map(
        shards,
        mesh=mesh,
        in_specs=(
            rows,
            P("batch", "seq"),
            matrix,
            vector,
            matrix,
            vector,
            matrix,
            vector,
            matrix,
            vector,
            vector,
            vector,
            vector,
            vector,
            rows,
        ),
        out_specs=(
            rows,
            rows,
            matrix,
            vector,
            matrix,
            vector,
            matrix,
            vector,
            matrix,
            vector,
            vector,
            vector,
            vector,
            vector,
        ),
        check_vma=False,
    )
```

time: 861 us -> 191 us (0.22)
  waiting for transfers between devices: 489 us -> 0 us
  Pallas kernels: 0 us -> 189 us
  blocking collectives: 141 us -> 0 us
  matrix products: 126 us -> 0 us
  local copies, waits for them, and re-layouts: 34.4 us -> 0.67 us
  starting transfers between devices: 24.9 us -> 0 us
  other arithmetic: 23.5 us -> 0.01 us
  between operations: 15.7 us -> 0.82 us
    reduce_scatter x6 -> x0, waiting for transfers between devices: 356 us -> none  [the longest x1 78.9 us: shards(): lax.psum_scatter(grad_w_down, 'batch', scatter_dimension=0, tiled=True)]
    pallas_call x0 -> x2, Pallas kernels: none -> 189 us  [the longest x1 186 us: layer(): pl.pallas_call(layer_kernel, out_shape=[jax.ShapeDtypeStruct(*o) for o in...]
    dot_general x17 -> x0, matrix products: 118 us -> none  [the longest x4 39.7 us: against(): lax.dot_general(left, right, (((1,), (1,)), ((), ())), preferred_element_...]
    unnamed x2 -> x0, blocking collectives: 98.2 us -> none
    unnamed x14 -> x0, waiting for transfers between devices: 95.6 us -> none
    all_gather x6 -> x0, waiting for transfers between devices: 32.8 us -> none  [the longest x1 32.8 us: shards(): w_down_f = lax.all_gather(w_down, 'batch', axis=0, tiled=True)]
    all_to_all x2 -> x0, blocking collectives: 26 us -> none  [the longest x1 14.2 us: shards(): lax.all_to_all(w_up_t, 'seq', split_axis=2, concat_axis=0, tiled=True)]
    all_gather x1 -> x0, blocking collectives: 16.8 us -> none  [shards(): pos_rows = lax.all_gather(positions[0], 'seq', axis=0, tiled=True)]
  transfers between devices with their start and end apart: 17 -> 0, of which waited for: 10 -> 0; matrix products, arithmetic and copies ran while one was open for 17% -> 0% of each run, Pallas kernels for 0% -> 0%
where the time goes in v4:
time: 191 us
  Pallas kernels  189 us (99%)
    pallas_call x1, Pallas kernels, layer(): pl.pallas_call(layer_kernel, out_shape=[jax.ShapeDtypeStruct(*o) for o in...  186 us

profile of v4, /device:TPU:1, one launch (start us, length us, event | category | flops | bytes accessed | tf_op | source)
XLA Modules:
  0.0 190.7 jit_solution(7702090143967199808)
XLA Ops:
  0.7 0.7 broadcast_in_dim.36.freq_ref
  1.3 186.0 %shard_map.254 = (bf16[128,2048]{1,0:T(8,128)(2,1)}, bf16[128,2048]{1,0:T(8,128)(2,1)}, f32[64,2048]{1,0:T(8,128)}, bf16[8,16,1024]{2,1,0:T(8,128)(2,1)}, bf16[8...) custom-call(bf16[128,2048]{1,0:T(8,128)(2,1)} %bitcast.20, bf16[128,2048]{1,0:T(8,128)(2,1)} %bitcast.21, ...), custom_call_target="tpu_custom_call" | custom-call | tf_op jit(solution)/shard_map/pallas_call | solution.py:934
  187.4 3.2 %shard_map.255 = (bf16[128,2048]{1,0:T(8,128)(2,1)}, bf16[128,2048]{1,0:T(8,128)(2,1)}, f32[64,2048]{1,0:T(8,128)}, f32[16,8192]{1,0:T(8,128)}, f32[16,6144]{1,0...) custom-call(bf16[128,2048]{1,0:T(8,128)(2,1)} %get-tuple-element.35., ...), custom_call_target="tpu_custom_call" | custom-call | tf_op jit(solution)/shard_map/pallas_call | solution.py:982
  (1 shorter events, 0.0 us)

commit v5 on v4

--- a/solution.py
+++ b/solution.py
@@ -593,7 +593,9 @@
             n = v * lax.rsqrt(jnp.mean(v * v, -1, keepdims=True) + EPS)
             NB[ky * 2 + kc, r] = n.astype(BF16)
             F1[ky, kc, r] = (n * vec[2:3, :] + vec[3:4, :]).astype(BF16)
-            F2[ky, kc, r] = (n * vec[4:5, :] + vec[5:6, :]).astype(BF16)
+            F2[ky, 2 * kc + t // 4, pl.ds(pl.multiple_of(t % 4 * 16, 16), 16)] = (
+                n * vec[4:5, :] + vec[5:6, :]
+            ).astype(BF16)
             return 0
 
         lax.fori_loop(0, 8, step, 0)
@@ -731,43 +733,9 @@
     for g in (sa, sb, so):
         g.mid()
 
-    def feed(t, _):
-        i, j = t // 4, t % 4
-        r = pl.ds(pl.multiple_of(i * 512, 512), 512)
-        q = pl.ds(pl.multiple_of(j * 512, 512), 512)
-        two = pl.ds(2 * i, 2)
-        total = dot(ACT[r], DN[:, :, :, q].reshape(1024, 512)) + X[two, :, :, q].reshape(512, 512).astype(F32)
-        X[two, :, :, q] = total.astype(BF16).reshape(2, 2, 128, 512)
-        return 0
-
-    lax.fori_loop(0, 8, feed, 0)
-    hear(4, y_peers)
-    fp.one()
-    for g in down:
-        sent(g.all)
-    tell(1, xz_peers)
-
-    sd = [Scatter(copies, GD, DN, "x", (0, 32)), Scatter(copies, GD, DN, "z", (32, 32))]
+    sd = [Scatter(copies, GD, F2, "x", (0, 32)), Scatter(copies, GD, F2, "z", (32, 32))]
     su = [Scatter(copies, GU, UP, "x", (0, 64)), Scatter(copies, GU, UP, "z", (64, 64))]
     sc = Scatter(copies, CT, CP, "z")
-
-    def grad_down(t, _):
-        i, j = t // 2, t % 2
-        u = pl.ds(pl.multiple_of(i * 256, 256), 256)
-        q = pl.ds(pl.multiple_of(j * 1024, 1024), 1024)
-        right = G[:, :, :, q].reshape(1024, 1024)
-        GD[i, :, :, q] = dot(ACT[:, u], right, 0, 0).astype(BF16).reshape(4, 64, 1024)
-        return 0
-
-    lax.fori_loop(0, 8, grad_down, 0)
-    sent(gs3 + [gf])
-    again = [local.start(x_ref, G.at[0, 0]), local.start(g_ref, G.at[0, 1])]
-    hear(1, xz_peers)
-    for g in sd:
-        g.one()
-    for g in (sa, sb, so):
-        g.two()
-    fp.two()
     vec[12:14, :] = jnp.zeros((2, C), F32)
 
     def second(t, _):
@@ -797,11 +765,28 @@
         return 0
 
     lax.fori_loop(0, 8, grad_up, 0)
+    tell(1, xz_peers)
+    hear(3, y_peers)
+    fq.one()
     hear(2, xz_peers)
     for g in su:
         g.one()
-    hear(3, y_peers)
-    fq.one()
+
+    def grad_down(t, _):
+        i, j = t // 2, t % 2
+        u = pl.ds(pl.multiple_of(i * 256, 256), 256)
+        q = pl.ds(pl.multiple_of(j * 1024, 1024), 1024)
+        right = G[:, :, :, q].reshape(1024, 1024)
+        GD[i, :, :, q] = dot(ACT[:, u], right, 0, 0).astype(BF16).reshape(4, 64, 1024)
+        return 0
+
+    lax.fori_loop(0, 8, grad_down, 0)
+    hear(1, xz_peers)
+    for g in sd:
+        g.one()
+    fq.two()
+    sent(gs3 + [gf])
+    again = [local.start(x_ref, G.at[0, 0]), local.start(g_ref, G.at[0, 1])]
 
     BQ[...] = jnp.zeros_like(BQ)
     for part in range(3):
@@ -816,9 +801,35 @@
     vs = [
         copies.start(VT, v_land.at[k], shifted(y=dy, c=dc)) for k, (dy, dc) in enumerate(SEQ_PEERS)
     ]
-    for g in sd:
+    def feed(t, _):
+        i, j = t // 4, t % 4
+        r = pl.ds(pl.multiple_of(i * 512, 512), 512)
+        q = pl.ds(pl.multiple_of(j * 512, 512), 512)
+        two = pl.ds(2 * i, 2)
+        total = dot(ACT[r], DN[:, :, :, q].reshape(1024, 512)) + X[two, :, :, q].reshape(512, 512).astype(F32)
+        X[two, :, :, q] = total.astype(BF16).reshape(2, 2, 128, 512)
+        return 0
+
+    lax.fori_loop(0, 8, feed, 0)
+    hear(4, y_peers)
+    fp.one()
+    for g in (sa, sb, so):
+        g.two()
+    for g in su:
         g.mid()
-    fp.mid()
+    fq.mid()
+    fp.two()
+
+    for cp in vs:
+        cp.wait_recv()
+    for b in range(16):
+        total = VT[b]
+        for k in range(7):
+            total += v_land[k, b]
+        CT[b // 4, b % 4, 0:8, :] = total
+        CT[b // 4, b % 4, 8:9, :] = gbu[:, b // 2 * 128 : b // 2 * 128 + 128]
+        CT[b // 4, b % 4, 9:16, :] = jnp.zeros((7, 128), F32)
+    sc.one()
 
     def store(ref, base=0):
         def put(r, total):
@@ -841,7 +852,6 @@
             )
         return made
 
-    fq.two()
     sa.three(store(gq_part))
     sb.three(store(gq_part, 48))
     backs = spread(gq_part, gq_all)
@@ -856,35 +866,14 @@
     def _():
         go_all[...] = go_part[...]
 
-    for cp in vs:
-        cp.wait_recv()
-    for b in range(16):
-        total = VT[b]
-        for k in range(7):
-            total += v_land[k, b]
-        CT[b // 4, b % 4, 0:8, :] = total
-        CT[b // 4, b % 4, 8:9, :] = gbu[:, b // 2 * 128 : b // 2 * 128 + 128]
-        CT[b // 4, b % 4, 9:16, :] = jnp.zeros((7, 128), F32)
-    sc.one()
+    for g in sd:
+        g.mid()
+    sc.mid()
     for g in su:
-        g.mid()
-    for g in sd:
         g.two()
-    fq.mid()
-    sc.mid()
-
-    def layer_out(r, total):
-        bias = vec[0:1, :] + vec[1:2, :]
-        y_out[r] = (G[0, 0, r].astype(F32) + total + bias).astype(BF16)
-
+    fp.mid()
     for cp in again:
         cp.wait()
-    fp.three(layer_out)
-    sc.two()
-    for g in su:
-        g.two()
-    for k, g in enumerate(sd):
-        g.three(store(gd_out, 32 * k))
 
     def grad_in(r, total):
         v = G[0, 0, r].astype(F32)
@@ -895,10 +884,21 @@
         x_out[r] = (G[0, 1, r].astype(F32) + total * inv).astype(BF16)
 
     fq.three(grad_in)
+    sc.two()
     for k, g in enumerate(su):
         g.three(store(gu_part, 64 * k))
     backs += spread(gu_part, gu_all)
+    for g in sd:
+        g.two()
+
+    def layer_out(r, total):
+        bias = vec[0:1, :] + vec[1:2, :]
+        y_out[r] = (G[0, 0, r].astype(F32) + total + bias).astype(BF16)
+
+    fp.three(layer_out)
     sc.three(store(sv))
+    for k, g in enumerate(sd):
+        g.three(store(gd_out, 32 * k))
 
     @pl.when(differs)
     def _():
@@ -920,7 +920,7 @@
     scratch = [
         (blocks, BF16), (blocks, BF16), ((8, 16, 128), BF16), ((8, 32, 128), F32), ((4, 4, 16, 128), BF16),
         (up_all, BF16), (qk_all, BF16), (dn_all, BF16), (wo_all, BF16),
-        (blocks, BF16), (blocks, BF16), ((8, 128, C), BF16), (unit, BF16), (unit, BF16),
+        (blocks, BF16), ((4, 4, 64, C), BF16), ((8, 128, C), BF16), (unit, BF16), (unit, BF16),
         (qk_all, BF16), (wo_all, BF16), (dn_all, BF16), (up_all, BF16), ((8, 128, C), BF16),
         ((1024, HD), F32), ((1024, HD), F32), ((1024, HD), F32), ((1024, HD), F32), ((1024, HD), F32),
         ((48, 128), F32), ((16, 8, 128), F32), ((7, 16, 8, 128), F32), ((4, 4, 16, 128), F32), ((4, 4, 16, 128), F32),

time: 191 us -> 188 us (0.984)
  Pallas kernels: 189 us -> 186 us
    pallas_call x1, Pallas kernels: 186 us -> 183 us  [layer(): pl.pallas_call(layer_kernel, out_shape=[jax.ShapeDtypeStruct(*o) for o in...]
where the time goes in v5:
time: 188 us
  Pallas kernels  186 us (99%)
    pallas_call x1, Pallas kernels, layer(): pl.pallas_call(layer_kernel, out_shape=[jax.ShapeDtypeStruct(*o) for o in...  183 us

profile of v5, /device:TPU:1, one launch (start us, length us, event | category | flops | bytes accessed | tf_op | source)
XLA Modules:
  0.0 187.7 jit_solution(11794364858366753091)
XLA Ops:
  0.7 0.7 broadcast_in_dim.36.freq_ref
  1.3 183.0 %shard_map.254 = (bf16[128,2048]{1,0:T(8,128)(2,1)}, bf16[128,2048]{1,0:T(8,128)(2,1)}, f32[64,2048]{1,0:T(8,128)}, bf16[8,16,1024]{2,1,0:T(8,128)(2,1)}, bf16[8...) custom-call(bf16[128,2048]{1,0:T(8,128)(2,1)} %bitcast.20, bf16[128,2048]{1,0:T(8,128)(2,1)} %bitcast.21, ...), custom_call_target="tpu_custom_call" | custom-call | tf_op jit(solution)/shard_map/pallas_call | solution.py:934
  184.3 3.2 %shard_map.255 = (bf16[128,2048]{1,0:T(8,128)(2,1)}, bf16[128,2048]{1,0:T(8,128)(2,1)}, f32[64,2048]{1,0:T(8,128)}, f32[16,8192]{1,0:T(8,128)}, f32[16,6144]{1,0...) custom-call(bf16[128,2048]{1,0:T(8,128)(2,1)} %get-tuple-element.35., ...), custom_call_target="tpu_custom_call" | custom-call | tf_op jit(solution)/shard_map/pallas_call | solution.py:982
  (1 shorter events, 0.0 us)

commit v6 on v5

--- a/solution.py
+++ b/solution.py
@@ -235,7 +235,8 @@
 
 
 class Scatter:
-    def __init__(self, copies, buf, pool, first, rows=None):
+    def __init__(self, copies, buf, pool, first, rows=None, wide=None):
+        self.wide = wide
         self.copies, self.buf, self.first, self.rows = copies, buf, first, rows
         cut = () if rows is None else (pl.ds(*rows),)
         self.pool = pool
@@ -254,17 +255,25 @@
         r = pl.ds(self.base + r.start, r.size)
         return (i, at, r) if self.first == "x" else (at, i, r)
 
+    def spot(self, i, span):
+        if self.wide is None:
+            return (i, span) + self.cut
+        return (span, i % 2) + self.cut + (pl.ds(1024 * (i // 2), self.wide),)
+
     def relay(self, k):
-        return self.pool.at[(0, pl.ds(2 * k, 2)) + self.cut]
+        return self.pool.at[self.spot(0, pl.ds(2 * k, 2))]
 
     def land(self, k, half):
-        return self.pool.at[(1 + k, pl.ds(2 * half, 2)) + self.cut]
+        return self.pool.at[self.spot(1 + k, pl.ds(2 * half, 2))]
 
     def last(self, k):
-        return self.pool.at[(3, k) + self.cut]
+        return self.pool.at[self.spot(3, k)]
 
     def held(self, i, j, r):
-        return self.pool[i, j, pl.ds(self.base + r.start, r.size)]
+        r = pl.ds(self.base + r.start, r.size)
+        if self.wide is None:
+            return self.pool[i, j, r]
+        return self.pool[j, i % 2, r, pl.ds(1024 * (i // 2), self.wide)]
 
     def one(self):
         start, to = self.copies.start, self.other
@@ -652,6 +661,8 @@
     lax.fori_loop(0, 4, mixed, 0)
     for g in down:
         g.three()
+    sent(xs + xs2 + [xf, xs3[2]])
+    tell(0, xz_peers)
     for h in range(2):
         head_pass(h, PP, DK, DV, TC, TA, TB, gbq)
     for g in upg:
@@ -672,47 +683,18 @@
         return 0
 
     lax.fori_loop(0, 4, grad_qkv, 0)
-    sent(xs + xs2 + [xf, xs3[2]])
-
-    def attend(t, _):
-        i, j = t // 2, t % 2
-        q = pl.ds(pl.multiple_of(j * 1024, 1024), 1024)
-        mix = PP[pl.ds(4 * i, 4), :, M_AT:].reshape(512, 256)
-        total = dot(mix, WO[:, :, :, q].reshape(256, 1024))
-        X[pl.ds(2 * i, 2), :, :, q] = total.astype(BF16).reshape(2, 2, 128, 1024)
-        return 0
-
-    lax.fori_loop(0, 4, attend, 0)
-    vec[10:12, :] = jnp.zeros((2, C), F32)
-
-    def grad_first(t, _):
-        i, j = t // 4, t % 4
-        q = pl.ds(pl.multiple_of(j * 512, 512), 512)
-        left = PP[pl.ds(2 * i, 2), :, L_AT:M_AT].reshape(256, 768)
-        u = dot(left, QK[j].reshape(512, 768), 1, 1)
-        n = NB[pl.ds(2 * i, 2), :, q].reshape(256, 512).astype(F32)
-        vec[10:11, q] += jnp.sum(u * n, 0, keepdims=True)
-        vec[11:12, q] += jnp.sum(u, 0, keepdims=True)
-        F1[i, :, :, q] = (u * vec[2:3, q]).astype(BF16).reshape(2, 128, 512)
-        return 0
-
-    lax.fori_loop(0, 16, grad_first, 0)
-
-    for g in (qa, qb, wo):
-        sent(g.all)
-    sent(qk + up)
-    tell(0, xz_peers)
-    tell(4, y_peers)
-
-    sa = Scatter(copies, GQ, QK, "x", (0, 48))
-    sb = Scatter(copies, GQ, QK, "z", (48, 80))
+
+    sa = Scatter(copies, GQ, X, "x", (0, 48), 768)
+    sb = Scatter(copies, GQ, X, "z", (48, 80), 768)
     so = Scatter(copies, GO, WO, "x")
     fp = SeqScatter(copies, X, PP)
     fq = SeqScatter(copies, F1, NB)
+    hear(0, xz_peers)
+    sa.one()
+    sb.one()
+
     gbu[...] = jnp.zeros_like(gbu)
-    hear(0, xz_peers)
-    for g in (sa, sb, so):
-        g.one()
+    sent(qk + up)
     for g in down + upg:
         g.done()
 
@@ -730,8 +712,8 @@
         return 0
 
     lax.fori_loop(0, 8, hidden, 0)
-    for g in (sa, sb, so):
-        g.mid()
+    sa.mid()
+    sb.mid()
 
     sd = [Scatter(copies, GD, F2, "x", (0, 32)), Scatter(copies, GD, F2, "z", (32, 32))]
     su = [Scatter(copies, GU, UP, "x", (0, 64)), Scatter(copies, GU, UP, "z", (64, 64))]
@@ -746,15 +728,13 @@
         n = NB[pl.ds(2 * i, 2), :, q].reshape(256, 512).astype(F32)
         vec[12:13, q] += jnp.sum(u * n, 0, keepdims=True)
         vec[13:14, q] += jnp.sum(u, 0, keepdims=True)
-        total = u * vec[4:5, q] + F1[i, :, :, q].reshape(256, 512).astype(F32)
-        F1[i, :, :, q] = total.astype(BF16).reshape(2, 128, 512)
+        F1[i, :, :, q] = (u * vec[4:5, q]).astype(BF16).reshape(2, 128, 512)
         return 0
 
     lax.fori_loop(0, 16, second, 0)
     for g in upg:
         sent(g.all)
     tell(2, xz_peers)
-    tell(3, y_peers)
 
     def grad_up(t, _):
         i, j = t // 2, t % 2
@@ -766,11 +746,73 @@
 
     lax.fori_loop(0, 8, grad_up, 0)
     tell(1, xz_peers)
-    hear(3, y_peers)
-    fq.one()
     hear(2, xz_peers)
     for g in su:
         g.one()
+    sa.two()
+    sb.two()
+
+    vec[10:12, :] = jnp.zeros((2, C), F32)
+
+    def grad_first(t, _):
+        i, j = t // 4, t % 4
+        q = pl.ds(pl.multiple_of(j * 512, 512), 512)
+        left = PP[pl.ds(2 * i, 2), :, L_AT:M_AT].reshape(256, 768)
+        u = dot(left, QK[j].reshape(512, 768), 1, 1)
+        n = NB[pl.ds(2 * i, 2), :, q].reshape(256, 512).astype(F32)
+        vec[10:11, q] += jnp.sum(u * n, 0, keepdims=True)
+        vec[11:12, q] += jnp.sum(u, 0, keepdims=True)
+        total = u * vec[2:3, q] + F1[i, :, :, q].reshape(256, 512).astype(F32)
+        F1[i, :, :, q] = total.astype(BF16).reshape(2, 128, 512)
+        return 0
+
+    lax.fori_loop(0, 16, grad_first, 0)
+
+    tell(3, y_peers)
+
+    def store(ref, base=0):
+        def put(r, total):
+            ref[pl.ds(base + r.start, r.size)] = total.astype(ref.dtype)
+
+        return put
+
+    gu_part = GHL.at[pl.ds(128, 128)]
+    gq_part = GHL.at[pl.ds(0, 128), pl.ds(0, 768)]
+
+    def spread(part, out):
+        out[s] = part[pl.ds(pl.multiple_of(s * 16, 16), 16)]
+        made = []
+        for dy, dc in SEQ_PEERS:
+            peer = moved(y, dy) * 2 + lax.rem(c + dc, 2)
+            made.append(
+                copies.start(
+                    part.at[pl.ds(pl.multiple_of(peer * 16, 16), 16)], out.at[s], shifted(y=dy, c=dc)
+                )
+            )
+        return made
+
+    sa.three(store(gq_part))
+    sb.three(store(gq_part, 48))
+    backs = spread(gq_part, gq_all)
+
+    def attend(t, _):
+        i, j = t // 2, t % 2
+        q = pl.ds(pl.multiple_of(j * 1024, 1024), 1024)
+        mix = PP[pl.ds(4 * i, 4), :, M_AT:].reshape(512, 256)
+        total = dot(mix, WO[:, :, :, q].reshape(256, 1024))
+        X[pl.ds(2 * i, 2), :, :, q] = total.astype(BF16).reshape(2, 2, 128, 1024)
+        return 0
+
+    lax.fori_loop(0, 4, attend, 0)
+    sent(wo.all)
+    tell(5, xz_peers)
+    tell(4, y_peers)
+    hear(3, y_peers)
+    fq.one()
+    for g in su:
+        g.mid()
+    hear(5, xz_peers)
+    so.one()
 
     def grad_down(t, _):
         i, j = t // 2, t % 2
@@ -813,10 +855,11 @@
     lax.fori_loop(0, 8, feed, 0)
     hear(4, y_peers)
     fp.one()
-    for g in (sa, sb, so):
+    so.mid()
+    for g in sd:
+        g.mid()
+    for g in su:
         g.two()
-    for g in su:
-        g.mid()
     fq.mid()
     fp.two()
 
@@ -831,30 +874,15 @@
         CT[b // 4, b % 4, 9:16, :] = jnp.zeros((7, 128), F32)
     sc.one()
 
-    def store(ref, base=0):
-        def put(r, total):
-            ref[pl.ds(base + r.start, r.size)] = total.astype(ref.dtype)
-
-        return put
-
-    gu_part = ACT.at[pl.ds(0, 128)]
-    gq_part = ACT.at[pl.ds(128, 128), pl.ds(0, 768)]
-
-    def spread(part, out):
-        out[s] = part[pl.ds(pl.multiple_of(s * 16, 16), 16)]
-        made = []
-        for dy, dc in SEQ_PEERS:
-            peer = moved(y, dy) * 2 + lax.rem(c + dc, 2)
-            made.append(
-                copies.start(
-                    part.at[pl.ds(pl.multiple_of(peer * 16, 16), 16)], out.at[s], shifted(y=dy, c=dc)
-                )
-            )
-        return made
-
-    sa.three(store(gq_part))
-    sb.three(store(gq_part, 48))
-    backs = spread(gq_part, gq_all)
+    so.two()
+    sc.mid()
+    for k, g in enumerate(su):
+        g.three(store(gu_part, 64 * k))
+    backs += spread(gu_part, gu_all)
+    for g in sd:
+        g.two()
+    fp.mid()
+    sc.two()
     so.three(store(go_part))
     out_back = copies.make(go_part, go_all, source)
 
@@ -866,12 +894,6 @@
     def _():
         go_all[...] = go_part[...]
 
-    for g in sd:
-        g.mid()
-    sc.mid()
-    for g in su:
-        g.two()
-    fp.mid()
     for cp in again:
         cp.wait()
 
@@ -884,12 +906,6 @@
         x_out[r] = (G[0, 1, r].astype(F32) + total * inv).astype(BF16)
 
     fq.three(grad_in)
-    sc.two()
-    for k, g in enumerate(su):
-        g.three(store(gu_part, 64 * k))
-    backs += spread(gu_part, gu_all)
-    for g in sd:
-        g.two()
 
     def layer_out(r, total):
         bias = vec[0:1, :] + vec[1:2, :]
@@ -937,7 +953,7 @@
         in_specs=[any_, any_] + [vm] * 10 + [any_] * 4,
         out_specs=[vm] * 7,
         scratch_shapes=[S(*h) for h in scratch]
-        + [pltpu.SemaphoreType.DMA((230,)), pltpu.SemaphoreType.DMA((230,)), pltpu.SemaphoreType.REGULAR((5,)), pltpu.SemaphoreType.DMA((16,))],
+        + [pltpu.SemaphoreType.DMA((230,)), pltpu.SemaphoreType.DMA((230,)), pltpu.SemaphoreType.REGULAR((6,)), pltpu.SemaphoreType.DMA((16,))],
         compiler_params=pltpu.CompilerParams(
             collective_id=1, has_side_effects=True, vmem_limit_bytes=64 * 2**20 - 2**16
         ),

time: 188 us -> 197 us (1.048); the launches traced: 188 us -> 194 us
  Pallas kernels: 186 us -> 193 us
    pallas_call x1, Pallas kernels: 183 us -> 190 us  [layer(): pl.pallas_call(layer_kernel, out_shape=[jax.ShapeDtypeStruct(*o) for o in...]
where the time goes in v6:
time: 197 us; the launch traced here: 194 us
  Pallas kernels  193 us (98%)
    pallas_call x1, Pallas kernels, layer(): pl.pallas_call(layer_kernel, out_shape=[jax.ShapeDtypeStruct(*o) for o in...  190 us

profile of v6, /device:TPU:1, one launch (start us, length us, event | category | flops | bytes accessed | tf_op | source)
XLA Modules:
  0.0 194.5 jit_solution(3422178876969422180)
XLA Ops:
  0.7 0.7 broadcast_in_dim.36.freq_ref
  1.3 189.8 %shard_map.254 = (bf16[128,2048]{1,0:T(8,128)(2,1)}, bf16[128,2048]{1,0:T(8,128)(2,1)}, f32[64,2048]{1,0:T(8,128)}, bf16[8,16,1024]{2,1,0:T(8,128)(2,1)}, bf16[8...) custom-call(bf16[128,2048]{1,0:T(8,128)(2,1)} %bitcast.20, bf16[128,2048]{1,0:T(8,128)(2,1)} %bitcast.21, ...), custom_call_target="tpu_custom_call" | custom-call | tf_op jit(solution)/shard_map/pallas_call | solution.py:950
  191.2 3.2 %shard_map.255 = (bf16[128,2048]{1,0:T(8,128)(2,1)}, bf16[128,2048]{1,0:T(8,128)(2,1)}, f32[64,2048]{1,0:T(8,128)}, f32[16,8192]{1,0:T(8,128)}, f32[16,6144]{1,0...) custom-call(bf16[128,2048]{1,0:T(8,128)(2,1)} %get-tuple-element.35., ...), custom_call_target="tpu_custom_call" | custom-call | tf_op jit(solution)/shard_map/pallas_call | solution.py:998
  (1 shorter events, 0.0 us)

commit v7 on v5

--- a/solution.py
+++ b/solution.py
@@ -771,6 +771,8 @@
     hear(2, xz_peers)
     for g in su:
         g.one()
+    for g in (sa, sb, so):
+        g.two()
 
     def grad_down(t, _):
         i, j = t // 2, t % 2
@@ -781,9 +783,6 @@
         return 0
 
     lax.fori_loop(0, 8, grad_down, 0)
-    hear(1, xz_peers)
-    for g in sd:
-        g.one()
     fq.two()
     sent(gs3 + [gf])
     again = [local.start(x_ref, G.at[0, 0]), local.start(g_ref, G.at[0, 1])]
@@ -811,12 +810,13 @@
         return 0
 
     lax.fori_loop(0, 8, feed, 0)
+    for g in su:
+        g.mid()
+    hear(1, xz_peers)
+    for g in sd:
+        g.one()
     hear(4, y_peers)
     fp.one()
-    for g in (sa, sb, so):
-        g.two()
-    for g in su:
-        g.mid()
     fq.mid()
     fp.two()
 
@@ -866,12 +866,19 @@
     def _():
         go_all[...] = go_part[...]
 
+    for g in su:
+        g.two()
     for g in sd:
         g.mid()
     sc.mid()
-    for g in su:
+    fp.mid()
+    sc.two()
+    for k, g in enumerate(su):
+        g.three(store(gu_part, 64 * k))
+    backs += spread(gu_part, gu_all)
+    for g in sd:
         g.two()
-    fp.mid()
+
     for cp in again:
         cp.wait()
 
@@ -884,12 +891,6 @@
         x_out[r] = (G[0, 1, r].astype(F32) + total * inv).astype(BF16)
 
     fq.three(grad_in)
-    sc.two()
-    for k, g in enumerate(su):
-        g.three(store(gu_part, 64 * k))
-    backs += spread(gu_part, gu_all)
-    for g in sd:
-        g.two()
 
     def layer_out(r, total):
         bias = vec[0:1, :] + vec[1:2, :]

time: 188 us -> 189 us (level)
  Pallas kernels: 186 us -> 188 us
where the time goes in v7:
time: 189 us
  Pallas kernels  188 us (99%)
    pallas_call x1, Pallas kernels, layer(): pl.pallas_call(layer_kernel, out_shape=[jax.ShapeDtypeStruct(*o) for o in...  184 us

profile of v7, /device:TPU:1, one launch (start us, length us, event | category | flops | bytes accessed | tf_op | source)
XLA Modules:
  0.0 189.1 jit_solution(10460308451737950173)
XLA Ops:
  0.7 0.7 broadcast_in_dim.36.freq_ref
  1.3 184.4 %shard_map.254 = (bf16[128,2048]{1,0:T(8,128)(2,1)}, bf16[128,2048]{1,0:T(8,128)(2,1)}, f32[64,2048]{1,0:T(8,128)}, bf16[8,16,1024]{2,1,0:T(8,128)(2,1)}, bf16[8...) custom-call(bf16[128,2048]{1,0:T(8,128)(2,1)} %bitcast.20, bf16[128,2048]{1,0:T(8,128)(2,1)} %bitcast.21, ...), custom_call_target="tpu_custom_call" | custom-call | tf_op jit(solution)/shard_map/pallas_call | solution.py:935
  185.8 3.2 %shard_map.255 = (bf16[128,2048]{1,0:T(8,128)(2,1)}, bf16[128,2048]{1,0:T(8,128)(2,1)}, f32[64,2048]{1,0:T(8,128)}, f32[16,8192]{1,0:T(8,128)}, f32[16,6144]{1,0...) custom-call(bf16[128,2048]{1,0:T(8,128)(2,1)} %get-tuple-element.35., ...), custom_call_target="tpu_custom_call" | custom-call | tf_op jit(solution)/shard_map/pallas_call | solution.py:983
  (1 shorter events, 0.0 us)

commit v8 on v5

--- a/solution.py
+++ b/solution.py
@@ -235,7 +235,8 @@
 
 
 class Scatter:
-    def __init__(self, copies, buf, pool, first, rows=None):
+    def __init__(self, copies, buf, pool, first, rows=None, wide=None):
+        self.wide = wide
         self.copies, self.buf, self.first, self.rows = copies, buf, first, rows
         cut = () if rows is None else (pl.ds(*rows),)
         self.pool = pool
@@ -254,17 +255,25 @@
         r = pl.ds(self.base + r.start, r.size)
         return (i, at, r) if self.first == "x" else (at, i, r)
 
+    def spot(self, i, span):
+        if self.wide is None:
+            return (i, span) + self.cut
+        return (span, i % 2) + self.cut + (pl.ds(1024 * (i // 2), self.wide),)
+
     def relay(self, k):
-        return self.pool.at[(0, pl.ds(2 * k, 2)) + self.cut]
+        return self.pool.at[self.spot(0, pl.ds(2 * k, 2))]
 
     def land(self, k, half):
-        return self.pool.at[(1 + k, pl.ds(2 * half, 2)) + self.cut]
+        return self.pool.at[self.spot(1 + k, pl.ds(2 * half, 2))]
 
     def last(self, k):
-        return self.pool.at[(3, k) + self.cut]
+        return self.pool.at[self.spot(3, k)]
 
     def held(self, i, j, r):
-        return self.pool[i, j, pl.ds(self.base + r.start, r.size)]
+        r = pl.ds(self.base + r.start, r.size)
+        if self.wide is None:
+            return self.pool[i, j, r]
+        return self.pool[j, i % 2, r, pl.ds(1024 * (i // 2), self.wide)]
 
     def one(self):
         start, to = self.copies.start, self.other
@@ -395,7 +404,7 @@
 def layer_kernel(x_ref, g_ref, pos_ref, freq_ref, bo_ref, bd_ref, ga_ref, sa_ref, gm_ref, sm_ref, bq_ref, bu_ref,
                  up_ref, qkv_ref, down_ref, out_ref,
                  y_out, x_out, gd_out, gu_all, gq_all, go_all, sv,
-                 X, G, SA, RA, SM, UP, QK, DN, WO, F1, F2, NB, ACT, GHL, GQ, GO, GD, GU, PP,
+                 X, G, SA, RA, SM, UP, QK, DN, WO, F1, F2, NB, ACT, GHL, GQ, GO, SP, GU, PP,
                  DK, DV, TC, TA, TB,
                  BQ, VT, v_land, CT, CP, vec, gsum, gbu, gbq, go_part,
                  send, recv, ready, loc):
@@ -733,9 +742,22 @@
     for g in (sa, sb, so):
         g.mid()
 
-    sd = [Scatter(copies, GD, F2, "x", (0, 32)), Scatter(copies, GD, F2, "z", (32, 32))]
-    su = [Scatter(copies, GU, UP, "x", (0, 64)), Scatter(copies, GU, UP, "z", (64, 64))]
+    GD = F2
+    sd = [Scatter(copies, GD, DN, "x", (0, 32)), Scatter(copies, GD, DN, "z", (32, 32))]
+    su = [Scatter(copies, GU, SP, "x", (0, 64), 1024), Scatter(copies, GU, SP, "z", (64, 64), 1024)]
     sc = Scatter(copies, CT, CP, "z")
+    def grad_up(t, _):
+        i, j = t // 2, t % 2
+        r = pl.ds(pl.multiple_of(i * 512, 512), 512)
+        q = pl.ds(pl.multiple_of(j * 512, 512), 512)
+        left = F2[:, :, :, r].reshape(1024, 512)
+        GU[i, :, :, q] = dot(left, GHL[:, q], 0, 0).astype(BF16).reshape(4, 128, 512)
+        return 0
+
+    lax.fori_loop(0, 8, grad_up, 0)
+    for g in su:
+        g.one()
+
     vec[12:14, :] = jnp.zeros((2, C), F32)
 
     def second(t, _):
@@ -751,26 +773,29 @@
         return 0
 
     lax.fori_loop(0, 16, second, 0)
-    for g in upg:
-        sent(g.all)
-    tell(2, xz_peers)
     tell(3, y_peers)
-
-    def grad_up(t, _):
-        i, j = t // 2, t % 2
+    for g in (sa, sb, so):
+        g.two()
+    hear(3, y_peers)
+    fq.one()
+
+    def feed(t, _):
+        i, j = t // 4, t % 4
         r = pl.ds(pl.multiple_of(i * 512, 512), 512)
         q = pl.ds(pl.multiple_of(j * 512, 512), 512)
-        left = F2[:, :, :, r].reshape(1024, 512)
-        GU[i, :, :, q] = dot(left, GHL[:, q], 0, 0).astype(BF16).reshape(4, 128, 512)
-        return 0
-
-    lax.fori_loop(0, 8, grad_up, 0)
+        two = pl.ds(2 * i, 2)
+        total = dot(ACT[r], DN[:, :, :, q].reshape(1024, 512)) + X[two, :, :, q].reshape(512, 512).astype(F32)
+        X[two, :, :, q] = total.astype(BF16).reshape(2, 2, 128, 512)
+        return 0
+
+    lax.fori_loop(0, 8, feed, 0)
+    for g in down:
+        sent(g.all)
     tell(1, xz_peers)
-    hear(3, y_peers)
-    fq.one()
-    hear(2, xz_peers)
+    hear(4, y_peers)
+    fp.one()
     for g in su:
-        g.one()
+        g.mid()
 
     def grad_down(t, _):
         i, j = t // 2, t % 2
@@ -801,22 +826,6 @@
     vs = [
         copies.start(VT, v_land.at[k], shifted(y=dy, c=dc)) for k, (dy, dc) in enumerate(SEQ_PEERS)
     ]
-    def feed(t, _):
-        i, j = t // 4, t % 4
-        r = pl.ds(pl.multiple_of(i * 512, 512), 512)
-        q = pl.ds(pl.multiple_of(j * 512, 512), 512)
-        two = pl.ds(2 * i, 2)
-        total = dot(ACT[r], DN[:, :, :, q].reshape(1024, 512)) + X[two, :, :, q].reshape(512, 512).astype(F32)
-        X[two, :, :, q] = total.astype(BF16).reshape(2, 2, 128, 512)
-        return 0
-
-    lax.fori_loop(0, 8, feed, 0)
-    hear(4, y_peers)
-    fp.one()
-    for g in (sa, sb, so):
-        g.two()
-    for g in su:
-        g.mid()
     fq.mid()
     fp.two()
 
@@ -921,7 +930,7 @@
         (blocks, BF16), (blocks, BF16), ((8, 16, 128), BF16), ((8, 32, 128), F32), ((4, 4, 16, 128), BF16),
         (up_all, BF16), (qk_all, BF16), (dn_all, BF16), (wo_all, BF16),
         (blocks, BF16), ((4, 4, 64, C), BF16), ((8, 128, C), BF16), (unit, BF16), (unit, BF16),
-        (qk_all, BF16), (wo_all, BF16), (dn_all, BF16), (up_all, BF16), ((8, 128, C), BF16),
+        (qk_all, BF16), (wo_all, BF16), (blocks, BF16), (up_all, BF16), ((8, 128, C), BF16),
         ((1024, HD), F32), ((1024, HD), F32), ((1024, HD), F32), ((1024, HD), F32), ((1024, HD), F32),
         ((48, 128), F32), ((16, 8, 128), F32), ((7, 16, 8, 128), F32), ((4, 4, 16, 128), F32), ((4, 4, 16, 128), F32),
         ((32, C), F32), ((1, C), F32), ((1, n_up), F32), ((1, n_qkv), F32),

time: 188 us -> 192 us (1.021)
  Pallas kernels: 186 us -> 190 us
    pallas_call x1, Pallas kernels: 183 us -> 187 us  [layer(): pl.pallas_call(layer_kernel, out_shape=[jax.ShapeDtypeStruct(*o) for o in...]
where the time goes in v8:
time: 192 us
  Pallas kernels  190 us (99%)
    pallas_call x1, Pallas kernels, layer(): pl.pallas_call(layer_kernel, out_shape=[jax.ShapeDtypeStruct(*o) for o in...  187 us

profile of v8, /device:TPU:1, one launch (start us, length us, event | category | flops | bytes accessed | tf_op | source)
XLA Modules:
  0.0 191.7 jit_solution(6034841928695392398)
XLA Ops:
  0.7 0.7 broadcast_in_dim.36.freq_ref
  1.3 187.0 %shard_map.254 = (bf16[128,2048]{1,0:T(8,128)(2,1)}, bf16[128,2048]{1,0:T(8,128)(2,1)}, f32[64,2048]{1,0:T(8,128)}, bf16[8,16,1024]{2,1,0:T(8,128)(2,1)}, bf16[8...) custom-call(bf16[128,2048]{1,0:T(8,128)(2,1)} %bitcast.20, bf16[128,2048]{1,0:T(8,128)(2,1)} %bitcast.21, ...), custom_call_target="tpu_custom_call" | custom-call | tf_op jit(solution)/shard_map/pallas_call | solution.py:943
  188.3 3.2 %shard_map.255 = (bf16[128,2048]{1,0:T(8,128)(2,1)}, bf16[128,2048]{1,0:T(8,128)(2,1)}, f32[64,2048]{1,0:T(8,128)}, f32[16,8192]{1,0:T(8,128)}, f32[16,6144]{1,0...) custom-call(bf16[128,2048]{1,0:T(8,128)(2,1)} %get-tuple-element.35., ...), custom_call_target="tpu_custom_call" | custom-call | tf_op jit(solution)/shard_map/pallas_call | solution.py:991
  (1 shorter events, 0.0 us)
